TPU v7x, 256 devices: a whole 4x4x8 slice. The times are simulated.
256 devices in a mesh: sec: 16 (over z, core), tile: 16 (over y, x).
Axes of the slice: x: 4, y: 4, z: 8, core: 2. Of those that a mesh axis runs over, the one named last changes fastest.
Arguments:
- raw_sections: bfloat16 [32, 128, 2048], P('sec', None, 'tile'), may hold values from -6 to 6
- shift_cols: int32 [32], P('sec'), may hold values from -64 to 63
- shift_rows: int32 [32], P('sec'), may hold values from -2 to 1
- w_first: bfloat16 [32, 1, 3, 3], replicated, may hold values from -2 to 2
- b_first: float32 [32], replicated, may hold values from -3 to 3
- w_second: bfloat16 [32, 32, 3, 3], replicated, may hold values from -0.375 to 0.375
- b_second: float32 [32], replicated, may hold values from -3 to 3
- w_stride: bfloat16 [32, 32, 2, 2], replicated, may hold values from -0.5 to 0.5
- b_stride: float32 [32], replicated, may hold values from -3 to 3
- w_depth: bfloat16 [64, 32, 3, 3, 3], replicated, may hold values from -0.21875 to 0.21875
- b_depth: float32 [64], replicated, may hold values from -3 to 3
- w_head: float32 [3, 64], replicated, may hold values from -0.75 to 0.75
- b_head: float32 [3], replicated, may hold values from -3 to 3
Outputs:
- affinity: float32 [3, 32, 64, 1024], P(None, 'sec', None, 'tile')
All inputs are finite; a program needn't handle non-finite values.
Results may differ from a plain program's by a relative error of at most 0.00081.
Values may be sent and summed in bfloat16 or wider, within the bound.
No kernel may reach another device: no remote copies, remote signals or barrier semaphores. Data moves between devices by JAX's collectives and lax.ppermute only.
A program may use at most 128 MiB of HBM per device.

v0:
```python
import jax
import jax.numpy as jnp
from jax import lax
from jax.experimental import pallas as pl
from jax.experimental.pallas import tpu as pltpu
from jax.sharding import PartitionSpec as P

BLK = 16
TILES = 16
SECS = 16
HALO = 4
OFF = -1e30
BF = jnp.bfloat16
F32 = jnp.float32
SG = 11
VMEM = pltpu.VMEM
SMEM = pltpu.SMEM


def floor_lane(shape, dim):
    return lax.broadcasted_iota(jnp.int32, shape, dim)


def align_kernel(cols, rows, pos, gathered, out, tiles, lifted, sems):
    tile = pos[0]
    copies = []
    for z in range(2):
        start = 128 * tile - BLK * cols[z] - HALO
        first_tile = lax.shift_right_arithmetic(start, 7)
        for k in range(3):
            index = jnp.clip(first_tile + k, 0, TILES - 1)
            copy = pltpu.make_async_copy(gathered.at[index, z], tiles.at[z, k], sems.at[z, k])
            copy.start()
            copies.append(copy)
    lifted[0:32, :] = jnp.zeros((32, 256), F32)
    lifted[160:192, :] = jnp.zeros((32, 256), F32)
    lane = floor_lane((128, 128), 1)
    for z in range(2):
        start = 128 * tile - BLK * cols[z] - HALO
        first_tile = lax.shift_right_arithmetic(start, 7)
        offset = start - first_tile * 128
        turned = []
        for k in range(3):
            copies[3 * z + k].wait()
            inside = ((first_tile + k >= 0) & (first_tile + k < TILES)).astype(F32)
            value = tiles[z, k].astype(F32) * inside
            turned.append(pltpu.roll(value, 128 - offset, 1))
        low = jnp.where(lane < 128 - offset, turned[0], turned[1])
        high = jnp.where(lane < 128 - offset, turned[1], turned[2])
        low = jnp.where((tile == 0) & (lane < HALO), 0.0, low)
        high = jnp.where((tile == TILES - 1) & (lane >= HALO), 0.0, high)
        lifted[32:160, 0:128] = low
        lifted[32:160, 128:256] = high
        base = pl.multiple_of(32 - BLK * rows[z], BLK)
        out[z] = lifted[pl.ds(base, 128), :].astype(BF)


def align(gathered, cols, rows, pos):
    return pl.pallas_call(
        align_kernel,
        out_shape=jax.ShapeDtypeStruct((2, 128, 256), BF),
        in_specs=[pl.BlockSpec(memory_space=SMEM)] * 3 + [pl.BlockSpec(memory_space=pl.ANY)],
        out_specs=pl.BlockSpec(memory_space=VMEM),
        scratch_shapes=[
            pltpu.VMEM((2, 3, 128, 128), BF),
            pltpu.VMEM((192, 256), F32),
            pltpu.SemaphoreType.DMA((2, 3)),
        ],
        name="align",
    )(cols, rows, pos, gathered)


def front(tile, window, w1, bias1, w2, bias2, ws, biass, left, right, feats, strided):
    value = window.astype(F32)
    left[2:130, :] = value[:, 0:128]
    right[2:130, :] = value[:, 128:256]
    lane = floor_lane((32, 128), 1)
    patches = [None] * SG
    for j in range(8):
        low = left[pl.ds(j, 32, stride=4), :]
        high = right[pl.ds(j, 32, stride=4), :]
        ring = jnp.where(lane < 8, high, low)
        mine = (lane >= 16 * j) & (lane < 16 * j + 16)
        for g in range(SG):
            source = low if g < SG - 1 else ring
            shift = (16 * j - 12 * g) % 128
            turned = pltpu.roll(source, shift, 1) if shift else source
            patches[g] = turned if j == 0 else jnp.where(mine, turned, patches[g])
    patch = jnp.concatenate(patches, axis=0).astype(BF)
    for q in range(7):
        made = jnp.dot(patch, w1[:, 384 * q : 384 * (q + 1)], preferred_element_type=F32)
        made = jnp.maximum(made.reshape(SG, 32, 384) + bias1[...][None], 0.0)
        feats[:, 384 * q : 384 * (q + 1)] = made.reshape(SG * 32, 384).astype(BF)

    @pl.when(tile == 0)
    def _():
        feats[0:32, 0:576] = jnp.zeros((32, 576), BF)

    @pl.when(tile == TILES - 1)
    def _():
        feats[320:352, 2112:2688] = jnp.zeros((32, 576), BF)

    lane = floor_lane((SG, 32, 128), 2)
    row = floor_lane((SG, 32, 128), 1)
    from_above = (lane < 32) & (row > 0)
    from_below = (lane >= 96) & (row < 31)
    kept = (lane >= 32) & (lane < 96)
    for p in range(6):
        second = jnp.dot(
            feats[:, 384 * p : 384 * p + 768], w2[...], preferred_element_type=F32
        )
        second = jnp.maximum(second + bias2[...], 0.0).astype(BF)
        made = jnp.dot(second, ws[...], preferred_element_type=F32)
        made = jnp.maximum(made + biass[...], 0.0)
        down = pltpu.roll(made, 1, 0).reshape(SG, 32, 128)
        up = pltpu.roll(made, SG * 32 - 1, 0).reshape(SG, 32, 128)
        made = made.reshape(SG, 32, 128)
        made = jnp.where(kept, made, jnp.where(from_above, down, jnp.where(from_below, up, 0.0)))
        made = made.astype(BF)
        for g in range(SG):
            strided[p % 2, 3 * g + p // 2] = made[g]

    @pl.when(tile == 0)
    def _():
        strided[0, 0] = jnp.zeros((32, 128), BF)

    @pl.when(tile == TILES - 1)
    def _():
        strided[1, 32] = jnp.zeros((32, 128), BF)


def main_kernel(
    pos, window, w1, bias1, w2, bias2, ws, biass, wd, biasd, wh, bh, out, left, right, feats, strided
):
    tile = pos[0]
    sec = pos[1]
    for side in (left, right):
        side[0:2, :] = jnp.zeros((2, 128), F32)
        side[130:136, :] = jnp.zeros((6, 128), F32)

    def one(z, carry):
        front(
            tile, window[z], w1, bias1, w2, bias2, ws, biass, left, right, feats, strided.at[z]
        )
        return carry

    lax.fori_loop(0, 4, one, 0)

    @pl.when(sec == 0)
    def _():
        strided[0] = jnp.zeros((2, 33, 32, 128), BF)

    @pl.when(sec == SECS - 1)
    def _():
        strided[3] = jnp.zeros((2, 33, 32, 128), BF)

    lane = floor_lane((32, 128), 1)
    for z in range(2):
        spots = [jnp.zeros((32, 128), F32)] * 3
        for part in range(4):
            blocks = []
            for dz in range(3):
                for kx in range(4):
                    first = kx // 2 + 8 * part
                    blocks.append(strided[z + dz, kx % 2, first : first + 8].reshape(256, 128))
            patch = jnp.concatenate(blocks, axis=1)
            deep = jnp.dot(patch, wd[...], preferred_element_type=F32)
            deep = jnp.maximum(deep + biasd[...], 0.0)
            high = deep.astype(BF)
            low = (deep - high.astype(F32)).astype(BF)
            logits = jnp.dot(
                jnp.concatenate([high, low, high], axis=1), wh[...], preferred_element_type=F32
            )
            for step in range(8):
                m = 8 * part + step
                slab = logits[32 * step : 32 * step + 32]
                mine = (lane == 2 * m) | (lane == 2 * m + 1) | (lane == 64 + 2 * m) | (lane == 65 + 2 * m)
                for i in range(3):
                    shift = (2 * m - 2 * i) % 128
                    turned = pltpu.roll(slab, shift, 1) if shift else slab
                    spots[i] = jnp.where(mine, turned, spots[i])
        for i in range(3):
            for half in range(2):
                yp, k = divmod(2 * i + half, 3)
                value = spots[i] if half == 0 else pltpu.roll(spots[i], 64, 1)
                value = jax.nn.sigmoid(value[:, 0:64] + bh[k])
                out[k, z, pl.ds(yp, 32, stride=2), :] = value


def main(pos, window, *weights):
    return pl.pallas_call(
        main_kernel,
        out_shape=jax.ShapeDtypeStruct((3, 2, 64, 64), F32),
        in_specs=[pl.BlockSpec(memory_space=SMEM)]
        + [pl.BlockSpec(memory_space=VMEM)] * 10
        + [pl.BlockSpec(memory_space=SMEM)],
        out_specs=pl.BlockSpec(memory_space=VMEM),
        scratch_shapes=[
            pltpu.VMEM((136, 128), F32),
            pltpu.VMEM((136, 128), F32),
            pltpu.VMEM((SG * 32, 2688), BF),
            pltpu.VMEM((4, 2, 33, 32, 128), BF),
        ],
        compiler_params=pltpu.CompilerParams(vmem_limit_bytes=48 * 1024 * 1024),
        name="convs",
    )(pos, window, *weights)


def prepare_kernel(
    t1, t2, ts, td, th, b1, b2, bs, bd, w1, bias1, w2, bias2, ws, biass, wd, biasd, wh
):
    row = floor_lane((128, 384), 0)
    group = floor_lane((128, 384), 1) // 32
    dy = row // 16 - group % 6
    dx = row % 16 - group // 6
    base = jnp.zeros((128, 384), F32)
    for a in range(3):
        for b in range(3):
            spread = jnp.concatenate([t1[a, b : b + 1, :].astype(F32)] * 12, axis=1)
            base = jnp.where((dy == a) & (dx == b), spread, base)
    for q in range(7):
        turned = pltpu.roll(base, 2 * q, 0) if q else base
        w1[:, 384 * q : 384 * (q + 1)] = turned.astype(BF)
    lone = jnp.concatenate([b1[...]] * 12, axis=1)
    row = floor_lane((32, 384), 0)
    group = floor_lane((32, 384), 1) // 32 % 6
    outside = ((row == 0) & (group == 0)) | ((row == 31) & (group == 5))
    bias1[...] = jnp.where(outside, OFF, lone)
    bias2[...] = jnp.concatenate([b2[...]] * 8, axis=1)
    biass[...] = jnp.concatenate([bs[...]] * 4, axis=1)
    biasd[...] = jnp.concatenate([bd[...]] * 4, axis=1)

    lane = floor_lane((32, 128), 1)
    none = jnp.zeros((32, 128), F32)
    tiled = [
        [jnp.concatenate([t2[a, b].astype(F32)] * 4, axis=1) for b in range(3)] for a in range(3)
    ]
    for kx in range(4):
        for xp in range(2):
            b = kx - xp
            for j in range(6):
                made = none
                if 0 <= b < 3:
                    for a in range(3):
                        if 0 <= j - a < 4:
                            made = jnp.where(lane // 32 == j - a, tiled[a][b], made)
                start = 32 * (6 * kx + j)
                w2[start : start + 32, 128 * xp : 128 * xp + 128] = made.astype(BF)

    tiled = [
        [jnp.concatenate([ts[a, b].astype(F32)] * 4, axis=1) for b in range(2)] for a in range(2)
    ]
    for xp in range(2):
        for yp in range(4):
            mine = (lane // 32) % 2 == (1 if yp < 2 else 0)
            start = 32 * (4 * xp + yp)
            ws[start : start + 32, :] = jnp.where(mine, tiled[yp % 2][xp], 0.0).astype(BF)

    for dz in range(3):
        tiled = [
            [jnp.concatenate([td[dz, a, b].astype(F32)] * 2, axis=1) for b in range(3)]
            for a in range(3)
        ]
        for kx in range(4):
            for xp in range(2):
                b = kx - xp
                for slot in range(4):
                    made = none
                    if 0 <= b < 3:
                        low = tiled[slot][b] if slot < 3 else none
                        high = tiled[slot - 1][b] if slot > 0 else none
                        made = jnp.where(lane < 64, low, high)
                    start = 128 * (4 * dz + kx) + 32 * slot
                    wd[start : start + 32, 128 * xp : 128 * xp + 128] = made.astype(BF)

    lane = floor_lane((64, 128), 1)
    for xp in range(2):
        for yp in range(2):
            made = jnp.zeros((64, 128), F32)
            for k in range(3):
                c = 3 * yp + k
                made = jnp.where(lane == 64 * (c % 2) + 2 * (c // 2) + xp, th[:, k : k + 1], made)
            high = made.astype(BF)
            low = (made - high.astype(F32)).astype(BF)
            start = 64 * (2 * xp + yp)
            wh[start : start + 64, :] = high
            wh[256 + start : 256 + start + 64, :] = high
            wh[512 + start : 512 + start + 64, :] = low


def prepare(w_first, b_first, w_second, b_second, w_stride, b_stride, w_depth, b_depth, w_head):
    shape = jax.ShapeDtypeStruct
    return pl.pallas_call(
        prepare_kernel,
        out_shape=(
            shape((128, 2688), BF),
            shape((32, 384), F32),
            shape((768, 256), BF),
            shape((1, 256), F32),
            shape((256, 128), BF),
            shape((1, 128), F32),
            shape((1536, 256), BF),
            shape((1, 256), F32),
            shape((768, 128), BF),
        ),
        in_specs=[pl.BlockSpec(memory_space=VMEM)] * 9,
        out_specs=[pl.BlockSpec(memory_space=VMEM)] * 9,
        compiler_params=pltpu.CompilerParams(vmem_limit_bytes=32 * 1024 * 1024),
        cost_estimate=pl.CostEstimate(flops=1000000, bytes_accessed=4000000, transcendentals=0),
        name="prepare",
    )(
        jnp.transpose(w_first[:, 0], (1, 2, 0)),
        jnp.transpose(w_second, (2, 3, 1, 0)),
        jnp.transpose(w_stride, (2, 3, 1, 0)),
        jnp.transpose(w_depth, (2, 3, 4, 1, 0)),
        jnp.transpose(w_head),
        b_first[None],
        b_second[None],
        b_stride[None],
        b_depth[None],
    )


def local(
    raw_sections,
    shift_cols,
    shift_rows,
    w_first,
    b_first,
    w_second,
    b_second,
    w_stride,
    b_stride,
    w_depth,
    b_depth,
    w_head,
    b_head,
):
    pos = jnp.stack([lax.axis_index("tile"), lax.axis_index("sec")]).astype(jnp.int32)
    weights = prepare(
        w_first, b_first, w_second, b_second, w_stride, b_stride, w_depth, b_depth, w_head
    )
    copies = jnp.broadcast_to(raw_sections[None], (TILES,) + raw_sections.shape)
    gathered = lax.all_to_all(copies, "tile", 0, 0)
    window = align(gathered, shift_cols, shift_rows, pos)
    before = lax.ppermute(window[1:], "sec", [(i, i + 1) for i in range(SECS - 1)])
    after = lax.ppermute(window[:1], "sec", [(i + 1, i) for i in range(SECS - 1)])
    window = jnp.concatenate([before, window, after], axis=0)
    return main(pos, window, *weights, b_head)


def solution(mesh):
    in_specs = (P("sec", None, "tile"), P("sec"), P("sec")) + (P(),) * 10
    out_specs = P(None, "sec", None, "tile")
    return jax.shard_map(local, mesh=mesh, in_specs=in_specs, out_specs=out_specs, check_vma=False)
```

profile of v0, /device:TPU:97, one launch (start us, length us, event | category | flops | bytes accessed | tf_op | source)
XLA Modules:
  0.0 64.6 jit_solution(14319516601843303484)
XLA Ops:
  0.0 2.1 %broadcast_in_dim.18 = bf16[16,2,128,128]{3,2,1,0:T(8,128)(2,1)} broadcast(bf16[2,128,128]{2,1,0:T(8,128)(2,1)} %param.13), dimensions={1,2,3} | broadcast | bytes 1114112 | tf_op jit(solution)/shard_map/broadcast_in_dim | solution.py:343
  2.1 6.8 %all-to-all-start = ((bf16[16,2,128,128]{3,2,1,0:T(8,128)(2,1)}), bf16[16,2,128,128]{3,2,1,0:T(8,128)(2,1)S(1)}, u32[]{:S(2)}, u32[]{:S(2)}) async-start(bf16[16,2,128,128]{3,2,1,0:T(8,128)(2,1)} %broadcast_in_dim.18), calls=%async_computation | async-start | bytes 2097152 | tf_op jit(solution)/shard_map/all_to_all | solution.py:344
  8.8 0.6 pad_add_fusion.pos
  9.4 15.4 %all-to-all-done.gathered = bf16[16,2,128,128]{3,2,1,0:T(8,128)(2,1)S(1)} async-done(((bf16[16,2,128,128]{3,2,1,0:T(8,128)(2,1)}), bf16[16,2,128,128]{3,2,1,0:T(8,128)(2,1)S(1)}, u32[]{:S(2)}, u32[]{:S(2)}) %all-to-all-start) | async-done | bytes 1048608 | tf_op jit(solution)/shard_map/all_to_all | solution.py:344
  24.8 0.0 copy-start.8
  24.8 1.0 %copy-done.8 = bf16[16,2,128,128]{3,2,1,0:T(8,128)(2,1)} copy-done((bf16[16,2,128,128]{3,2,1,0:T(8,128)(2,1)}, bf16[16,2,128,128]{3,2,1,0:T(8,128)(2,1)S(1)}, u32[]{:S(2)}) %copy-start.8) | copy-done | bytes 1048600
  25.8 2.7 %align.1 = bf16[2,128,256]{2,1,0:T(8,128)(2,1)} custom-call(s32[2]{0:T(128)} %cols.1, s32[2]{0:T(128)} %rows.1, s32[2]{0:T(128)} %pad_add_fusion.pos, bf16[16,2,128,128]{3,2,1,0:T(8,128)(2,1)} %copy-done.8), custom_call_target="tpu_custom_call" | custom-call | tf_op jit(solution)/shard_map/align/pallas_call | solution.py:59
  28.5 0.0 copy-start.11
  28.5 0.0 copy-start.12
  28.5 0.0 copy-start
  28.5 0.9 %fusion = (bf16[1,128,256]{2,1,0:T(8,128)(2,1)S(1)}, bf16[1,128,256]{2,1,0:T(8,128)(2,1)S(1)}) fusion(bf16[2,128,256]{2,1,0:T(8,128)(2,1)} %align.1), kind=kLoop, calls=%fused_computation.2 | loop fusion | bytes 262144 | tf_op jit(solution)/shard_map/slice | solution.py:346
  29.5 0.0 copy-start.10
  29.5 7.4 %collective-permute-start = (bf16[1,128,256]{2,1,0:T(8,128)(2,1)S(1)}, bf16[1,128,256]{2,1,0:T(8,128)(2,1)S(1)}, u32[]{:S(2)}, u32[]{:S(2)}) collective-permute-start(bf16[1,128,256]{2,1,0:T(8,128)(2,1)S(1)} %get-tuple-element.23), channel_id=1, source_target_pairs={{0,16},{16,32},{32,48},{48,64},{64,80},{80,96},{96,112},{112,128},... | collective-permute-start | bytes 196616 | tf_op jit(solution)/shard_map/ppermute | solution.py:346
  36.9 1.9 %collective-permute-start.1 = (bf16[1,128,256]{2,1,0:T(8,128)(2,1)S(1)}, bf16[1,128,256]{2,1,0:T(8,128)(2,1)S(1)}, u32[]{:S(2)}, u32[]{:S(2)}) collective-permute-start(bf16[1,128,256]{2,1,0:T(8,128)(2,1)S(1)} %get-tuple-element.24), channel_id=1, source_target_pairs={{16,0},{32,16},{48,32},{64,48},{80,64},{96,80},{112,96},{128,112},... | collective-permute-start | bytes 196616 | tf_op jit(solution)/shard_map/ppermute | solution.py:347
  38.8 0.0 copy-done.11
  38.8 0.1 copy.15
  38.9 0.0 copy-done.12
  38.9 0.1 copy.16
  39.0 0.0 copy-done.10
  39.0 0.0 copy-start.6
  39.0 0.1 copy.14
  39.1 0.0 copy-start.1
  39.1 0.0 copy-start.3
  39.2 0.0 copy-start.4
  39.2 0.0 copy-start.5
  39.2 0.0 copy-done
  39.2 0.5 copy-done.6
  39.7 0.2 copy-done.1
  39.8 0.0 copy-done.3
  39.8 0.0 copy-done.4
  39.8 0.0 copy-done.5
  39.8 0.0 copy-start.9
  39.8 0.8 %prepare.1 = (bf16[128,2688]{1,0:T(8,128)(2,1)S(1)}, f32[32,384]{1,0:T(8,128)S(1)}, bf16[768,256]{1,0:T(8,128)(2,1)S(1)}, f32[1,256]{1,0:T(1,128)S(1)}, bf16[256...) custom-call(bf16[3,3,32]{2,1,0:T(4,128)(2,1)S(1)} %bitcast.17, ...), custom_call_target="tpu_custom_call" | custom-call | flops 1000000 | bytes 4000000 | tf_op jit(solution)/shard_map/prepare/pallas_call | solution.py:293
  40.6 0.0 collective-permute-done
  40.6 3.1 %collective-permute-done.1 = bf16[1,128,256]{2,1,0:T(8,128)(2,1)S(1)} collective-permute-done((bf16[1,128,256]{2,1,0:T(8,128)(2,1)S(1)}, bf16[1,128,256]{2,1,0:T(8,128)(2,1)S(1)}, u32[]{:S(2)}, u32[]{:S(2)}) %collective-permute-start.1) | collective-permute-done | bytes 65568 | tf_op jit(solution)/shard_map/ppermute | solution.py:347
  43.7 0.0 copy-done.9
  43.7 0.0 copy-start.2
  43.7 0.0 copy-start.7
  43.7 0.6 copy-done.2
  44.3 0.1 copy-done.7
  44.4 20.2 %convs.1 = f32[3,2,64,64]{3,2,1,0:T(8,128)} custom-call(s32[2]{0:T(128)S(1)} %copy-done.2, bf16[4,128,256]{2,1,0:T(8,128)(2,1)S(1)} %pad_maximum_fusion.window, bf16[128,2688]{1,0:T(8,128)(2,1)S(1)} %get-tuple-element.14.w1, f32[32,384]{1,0:T(8,128)S(1)} %get-tuple-element.15.bias1, bf16[768,256]{1,0:T(8,128)(2,1)S(1)} %get-tuple-element.16.w2, ...), custom_call_target="tpu_custom_call" | custom-call | tf_op jit(solution)/shard_map/convs/pallas_call | solution.py:191
  (1 shorter events, 0.0 us)
Async XLA Ops:
  2.1 22.7 %all-to-all-start = ((bf16[16,2,128,128]{3,2,1,0:T(8,128)(2,1)}), bf16[16,2,128,128]{3,2,1,0:T(8,128)(2,1)S(1)}, u32[]{:S(2)}, u32[]{:S(2)}) async-start(bf16[16,2,128,128]{3,2,1,0:T(8,128)(2,1)} %broadcast_in_dim.18), calls=%async_computation | async-start | bytes 2097152 | tf_op jit(solution)/shard_map/all_to_all | solution.py:344
  24.8 1.0 %copy-start.8 = (bf16[16,2,128,128]{3,2,1,0:T(8,128)(2,1)}, bf16[16,2,128,128]{3,2,1,0:T(8,128)(2,1)S(1)}, u32[]{:S(2)}) copy-start(bf16[16,2,128,128]{3,2,1,0:T(8,128)(2,1)S(1)} %all-to-all-done.gathered) | copy-start | bytes 3145732
  28.5 10.3 %copy-start.11 = (bf16[32,32,2,2]{1,3,2,0:T(2,128)(2,1)S(1)}, bf16[32,32,2,2]{1,3,2,0:T(2,128)(2,1)}, u32[]{:S(2)}) copy-start(bf16[32,32,2,2]{1,3,2,0:T(2,128)(2,1)} %param.20) | copy-start | bytes 24580
  28.5 10.4 %copy-start.12 = (f32[3,64]{1,0:T(4,128)S(1)}, f32[3,64]{1,0:T(4,128)}, u32[]{:S(2)}) copy-start(f32[3,64]{1,0:T(4,128)} %param.24) | copy-start | bytes 2308
  28.5 10.7 %copy-start = (bf16[64,32,3,3,3]{0,1,4,3,2:T(8,128)(2,1)S(1)}, bf16[64,32,3,3,3]{0,1,4,3,2:T(8,128)(2,1)}, u32[]{:S(2)}) copy-start(bf16[64,32,3,3,3]{0,1,4,3,2:T(8,128)(2,1)} %param.22) | copy-start | bytes 331780
  29.5 9.5 %copy-start.10 = (bf16[32,32,3,3]{1,0,3,2:T(8,128)(2,1)S(1)}, bf16[32,32,3,3]{1,0,3,2:T(8,128)(2,1)}, u32[]{:S(2)}) copy-start(bf16[32,32,3,3]{1,0,3,2:T(8,128)(2,1)} %param.18) | copy-start | bytes 55300
  29.5 11.1 %collective-permute-start = (bf16[1,128,256]{2,1,0:T(8,128)(2,1)S(1)}, bf16[1,128,256]{2,1,0:T(8,128)(2,1)S(1)}, u32[]{:S(2)}, u32[]{:S(2)}) collective-permute-start(bf16[1,128,256]{2,1,0:T(8,128)(2,1)S(1)} %get-tuple-element.23), channel_id=1, source_target_pairs={{0,16},{16,32},{32,48},{48,64},{64,80},{80,96},{96,112},{112,128},... | collective-permute-start | bytes 196616 | tf_op jit(solution)/shard_map/ppermute | solution.py:346
  36.9 6.8 %collective-permute-start.1 = (bf16[1,128,256]{2,1,0:T(8,128)(2,1)S(1)}, bf16[1,128,256]{2,1,0:T(8,128)(2,1)S(1)}, u32[]{:S(2)}, u32[]{:S(2)}) collective-permute-start(bf16[1,128,256]{2,1,0:T(8,128)(2,1)S(1)} %get-tuple-element.24), channel_id=1, source_target_pairs={{16,0},{32,16},{48,32},{64,48},{80,64},{96,80},{112,96},{128,112},... | collective-permute-start | bytes 196616 | tf_op jit(solution)/shard_map/ppermute | solution.py:347
  39.0 0.7 %copy-start.6 = (f32[64]{0:T(128)S(1)}, f32[64]{0:T(128)}, u32[]{:S(2)}) copy-start(f32[64]{0:T(128)} %param.23) | copy-start | bytes 772
  39.1 0.7 %copy-start.1 = (bf16[32,1,3,3]{0,3,2,1:T(4,128)(2,1)S(1)}, bf16[32,1,3,3]{0,3,2,1:T(4,128)(2,1)}, u32[]{:S(2)}) copy-start(bf16[32,1,3,3]{0,3,2,1:T(4,128)(2,1)} %param.16) | copy-start | bytes 1732
  39.1 0.7 %copy-start.3 = (f32[32]{0:T(128)S(1)}, f32[32]{0:T(128)}, u32[]{:S(2)}) copy-start(f32[32]{0:T(128)} %param.17) | copy-start | bytes 388
  39.2 0.7 %copy-start.4 = (f32[32]{0:T(128)S(1)}, f32[32]{0:T(128)}, u32[]{:S(2)}) copy-start(f32[32]{0:T(128)} %param.19) | copy-start | bytes 388
  39.2 0.7 %copy-start.5 = (f32[32]{0:T(128)S(1)}, f32[32]{0:T(128)}, u32[]{:S(2)}) copy-start(f32[32]{0:T(128)} %param.21) | copy-start | bytes 388
  39.8 3.8 %copy-start.9 = (bf16[2,128,256]{2,1,0:T(8,128)(2,1)S(1)}, bf16[2,128,256]{2,1,0:T(8,128)(2,1)}, u32[]{:S(2)}) copy-start(bf16[2,128,256]{2,1,0:T(8,128)(2,1)} %align.1) | copy-start | bytes 393220
  43.7 0.6 copy-start.2
  43.7 0.7 %copy-start.7 = (f32[3]{0:T(128)S(1)}, f32[3]{0:T(128)}, u32[]{:S(2)}) copy-start(f32[3]{0:T(128)} %bh.1) | copy-start | bytes 40
where the time goes:
time: 65 us; the launch traced here: 64.6 us
  Pallas kernels  23.7 us (36%)
  waiting for transfers between devices  18.4 us (28%)
  starting transfers between devices  16.1 us (25%)
  local copies, waits for them, and re-layouts  5.61 us (9%)
    pallas_call x1, Pallas kernels, main(): pl.pallas_call(main_kernel, out_shape=jax.ShapeDtypeStruct((3, 2, 64, 64)...  20.2 us
    all_to_all x1, waiting for transfers between devices, local(): gathered = lax.all_to_all(copies, 'tile', 0, 0)  15.4 us
    ppermute x1, starting transfers between devices, local(): lax.ppermute(window[1:], 'sec', [(i, i + 1) for i in range(SECS - 1)])  7.39 us
    all_to_all x1, starting transfers between devices, local(): gathered = lax.all_to_all(copies, 'tile', 0, 0)  6.75 us
    ppermute x1, waiting for transfers between devices, local(): lax.ppermute(window[:1], 'sec', [(i + 1, i) for i in range(SECS - 1)])  3.06 us
    pallas_call x1, Pallas kernels, align(): pl.pallas_call(align_kernel, out_shape=jax.ShapeDtypeStruct((2, 128, 256)...  2.7 us
    unnamed x29, local copies, waits for them, and re-layouts  2.63 us
    broadcast_in_dim x1, local copies, waits for them, and re-layouts, local(): copies = jnp.broadcast_to(raw_sections[None], (TILES,) + raw_sections.shape)  2.06 us
  transfers between devices with their start and end apart: 3, of which 2 were waited for; matrix products, arithmetic and copies ran while one was open for 1% of the time, Pallas kernels for 1%

commit v1 on v0

--- a/solution.py
+++ b/solution.py
@@ -70,7 +70,7 @@
     )(cols, rows, pos, gathered)
 
 
-def front(tile, window, w1, bias1, w2, bias2, ws, biass, left, right, feats, strided):
+def front(tile, window, w1, bias1, w2, bias2, ws, biass, left, right, feats, second, strided):
     value = window.astype(F32)
     left[2:130, :] = value[:, 0:128]
     right[2:130, :] = value[:, 128:256]
@@ -106,11 +106,12 @@
     from_below = (lane >= 96) & (row < 31)
     kept = (lane >= 32) & (lane < 96)
     for p in range(6):
-        second = jnp.dot(
+        made = jnp.dot(
             feats[:, 384 * p : 384 * p + 768], w2[...], preferred_element_type=F32
         )
-        second = jnp.maximum(second + bias2[...], 0.0).astype(BF)
-        made = jnp.dot(second, ws[...], preferred_element_type=F32)
+        second[p] = jnp.maximum(made + bias2[...], 0.0).astype(BF)
+    for p in range(6):
+        made = jnp.dot(second[p], ws[...], preferred_element_type=F32)
         made = jnp.maximum(made + biass[...], 0.0)
         down = pltpu.roll(made, 1, 0).reshape(SG, 32, 128)
         up = pltpu.roll(made, SG * 32 - 1, 0).reshape(SG, 32, 128)
@@ -129,48 +130,94 @@
         strided[1, 32] = jnp.zeros((32, 128), BF)
 
 
+def clear_edges(left, right):
+    for side in (left, right):
+        side[0:2, :] = jnp.zeros((2, 128), F32)
+        side[130:136, :] = jnp.zeros((6, 128), F32)
+
+
+def own_kernel(pos, window, w1, bias1, w2, bias2, ws, biass, out, left, right, feats, second):
+    clear_edges(left, right)
+
+    def one(z, carry):
+        front(
+            pos[0], window[z], w1, bias1, w2, bias2, ws, biass, left, right, feats, second, out.at[z]
+        )
+        return carry
+
+    lax.fori_loop(0, 2, one, 0)
+
+
+SCRATCH = [
+    pltpu.VMEM((136, 128), F32),
+    pltpu.VMEM((136, 128), F32),
+    pltpu.VMEM((SG * 32, 2688), BF),
+    pltpu.VMEM((6, SG * 32, 256), BF),
+]
+
+
+def own(pos, window, *weights):
+    return pl.pallas_call(
+        own_kernel,
+        out_shape=jax.ShapeDtypeStruct((2, 2, 33, 32, 128), BF),
+        in_specs=[pl.BlockSpec(memory_space=SMEM)] + [pl.BlockSpec(memory_space=VMEM)] * 7,
+        out_specs=pl.BlockSpec(memory_space=VMEM),
+        scratch_shapes=SCRATCH,
+        compiler_params=pltpu.CompilerParams(vmem_limit_bytes=24 * 1024 * 1024),
+        cost_estimate=pl.CostEstimate(flops=4000000000, bytes_accessed=4000000, transcendentals=0),
+        name="own",
+    )(pos, window, *weights)
+
+
 def main_kernel(
-    pos, window, w1, bias1, w2, bias2, ws, biass, wd, biasd, wh, bh, out, left, right, feats, strided
+    pos, before, after, middle, w1, bias1, w2, bias2, ws, biass, wd, biasd, wh, bh, out,
+    left, right, feats, second, outer, deeps,
 ):
     tile = pos[0]
     sec = pos[1]
-    for side in (left, right):
-        side[0:2, :] = jnp.zeros((2, 128), F32)
-        side[130:136, :] = jnp.zeros((6, 128), F32)
+    clear_edges(left, right)
+
+    @pl.when(sec == 0)
+    def _():
+        outer[0] = jnp.zeros((2, 33, 32, 128), BF)
+
+    @pl.when(sec == SECS - 1)
+    def _():
+        outer[1] = jnp.zeros((2, 33, 32, 128), BF)
 
     def one(z, carry):
-        front(
-            tile, window[z], w1, bias1, w2, bias2, ws, biass, left, right, feats, strided.at[z]
-        )
+        @pl.when((sec > 0) | (z > 0))
+        def _():
+            @pl.when((sec < SECS - 1) | (z < 1))
+            def _():
+                window = jnp.where(z == 0, before[0], after[0])
+                front(
+                    tile, window, w1, bias1, w2, bias2, ws, biass, left, right, feats, second, outer.at[z]
+                )
+
         return carry
 
-    lax.fori_loop(0, 4, one, 0)
-
-    @pl.when(sec == 0)
-    def _():
-        strided[0] = jnp.zeros((2, 33, 32, 128), BF)
-
-    @pl.when(sec == SECS - 1)
-    def _():
-        strided[3] = jnp.zeros((2, 33, 32, 128), BF)
-
+    lax.fori_loop(0, 2, one, 0)
+    for z in range(2):
+        for part in range(4):
+            blocks = []
+            for dz in range(3):
+                source = (outer.at[0], middle.at[0], middle.at[1], outer.at[1])[z + dz]
+                for kx in range(4):
+                    first = kx // 2 + 8 * part
+                    blocks.append(source[kx % 2, first : first + 8].reshape(256, 128))
+            patch = jnp.concatenate(blocks, axis=1)
+            deep = jnp.dot(patch, wd[...], preferred_element_type=F32)
+            deep = jnp.maximum(deep + biasd[...], 0.0)
+            high = deep.astype(BF)
+            deeps[z, part, :, 0:256] = high
+            deeps[z, part, :, 256:512] = (deep - high.astype(F32)).astype(BF)
+            deeps[z, part, :, 512:768] = high
     lane = floor_lane((32, 128), 1)
     for z in range(2):
         spots = [jnp.zeros((32, 128), F32)] * 3
         for part in range(4):
-            blocks = []
-            for dz in range(3):
-                for kx in range(4):
-                    first = kx // 2 + 8 * part
-                    blocks.append(strided[z + dz, kx % 2, first : first + 8].reshape(256, 128))
-            patch = jnp.concatenate(blocks, axis=1)
-            deep = jnp.dot(patch, wd[...], preferred_element_type=F32)
-            deep = jnp.maximum(deep + biasd[...], 0.0)
-            high = deep.astype(BF)
-            low = (deep - high.astype(F32)).astype(BF)
-            logits = jnp.dot(
-                jnp.concatenate([high, low, high], axis=1), wh[...], preferred_element_type=F32
-            )
+            logits = jnp.dot(deeps[z, part], wh[...], preferred_element_type=F32)
             for step in range(8):
                 m = 8 * part + step
                 slab = logits[32 * step : 32 * step + 32]
@@ -187,23 +234,19 @@
                 out[k, z, pl.ds(yp, 32, stride=2), :] = value
 
 
-def main(pos, window, *weights):
+def main(pos, before, after, middle, *weights):
     return pl.pallas_call(
         main_kernel,
         out_shape=jax.ShapeDtypeStruct((3, 2, 64, 64), F32),
         in_specs=[pl.BlockSpec(memory_space=SMEM)]
-        + [pl.BlockSpec(memory_space=VMEM)] * 10
+        + [pl.BlockSpec(memory_space=VMEM)] * 12
         + [pl.BlockSpec(memory_space=SMEM)],
         out_specs=pl.BlockSpec(memory_space=VMEM),
-        scratch_shapes=[
-            pltpu.VMEM((136, 128), F32),
-            pltpu.VMEM((136, 128), F32),
-            pltpu.VMEM((SG * 32, 2688), BF),
-            pltpu.VMEM((4, 2, 33, 32, 128), BF),
-        ],
-        compiler_params=pltpu.CompilerParams(vmem_limit_bytes=48 * 1024 * 1024),
+        scratch_shapes=SCRATCH
+        + [pltpu.VMEM((2, 2, 33, 32, 128), BF), pltpu.VMEM((2, 4, 256, 768), BF)],
+        compiler_params=pltpu.CompilerParams(vmem_limit_bytes=32 * 1024 * 1024),
         name="convs",
-    )(pos, window, *weights)
+    )(pos, before, after, middle, *weights)
 
 
 def prepare_kernel(
@@ -345,8 +388,8 @@
     window = align(gathered, shift_cols, shift_rows, pos)
     before = lax.ppermute(window[1:], "sec", [(i, i + 1) for i in range(SECS - 1)])
     after = lax.ppermute(window[:1], "sec", [(i + 1, i) for i in range(SECS - 1)])
-    window = jnp.concatenate([before, window, after], axis=0)
-    return main(pos, window, *weights, b_head)
+    middle = own(pos, window, *weights[:6])
+    return main(pos, before, after, middle, *weights, b_head)
 
 
 def solution(mesh):

time: 65 us -> 52.7 us (0.81)
  Pallas kernels: 23.7 us -> 16.9 us
  waiting for transfers between devices: 18.4 us -> 14.2 us
  local copies, waits for them, and re-layouts: 5.61 us -> 4.21 us
    pallas_call x1, Pallas kernels: 20.2 us -> 8.53 us  [main(): pl.pallas_call(main_kernel, out_shape=jax.ShapeDtypeStruct((3, 2, 64, 64)...]
    pallas_call x0 -> x1, Pallas kernels: none -> 4.9 us  [own(): pl.pallas_call(own_kernel, out_shape=jax.ShapeDtypeStruct((2, 2, 33, 32,...]
    ppermute x1, waiting for transfers between devices: 3.06 us -> 0.01 us  [local(): lax.ppermute(window[:1], 'sec', [(i + 1, i) for i in range(SECS - 1)])]
    ppermute x1, starting transfers between devices: 7.39 us -> 4.65 us  [local(): lax.ppermute(window[1:], 'sec', [(i, i + 1) for i in range(SECS - 1)])]
    ppermute x1, starting transfers between devices: 1.92 us -> 4.52 us  [local(): lax.ppermute(window[:1], 'sec', [(i + 1, i) for i in range(SECS - 1)])]
    unnamed x29 -> x27, local copies, waits for them, and re-layouts: 2.63 us -> 1.25 us
    all_to_all x1, waiting for transfers between devices: 15.4 us -> 14.2 us  [local(): gathered = lax.all_to_all(copies, 'tile', 0, 0)]
  transfers between devices with their start and end apart: 3 -> 3, of which waited for: 2 -> 1; matrix products, arithmetic and copies ran while one was open for 1% -> 2% of each run, Pallas kernels for 1% -> 11%
where the time goes in v1:
time: 52.7 us; the launch traced here: 52.3 us
  Pallas kernels  16.9 us (32%)
  starting transfers between devices  16.1 us (31%)
  waiting for transfers between devices  14.2 us (27%)
  local copies, waits for them, and re-layouts  4.21 us (8%)
  other arithmetic  0.67 us (1%)
    all_to_all x1, waiting for transfers between devices, local(): gathered = lax.all_to_all(copies, 'tile', 0, 0)  14.2 us
    pallas_call x1, Pallas kernels, main(): pl.pallas_call(main_kernel, out_shape=jax.ShapeDtypeStruct((3, 2, 64, 64)...  8.53 us
    all_to_all x1, starting transfers between devices, local(): gathered = lax.all_to_all(copies, 'tile', 0, 0)  6.95 us
    pallas_call x1, Pallas kernels, own(): pl.pallas_call(own_kernel, out_shape=jax.ShapeDtypeStruct((2, 2, 33, 32,...  4.9 us
    ppermute x1, starting transfers between devices, local(): lax.ppermute(window[1:], 'sec', [(i, i + 1) for i in range(SECS - 1)])  4.65 us
    ppermute x1, starting transfers between devices, local(): lax.ppermute(window[:1], 'sec', [(i + 1, i) for i in range(SECS - 1)])  4.52 us
    pallas_call x1, Pallas kernels, align(): pl.pallas_call(align_kernel, out_shape=jax.ShapeDtypeStruct((2, 128, 256)...  2.7 us
    broadcast_in_dim x1, local copies, waits for them, and re-layouts, local(): copies = jnp.broadcast_to(raw_sections[None], (TILES,) + raw_sections.shape)  2.08 us
  transfers between devices with their start and end apart: 3, of which 1 were waited for; matrix products, arithmetic and copies ran while one was open for 2% of the time, Pallas kernels for 11%

profile of v1, /device:TPU:97, one launch (start us, length us, event | category | flops | bytes accessed | tf_op | source)
XLA Modules:
  0.0 52.3 jit_solution(2371952425132257054)
XLA Ops:
  0.0 2.1 %broadcast_in_dim.18 = bf16[16,2,128,128]{3,2,1,0:T(8,128)(2,1)} broadcast(bf16[2,128,128]{2,1,0:T(8,128)(2,1)} %param.13), dimensions={1,2,3} | broadcast | bytes 1114112 | tf_op jit(solution)/shard_map/broadcast_in_dim | solution.py:386
  2.1 0.0 copy-start.10
  2.1 0.0 copy-start.11
  2.1 0.0 copy-start.9
  2.1 0.0 copy-start.1
  2.1 0.0 copy-start.2
  2.1 0.0 copy-start.4
  2.1 0.0 copy-start.5
  2.1 0.0 copy-start.6
  2.1 0.0 copy-start.7
  2.1 6.9 %all-to-all-start = ((bf16[16,2,128,128]{3,2,1,0:T(8,128)(2,1)}), bf16[16,2,128,128]{3,2,1,0:T(8,128)(2,1)}, u32[]{:S(2)}, u32[]{:S(2)}) async-start(bf16[16,2,128,128]{3,2,1,0:T(8,128)(2,1)} %broadcast_in_dim.18), calls=%async_computation | async-start | bytes 2097152 | tf_op jit(solution)/shard_map/all_to_all | solution.py:387
  9.1 0.0 copy-done.10
  9.1 0.1 copy.15
  9.2 0.0 copy-done.11
  9.2 0.1 copy.16
  9.3 0.0 copy-done.9
  9.3 0.1 copy.14
  9.4 0.0 copy-done.1
  9.4 0.0 copy-done.2
  9.5 0.0 copy-done.4
  9.5 0.0 copy-done.5
  9.5 0.0 copy-done.6
  9.5 0.0 copy-done.7
  9.5 0.8 %prepare.1 = (bf16[128,2688]{1,0:T(8,128)(2,1)S(1)}, f32[32,384]{1,0:T(8,128)S(1)}, bf16[768,256]{1,0:T(8,128)(2,1)S(1)}, f32[1,256]{1,0:T(1,128)S(1)}, bf16[256...) custom-call(bf16[3,3,32]{2,1,0:T(4,128)(2,1)S(1)} %bitcast.17, ...), custom_call_target="tpu_custom_call" | custom-call | flops 1000000 | bytes 4000000 | tf_op jit(solution)/shard_map/prepare/pallas_call | solution.py:336
  10.3 0.7 %pad_add_fusion.pos = s32[2]{0:T(128)} fusion(s32[1]{0:T(128)} %bitcast.1, s32[1]{0:T(128)} %bitcast), kind=kLoop, calls=%fused_computation | loop fusion | flops 2 | bytes 16 | tf_op jit(solution)/shard_map/stack | solution.py:382
  10.9 0.0 copy-start.3
  10.9 14.2 %all-to-all-done.gathered = bf16[16,2,128,128]{3,2,1,0:T(8,128)(2,1)} async-done(((bf16[16,2,128,128]{3,2,1,0:T(8,128)(2,1)}), bf16[16,2,128,128]{3,2,1,0:T(8,128)(2,1)}, u32[]{:S(2)}, u32[]{:S(2)}) %all-to-all-start) | async-done | bytes 1048608 | tf_op jit(solution)/shard_map/all_to_all | solution.py:387
  25.1 2.7 %align.1.window = bf16[2,128,256]{2,1,0:T(8,128)(2,1)} custom-call(s32[2]{0:T(128)} %cols.1, s32[2]{0:T(128)} %rows.1, s32[2]{0:T(128)} %pad_add_fusion.pos, bf16[16,2,128,128]{3,2,1,0:T(8,128)(2,1)} %all-to-all-done.gathered), custom_call_target="tpu_custom_call" | custom-call | tf_op jit(solution)/shard_map/align/pallas_call | solution.py:59
  27.9 0.9 %fusion = (bf16[1,128,256]{2,1,0:T(8,128)(2,1)S(1)}, bf16[1,128,256]{2,1,0:T(8,128)(2,1)S(1)}) fusion(bf16[2,128,256]{2,1,0:T(8,128)(2,1)} %align.1.window), kind=kLoop, calls=%fused_computation.1 | loop fusion | bytes 262144 | tf_op jit(solution)/shard_map/slice | solution.py:390
  28.7 4.5 %collective-permute-start.1 = (bf16[1,128,256]{2,1,0:T(8,128)(2,1)S(1)}, bf16[1,128,256]{2,1,0:T(8,128)(2,1)S(1)}, u32[]{:S(2)}, u32[]{:S(2)}) collective-permute-start(bf16[1,128,256]{2,1,0:T(8,128)(2,1)S(1)} %get-tuple-element.23), channel_id=1, source_target_pairs={{16,0},{32,16},{48,32},{64,48},{80,64},{96,80},{112,96},{128,112},... | collective-permute-start | bytes 196616 | tf_op jit(solution)/shard_map/ppermute | solution.py:390
  33.3 4.7 %collective-permute-start = (bf16[1,128,256]{2,1,0:T(8,128)(2,1)S(1)}, bf16[1,128,256]{2,1,0:T(8,128)(2,1)S(1)}, u32[]{:S(2)}, u32[]{:S(2)}) collective-permute-start(bf16[1,128,256]{2,1,0:T(8,128)(2,1)S(1)} %get-tuple-element.24), channel_id=1, source_target_pairs={{0,16},{16,32},{32,48},{48,64},{64,80},{80,96},{96,112},{112,128},... | collective-permute-start | bytes 196616 | tf_op jit(solution)/shard_map/ppermute | solution.py:389
  37.9 0.0 copy-done.3
  37.9 0.0 copy-start
  38.0 0.9 %copy-done = bf16[2,128,256]{2,1,0:T(8,128)(2,1)S(1)} copy-done((bf16[2,128,256]{2,1,0:T(8,128)(2,1)S(1)}, bf16[2,128,256]{2,1,0:T(8,128)(2,1)}, u32[]{:S(2)}) %copy-start) | copy-done | bytes 131096
  38.8 0.0 copy-start.8
  38.9 4.9 %own.1.middle = bf16[2,2,33,32,128]{4,3,2,1,0:T(8,128)(2,1)S(1)} custom-call(s32[2]{0:T(128)S(1)} %copy-done.3, bf16[2,128,256]{2,1,0:T(8,128)(2,1)S(1)} %copy-done, bf16[128,2688]{1,0:T(8,128)(2,1)S(1)} %get-tuple-element.14.w1, f32[32,384]{1,0:T(8,128)S(1)} %get-tuple-element.15.bias1, bf16[768,256]{1,0:T(8,128)(2,1)S(1)} %get-tuple-element.16.w2, ...), custom_call_target="tpu_custom_call" | custom-call | flops 4000000000 | bytes 4000000 | tf_op jit(solution)/shard_map/own/pallas_call | solution.py:160
  43.8 0.0 collective-permute-done.1.after
  43.8 0.0 collective-permute-done.before
  43.8 0.0 copy-done.8
  43.8 8.5 %convs.1 = f32[3,2,64,64]{3,2,1,0:T(8,128)} custom-call(s32[2]{0:T(128)S(1)} %copy-done.3, bf16[1,128,256]{2,1,0:T(8,128)(2,1)S(1)} %collective-permute-done.before, bf16[1,128,256]{2,1,0:T(8,128)(2,1)S(1)} %collective-permute-done.1.after, bf16[2,2,33,32,128]{4,3,2,1,0:T(8,128)(2,1)S(1)} %own.1.middle, bf16[128,2688]{1,0:T(8,128)(2,1)S(1)} %get-tuple-element.14.w1, ...), custom_call_target="tpu_custom_call" | custom-call | tf_op jit(solution)/shard_map/convs/pallas_call | solution.py:238
Async XLA Ops:
  2.1 7.0 %copy-start.10 = (bf16[32,32,2,2]{1,3,2,0:T(2,128)(2,1)S(1)}, bf16[32,32,2,2]{1,3,2,0:T(2,128)(2,1)}, u32[]{:S(2)}) copy-start(bf16[32,32,2,2]{1,3,2,0:T(2,128)(2,1)} %param.20) | copy-start | bytes 24580
  2.1 7.1 %copy-start.11 = (f32[3,64]{1,0:T(4,128)S(1)}, f32[3,64]{1,0:T(4,128)}, u32[]{:S(2)}) copy-start(f32[3,64]{1,0:T(4,128)} %param.24) | copy-start | bytes 2308
  2.1 7.2 %copy-start.9 = (bf16[32,32,3,3]{1,0,3,2:T(8,128)(2,1)S(1)}, bf16[32,32,3,3]{1,0,3,2:T(8,128)(2,1)}, u32[]{:S(2)}) copy-start(bf16[32,32,3,3]{1,0,3,2:T(8,128)(2,1)} %param.18) | copy-start | bytes 55300
  2.1 7.4 %copy-start.1 = (bf16[64,32,3,3,3]{0,1,4,3,2:T(8,128)(2,1)S(1)}, bf16[64,32,3,3,3]{0,1,4,3,2:T(8,128)(2,1)}, u32[]{:S(2)}) copy-start(bf16[64,32,3,3,3]{0,1,4,3,2:T(8,128)(2,1)} %param.22) | copy-start | bytes 331780
  2.1 7.4 %copy-start.2 = (bf16[32,1,3,3]{0,3,2,1:T(4,128)(2,1)S(1)}, bf16[32,1,3,3]{0,3,2,1:T(4,128)(2,1)}, u32[]{:S(2)}) copy-start(bf16[32,1,3,3]{0,3,2,1:T(4,128)(2,1)} %param.16) | copy-start | bytes 1732
  2.1 7.4 %copy-start.4 = (f32[32]{0:T(128)S(1)}, f32[32]{0:T(128)}, u32[]{:S(2)}) copy-start(f32[32]{0:T(128)} %param.17) | copy-start | bytes 388
  2.1 7.4 %copy-start.5 = (f32[32]{0:T(128)S(1)}, f32[32]{0:T(128)}, u32[]{:S(2)}) copy-start(f32[32]{0:T(128)} %param.19) | copy-start | bytes 388
  2.1 7.4 %copy-start.6 = (f32[32]{0:T(128)S(1)}, f32[32]{0:T(128)}, u32[]{:S(2)}) copy-start(f32[32]{0:T(128)} %param.21) | copy-start | bytes 388
  2.1 7.4 %copy-start.7 = (f32[64]{0:T(128)S(1)}, f32[64]{0:T(128)}, u32[]{:S(2)}) copy-start(f32[64]{0:T(128)} %param.23) | copy-start | bytes 772
  2.1 23.0 %all-to-all-start = ((bf16[16,2,128,128]{3,2,1,0:T(8,128)(2,1)}), bf16[16,2,128,128]{3,2,1,0:T(8,128)(2,1)}, u32[]{:S(2)}, u32[]{:S(2)}) async-start(bf16[16,2,128,128]{3,2,1,0:T(8,128)(2,1)} %broadcast_in_dim.18), calls=%async_computation | async-start | bytes 2097152 | tf_op jit(solution)/shard_map/all_to_all | solution.py:387
  10.9 27.0 %copy-start.3 = (s32[2]{0:T(128)S(1)}, s32[2]{0:T(128)}, u32[]{:S(2)}) copy-start(s32[2]{0:T(128)} %pad_add_fusion.pos) | copy-start | bytes 28
  28.7 15.0 %collective-permute-start.1 = (bf16[1,128,256]{2,1,0:T(8,128)(2,1)S(1)}, bf16[1,128,256]{2,1,0:T(8,128)(2,1)S(1)}, u32[]{:S(2)}, u32[]{:S(2)}) collective-permute-start(bf16[1,128,256]{2,1,0:T(8,128)(2,1)S(1)} %get-tuple-element.23), channel_id=1, source_target_pairs={{16,0},{32,16},{48,32},{64,48},{80,64},{96,80},{112,96},{128,112},... | collective-permute-start | bytes 196616 | tf_op jit(solution)/shard_map/ppermute | solution.py:390
  33.3 10.5 %collective-permute-start = (bf16[1,128,256]{2,1,0:T(8,128)(2,1)S(1)}, bf16[1,128,256]{2,1,0:T(8,128)(2,1)S(1)}, u32[]{:S(2)}, u32[]{:S(2)}) collective-permute-start(bf16[1,128,256]{2,1,0:T(8,128)(2,1)S(1)} %get-tuple-element.24), channel_id=1, source_target_pairs={{0,16},{16,32},{32,48},{48,64},{64,80},{80,96},{96,112},{112,128},... | collective-permute-start | bytes 196616 | tf_op jit(solution)/shard_map/ppermute | solution.py:389
  37.9 0.9 %copy-start = (bf16[2,128,256]{2,1,0:T(8,128)(2,1)S(1)}, bf16[2,128,256]{2,1,0:T(8,128)(2,1)}, u32[]{:S(2)}) copy-start(bf16[2,128,256]{2,1,0:T(8,128)(2,1)} %align.1.window) | copy-start | bytes 393220
  38.8 4.9 %copy-start.8 = (f32[3]{0:T(128)S(1)}, f32[3]{0:T(128)}, u32[]{:S(2)}) copy-start(f32[3]{0:T(128)} %bh.1) | copy-start | bytes 40

commit v2 on v1

--- a/solution.py
+++ b/solution.py
@@ -21,29 +21,56 @@
     return lax.broadcasted_iota(jnp.int32, shape, dim)
 
 
-def align_kernel(cols, rows, pos, gathered, out, tiles, lifted, sems):
-    tile = pos[0]
-    copies = []
+def first_tile_of(tile, shift):
+    start = 128 * tile - BLK * shift - HALO
+    first = lax.shift_right_arithmetic(start, 7)
+    return first, start - first * 128
+
+
+def chosen(sources, index, z):
+    value = sources[0][z]
+    for k in range(1, len(sources)):
+        value = jnp.where(index == k, sources[k][z], value)
+    return value
+
+
+def pick_kernel(spot, mine, one, two, three, keep, send_1, send_2, send_3):
+    sources = (mine, one, two, three)
+    tile = spot[4]
+    place = tile & 3
     for z in range(2):
-        start = 128 * tile - BLK * cols[z] - HALO
-        first_tile = lax.shift_right_arithmetic(start, 7)
-        for k in range(3):
-            index = jnp.clip(first_tile + k, 0, TILES - 1)
-            copy = pltpu.make_async_copy(gathered.at[index, z], tiles.at[z, k], sems.at[z, k])
-            copy.start()
-            copies.append(copy)
+        for step, out in enumerate((keep, send_1, send_2, send_3)):
+            goal = (tile - place) + ((place + step) & 3)
+            first, _ = first_tile_of(goal, spot[z])
+            wanted = first + ((place - first) & 3)
+            index = (lax.shift_right_arithmetic(tile, 2) - lax.shift_right_arithmetic(wanted, 2)) & 3
+            out[z] = chosen(sources, index, z)
+
+
+def pick(spot, *sources):
+    return pl.pallas_call(
+        pick_kernel,
+        out_shape=[jax.ShapeDtypeStruct((2, 128, 128), BF)] * 4,
+        in_specs=[pl.BlockSpec(memory_space=SMEM)] + [pl.BlockSpec(memory_space=VMEM)] * 4,
+        out_specs=[pl.BlockSpec(memory_space=VMEM)] * 4,
+        compiler_params=pltpu.CompilerParams(vmem_limit_bytes=8 * 1024 * 1024),
+        cost_estimate=pl.CostEstimate(flops=0, bytes_accessed=16000000, transcendentals=0),
+        name="pick",
+    )(spot, *sources)
+
+
+def align_kernel(spot, keep, one, two, three, low_section, high_section, lifted):
+    sources = (keep, one, two, three)
+    tile = spot[4]
     lifted[0:32, :] = jnp.zeros((32, 256), F32)
     lifted[160:192, :] = jnp.zeros((32, 256), F32)
     lane = floor_lane((128, 128), 1)
-    for z in range(2):
-        start = 128 * tile - BLK * cols[z] - HALO
-        first_tile = lax.shift_right_arithmetic(start, 7)
-        offset = start - first_tile * 128
+    for z, out in enumerate((low_section, high_section)):
+        first, offset = first_tile_of(tile, spot[z])
         turned = []
         for k in range(3):
-            copies[3 * z + k].wait()
-            inside = ((first_tile + k >= 0) & (first_tile + k < TILES)).astype(F32)
-            value = tiles[z, k].astype(F32) * inside
+            inside = ((first + k >= 0) & (first + k < TILES)).astype(F32)
+            value = chosen(sources, (tile - first - k) & 3, z).astype(F32) * inside
             turned.append(pltpu.roll(value, 128 - offset, 1))
         low = jnp.where(lane < 128 - offset, turned[0], turned[1])
         high = jnp.where(lane < 128 - offset, turned[1], turned[2])
@@ -51,23 +78,21 @@
         high = jnp.where((tile == TILES - 1) & (lane >= HALO), 0.0, high)
         lifted[32:160, 0:128] = low
         lifted[32:160, 128:256] = high
-        base = pl.multiple_of(32 - BLK * rows[z], BLK)
-        out[z] = lifted[pl.ds(base, 128), :].astype(BF)
-
-
-def align(gathered, cols, rows, pos):
+        base = pl.multiple_of(32 - BLK * spot[2 + z], BLK)
+        out[0] = lifted[pl.ds(base, 128), :].astype(BF)
+
+
+def align(spot, *sources):
     return pl.pallas_call(
         align_kernel,
-        out_shape=jax.ShapeDtypeStruct((2, 128, 256), BF),
-        in_specs=[pl.BlockSpec(memory_space=SMEM)] * 3 + [pl.BlockSpec(memory_space=pl.ANY)],
-        out_specs=pl.BlockSpec(memory_space=VMEM),
-        scratch_shapes=[
-            pltpu.VMEM((2, 3, 128, 128), BF),
-            pltpu.VMEM((192, 256), F32),
-            pltpu.SemaphoreType.DMA((2, 3)),
-        ],
+        out_shape=[jax.ShapeDtypeStruct((1, 128, 256), BF)] * 2,
+        in_specs=[pl.BlockSpec(memory_space=SMEM)] + [pl.BlockSpec(memory_space=VMEM)] * 4,
+        out_specs=[pl.BlockSpec(memory_space=VMEM)] * 2,
+        scratch_shapes=[pltpu.VMEM((192, 256), F32)],
+        compiler_params=pltpu.CompilerParams(vmem_limit_bytes=8 * 1024 * 1024),
+        cost_estimate=pl.CostEstimate(flops=0, bytes_accessed=4000000, transcendentals=0),
         name="align",
-    )(cols, rows, pos, gathered)
+    )(spot, *sources)
 
 
 def front(tile, window, w1, bias1, w2, bias2, ws, biass, left, right, feats, second, strided):
@@ -136,12 +161,13 @@
         side[130:136, :] = jnp.zeros((6, 128), F32)
 
 
-def own_kernel(pos, window, w1, bias1, w2, bias2, ws, biass, out, left, right, feats, second):
+def own_kernel(spot, low_section, high_section, w1, bias1, w2, bias2, ws, biass, out, left, right, feats, second):
     clear_edges(left, right)
 
     def one(z, carry):
+        window = jnp.where(z == 0, low_section[0], high_section[0])
         front(
-            pos[0], window[z], w1, bias1, w2, bias2, ws, biass, left, right, feats, second, out.at[z]
+            spot[4], window, w1, bias1, w2, bias2, ws, biass, left, right, feats, second, out.at[z]
         )
         return carry
 
@@ -156,25 +182,25 @@
 ]
 
 
-def own(pos, window, *weights):
+def own(spot, low_section, high_section, *weights):
     return pl.pallas_call(
         own_kernel,
         out_shape=jax.ShapeDtypeStruct((2, 2, 33, 32, 128), BF),
-        in_specs=[pl.BlockSpec(memory_space=SMEM)] + [pl.BlockSpec(memory_space=VMEM)] * 7,
+        in_specs=[pl.BlockSpec(memory_space=SMEM)] + [pl.BlockSpec(memory_space=VMEM)] * 8,
         out_specs=pl.BlockSpec(memory_space=VMEM),
         scratch_shapes=SCRATCH,
         compiler_params=pltpu.CompilerParams(vmem_limit_bytes=24 * 1024 * 1024),
         cost_estimate=pl.CostEstimate(flops=4000000000, bytes_accessed=4000000, transcendentals=0),
         name="own",
-    )(pos, window, *weights)
+    )(spot, low_section, high_section, *weights)
 
 
 def main_kernel(
-    pos, before, after, middle, w1, bias1, w2, bias2, ws, biass, wd, biasd, wh, bh, out,
+    spot, before, after, middle, w1, bias1, w2, bias2, ws, biass, wd, biasd, wh, bh, out,
     left, right, feats, second, outer, deeps,
 ):
-    tile = pos[0]
-    sec = pos[1]
+    tile = spot[4]
+    sec = spot[5]
     clear_edges(left, right)
 
     @pl.when(sec == 0)
@@ -234,7 +260,7 @@
                 out[k, z, pl.ds(yp, 32, stride=2), :] = value
 
 
-def main(pos, before, after, middle, *weights):
+def main(spot, before, after, middle, *weights):
     return pl.pallas_call(
         main_kernel,
         out_shape=jax.ShapeDtypeStruct((3, 2, 64, 64), F32),
@@ -246,12 +272,14 @@
         + [pltpu.VMEM((2, 2, 33, 32, 128), BF), pltpu.VMEM((2, 4, 256, 768), BF)],
         compiler_params=pltpu.CompilerParams(vmem_limit_bytes=32 * 1024 * 1024),
         name="convs",
-    )(pos, before, after, middle, *weights)
-
-
-def prepare_kernel(
-    t1, t2, ts, td, th, b1, b2, bs, bd, w1, bias1, w2, bias2, ws, biass, wd, biasd, wh
-):
+    )(spot, before, after, middle, *weights)
+
+
+def prepare_kernel(*refs):
+    small, t2, ts, td = refs[:4]
+    w1, bias1, w2, bias2, ws, biass, wd, biasd, wh = refs[4:]
+    b1, b2, bs = (small[12 + i : 13 + i, 0:32] for i in range(3))
+    bd = small[15:16, :]
     row = floor_lane((128, 384), 0)
     group = floor_lane((128, 384), 1) // 32
     dy = row // 16 - group % 6
@@ -259,24 +287,24 @@
     base = jnp.zeros((128, 384), F32)
     for a in range(3):
         for b in range(3):
-            spread = jnp.concatenate([t1[a, b : b + 1, :].astype(F32)] * 12, axis=1)
+            spread = jnp.concatenate([small[3 * a + b : 3 * a + b + 1, 0:32]] * 12, axis=1)
             base = jnp.where((dy == a) & (dx == b), spread, base)
     for q in range(7):
         turned = pltpu.roll(base, 2 * q, 0) if q else base
         w1[:, 384 * q : 384 * (q + 1)] = turned.astype(BF)
-    lone = jnp.concatenate([b1[...]] * 12, axis=1)
+    lone = jnp.concatenate([b1] * 12, axis=1)
     row = floor_lane((32, 384), 0)
     group = floor_lane((32, 384), 1) // 32 % 6
     outside = ((row == 0) & (group == 0)) | ((row == 31) & (group == 5))
     bias1[...] = jnp.where(outside, OFF, lone)
-    bias2[...] = jnp.concatenate([b2[...]] * 8, axis=1)
-    biass[...] = jnp.concatenate([bs[...]] * 4, axis=1)
-    biasd[...] = jnp.concatenate([bd[...]] * 4, axis=1)
+    bias2[...] = jnp.concatenate([b2] * 8, axis=1)
+    biass[...] = jnp.concatenate([bs] * 4, axis=1)
+    biasd[...] = jnp.concatenate([bd] * 4, axis=1)
 
     lane = floor_lane((32, 128), 1)
     none = jnp.zeros((32, 128), F32)
     tiled = [
-        [jnp.concatenate([t2[a, b].astype(F32)] * 4, axis=1) for b in range(3)] for a in range(3)
+        [jnp.concatenate([t2[a, b].astype(F32).T] * 4, axis=1) for b in range(3)] for a in range(3)
     ]
     for kx in range(4):
         for xp in range(2):
@@ -317,12 +345,13 @@
                     wd[start : start + 32, 128 * xp : 128 * xp + 128] = made.astype(BF)
 
     lane = floor_lane((64, 128), 1)
+    heads = jnp.concatenate([small[9:12, :], jnp.zeros((5, 64), F32)], axis=0).T
     for xp in range(2):
         for yp in range(2):
             made = jnp.zeros((64, 128), F32)
             for k in range(3):
                 c = 3 * yp + k
-                made = jnp.where(lane == 64 * (c % 2) + 2 * (c // 2) + xp, th[:, k : k + 1], made)
+                made = jnp.where(lane == 64 * (c % 2) + 2 * (c // 2) + xp, heads[:, k : k + 1], made)
             high = made.astype(BF)
             low = (made - high.astype(F32)).astype(BF)
             start = 64 * (2 * xp + yp)
@@ -333,6 +362,21 @@
 
 def prepare(w_first, b_first, w_second, b_second, w_stride, b_stride, w_depth, b_depth, w_head):
     shape = jax.ShapeDtypeStruct
+    lines = (
+        jnp.transpose(w_first[:, 0], (1, 2, 0)).reshape(9, 32).astype(F32),
+        w_head,
+        b_first[None],
+        b_second[None],
+        b_stride[None],
+        b_depth[None],
+    )
+    small = jnp.concatenate([jnp.pad(v, ((0, 0), (0, 64 - v.shape[1]))) for v in lines], axis=0)
+    given = (
+        small,
+        jnp.transpose(w_second, (2, 3, 0, 1)),
+        jnp.transpose(w_stride, (2, 3, 1, 0)),
+        jnp.transpose(w_depth, (2, 3, 4, 1, 0)),
+    )
     return pl.pallas_call(
         prepare_kernel,
         out_shape=(
@@ -346,22 +390,12 @@
             shape((1, 256), F32),
             shape((768, 128), BF),
         ),
-        in_specs=[pl.BlockSpec(memory_space=VMEM)] * 9,
+        in_specs=[pl.BlockSpec(memory_space=VMEM)] * 4,
         out_specs=[pl.BlockSpec(memory_space=VMEM)] * 9,
-        compiler_params=pltpu.CompilerParams(vmem_limit_bytes=32 * 1024 * 1024),
+        compiler_params=pltpu.CompilerParams(vmem_limit_bytes=16 * 1024 * 1024),
         cost_estimate=pl.CostEstimate(flops=1000000, bytes_accessed=4000000, transcendentals=0),
         name="prepare",
-    )(
-        jnp.transpose(w_first[:, 0], (1, 2, 0)),
-        jnp.transpose(w_second, (2, 3, 1, 0)),
-        jnp.transpose(w_stride, (2, 3, 1, 0)),
-        jnp.transpose(w_depth, (2, 3, 4, 1, 0)),
-        jnp.transpose(w_head),
-        b_first[None],
-        b_second[None],
-        b_stride[None],
-        b_depth[None],
-    )
+    )(*given)
 
 
 def local(
@@ -379,17 +413,25 @@
     w_head,
     b_head,
 ):
-    pos = jnp.stack([lax.axis_index("tile"), lax.axis_index("sec")]).astype(jnp.int32)
+    place = jnp.stack([lax.axis_index("tile"), lax.axis_index("sec")]).astype(jnp.int32)
+    spot = jnp.concatenate([shift_cols, shift_rows, place])
     weights = prepare(
         w_first, b_first, w_second, b_second, w_stride, b_stride, w_depth, b_depth, w_head
     )
-    copies = jnp.broadcast_to(raw_sections[None], (TILES,) + raw_sections.shape)
-    gathered = lax.all_to_all(copies, "tile", 0, 0)
-    window = align(gathered, shift_cols, shift_rows, pos)
-    before = lax.ppermute(window[1:], "sec", [(i, i + 1) for i in range(SECS - 1)])
-    after = lax.ppermute(window[:1], "sec", [(i + 1, i) for i in range(SECS - 1)])
-    middle = own(pos, window, *weights[:6])
-    return main(pos, before, after, middle, *weights, b_head)
+    columns = [
+        lax.ppermute(raw_sections, "tile", [(i, (i + 4 * k) % TILES) for i in range(TILES)])
+        for k in (1, 2, 3)
+    ]
+    keep, *sends = pick(spot, raw_sections, *columns)
+    pieces = [
+        lax.ppermute(send, "tile", [(i, i - i % 4 + (i + k) % 4) for i in range(TILES)])
+        for k, send in zip((1, 2, 3), sends)
+    ]
+    low_section, high_section = align(spot, keep, *pieces)
+    before = lax.ppermute(high_section, "sec", [(i, i + 1) for i in range(SECS - 1)])
+    after = lax.ppermute(low_section, "sec", [(i + 1, i) for i in range(SECS - 1)])
+    middle = own(spot, low_section, high_section, *weights[:6])
+    return main(spot, before, after, middle, *weights, b_head)
 
 
 def solution(mesh):

time: 52.7 us -> 43.2 us (0.82)
  waiting for transfers between devices: 14.2 us -> 0.02 us
  starting transfers between devices: 16.1 us -> 19.4 us
  local copies, waits for them, and re-layouts: 4.21 us -> 6.89 us
  Pallas kernels: 16.9 us -> 15.6 us
    all_to_all x1 -> x0, waiting for transfers between devices: 14.2 us -> none  [local(): gathered = lax.all_to_all(copies, 'tile', 0, 0)]
    ppermute x2 -> x8, starting transfers between devices: 9.18 us -> 19.4 us  [the longest x1 7 us: local(): lax.ppermute(high_section, 'sec', [(i, i + 1) for i in range(SECS - 1)])]
    all_to_all x1 -> x0, starting transfers between devices: 6.95 us -> none  [local(): gathered = lax.all_to_all(copies, 'tile', 0, 0)]
    unnamed x27 -> x9, local copies, waits for them, and re-layouts: 1.25 us -> 3.51 us
    broadcast_in_dim x1 -> x0, local copies, waits for them, and re-layouts: 2.08 us -> none  [local(): copies = jnp.broadcast_to(raw_sections[None], (TILES,) + raw_sections.shape)]
    pad x0 -> x3, local copies, waits for them, and re-layouts: none -> 1.98 us  [prepare(): jnp.pad(v, ((0, 0), (0, 64 - v.shape[1])))]
    pallas_call x1 -> x2, Pallas kernels: 2.7 us -> 1.35 us  [the longest x1 0.73 us: align(): pl.pallas_call(align_kernel, out_shape=[jax.ShapeDtypeStruct((1, 128, 256...]
    slice x1 -> x0, local copies, waits for them, and re-layouts: 0.88 us -> none  [local(): window[:1]]
  transfers between devices with their start and end apart: 3 -> 8, of which waited for: 1 -> 0; matrix products, arithmetic and copies ran while one was open for 2% -> 12% of each run, Pallas kernels for 11% -> 13%
where the time goes in v2:
time: 43.2 us; the launch traced here: 42.8 us
  starting transfers between devices  19.4 us (45%)
  Pallas kernels  15.6 us (36%)
  local copies, waits for them, and re-layouts  6.89 us (16%)
  other arithmetic  0.76 us (2%)
    pallas_call x1, Pallas kernels, main(): pl.pallas_call(main_kernel, out_shape=jax.ShapeDtypeStruct((3, 2, 64, 64)...  8.58 us
    ppermute x1, starting transfers between devices, local(): lax.ppermute(high_section, 'sec', [(i, i + 1) for i in range(SECS - 1)])  7 us
    ppermute x3, starting transfers between devices, local(): lax.ppermute(raw_sections, 'tile', [(i, (i + 4 * k) % TILES) for i in ran...  5.59 us
    pallas_call x1, Pallas kernels, own(): pl.pallas_call(own_kernel, out_shape=jax.ShapeDtypeStruct((2, 2, 33, 32,...  4.93 us
    ppermute x3, starting transfers between devices, local(): lax.ppermute(send, 'tile', [(i, i - i % 4 + (i + k) % 4) for i in range(T...  4.89 us
    unnamed x9, local copies, waits for them, and re-layouts  3.51 us
    pad x3, local copies, waits for them, and re-layouts, prepare(): jnp.pad(v, ((0, 0), (0, 64 - v.shape[1])))  1.98 us
    ppermute x1, starting transfers between devices, local(): lax.ppermute(low_section, 'sec', [(i + 1, i) for i in range(SECS - 1)])  1.92 us
  transfers between devices with their start and end apart: 8, of which 0 were waited for; matrix products, arithmetic and copies ran while one was open for 12% of the time, Pallas kernels for 13%

profile of v2, /device:TPU:97, one launch (start us, length us, event | category | flops | bytes accessed | tf_op | source)
XLA Modules:
  0.0 42.8 jit_solution(15390242288839987083)
XLA Ops:
  0.0 2.9 %collective-permute-start.1 = (bf16[2,128,128]{2,1,0:T(8,128)(2,1)}, bf16[2,128,128]{2,1,0:T(8,128)(2,1)S(1)}, u32[]{:S(2)}, u32[]{:S(2)}) collective-permute-start(bf16[2,128,128]{2,1,0:T(8,128)(2,1)} %mine.1), channel_id=1, source_target_pairs={{0,8},{1,9},{2,10},{3,11},{4,12},{5,13},{6,14},{7,15},{8,0},{9,1},... | collective-permute-start | bytes 196616 | tf_op jit(solution)/shard_map/ppermute | solution.py:422
  2.9 0.4 collective-permute-start
  3.3 2.3 %collective-permute-start.2 = (bf16[2,128,128]{2,1,0:T(8,128)(2,1)}, bf16[2,128,128]{2,1,0:T(8,128)(2,1)S(1)}, u32[]{:S(2)}, u32[]{:S(2)}) collective-permute-start(bf16[2,128,128]{2,1,0:T(8,128)(2,1)} %mine.1), channel_id=1, source_target_pairs={{0,12},{1,13},{2,14},{3,15},{4,0},{5,1},{6,2},{7,3},{8,4},{9,5},{1... | collective-permute-start | bytes 196616 | tf_op jit(solution)/shard_map/ppermute | solution.py:422
  5.6 0.7 %pad.19 = f32[1,64]{1,0:T(1,128)S(1)} pad(f32[1,32]{1,0:T(1,128)} %bitcast.17, f32[]{:T(128)} %constant.11.clone.1), padding=0_0x0_32 | pad | bytes 388 | tf_op jit(solution)/shard_map/jit(_pad)/pad | solution.py:373
  6.3 0.7 %pad.20 = f32[1,64]{1,0:T(1,128)S(1)} pad(f32[1,32]{1,0:T(1,128)} %bitcast.18, f32[]{:T(128)} %constant.11.clone.1), padding=0_0x0_32 | pad | bytes 388 | tf_op jit(solution)/shard_map/jit(_pad)/pad | solution.py:373
  6.9 0.7 %pad.21 = f32[1,64]{1,0:T(1,128)S(1)} pad(f32[1,32]{1,0:T(1,128)} %bitcast.19, f32[]{:T(128)} %constant.11.clone.1), padding=0_0x0_32 | pad | bytes 388 | tf_op jit(solution)/shard_map/jit(_pad)/pad | solution.py:373
  7.6 0.7 %convert_element_type.18 = bf16[9,32]{1,0:T(8,128)(2,1)S(1)} reshape(bf16[3,3,32]{2,1,0:T(4,128)(2,1)} %bitcast.15) | data formatting | bytes 1152 | tf_op jit(solution)/shard_map/convert_element_type | solution.py:366
  8.3 0.8 %copy.14 = bf16[32,32,2,2]{0,1,3,2:T(8,128)(2,1)S(1)} copy(bf16[32,32,2,2]{1,3,2,0:T(2,128)(2,1)} %param.20) | data formatting | bytes 16384 | tf_op args[7]
  9.1 0.8 %pad_add_fusion.spot = s32[6]{0:T(128)S(1)} fusion(s32[1]{0:T(128)} %bitcast.1, s32[1]{0:T(128)} %bitcast, s32[2]{0:T(128)} %param.15, s32[2]{0:T(128)} %param.14), kind=kLoop, calls=%fused_computation.1 | loop fusion | flops 18 | bytes 48 | tf_op jit(solution)/shard_map/concatenate | solution.py:417
  9.9 0.0 collective-permute-done.1.two
  9.9 0.0 collective-permute-done.one
  9.9 0.0 collective-permute-done.2.three
  9.9 0.0 copy-start.2
  9.9 0.8 %copy-done.2 = bf16[2,128,128]{2,1,0:T(8,128)(2,1)S(1)} copy-done((bf16[2,128,128]{2,1,0:T(8,128)(2,1)S(1)}, bf16[2,128,128]{2,1,0:T(8,128)(2,1)}, u32[]{:S(2)}) %copy-start.2) | copy-done | bytes 65560
  10.7 0.6 %pick.1 = (bf16[2,128,128]{2,1,0:T(8,128)(2,1)S(1)}, bf16[2,128,128]{2,1,0:T(8,128)(2,1)S(1)}, bf16[2,128,128]{2,1,0:T(8,128)(2,1)S(1)}, bf16[2,128,128]{2,1,0:T(8,128)(2,1)S(1)}) custom-call(s32[6]{0:T(128)S(1)} %pad_add_fusion.spot, bf16[2,128,128]{2,1,0:T(8,128)(2,1)S(1)} %copy-done.2, bf16[2,128,128]{2,1,0:T(8,128)(2,1)S(1)} %collective-permute-done.one, ...), custom_call_target="tpu_custom_call" | custom-call | bytes 16000000 | tf_op jit(solution)/shard_map/pick/pallas_call | solution.py:51
  11.4 1.3 %collective-permute-start.3 = (bf16[2,128,128]{2,1,0:T(8,128)(2,1)S(1)}, bf16[2,128,128]{2,1,0:T(8,128)(2,1)S(1)}, u32[]{:S(2)}, u32[]{:S(2)}) collective-permute-start(bf16[2,128,128]{2,1,0:T(8,128)(2,1)S(1)} %get-tuple-element.21), channel_id=1, source_target_pairs={{0,1},{1,2},{2,3},{3,0},{4,5},{5,6},{6,7},{7,4},{8,9},{9,10},{10,1... | collective-permute-start | bytes 196616 | tf_op jit(solution)/shard_map/ppermute | solution.py:427
  12.7 2.5 %collective-permute-start.4 = (bf16[2,128,128]{2,1,0:T(8,128)(2,1)S(1)}, bf16[2,128,128]{2,1,0:T(8,128)(2,1)S(1)}, u32[]{:S(2)}, u32[]{:S(2)}) collective-permute-start(bf16[2,128,128]{2,1,0:T(8,128)(2,1)S(1)} %get-tuple-element.22), channel_id=1, source_target_pairs={{0,2},{1,3},{2,0},{3,1},{4,6},{5,7},{6,4},{7,5},{8,10},{9,11},{10,... | collective-permute-start | bytes 196616 | tf_op jit(solution)/shard_map/ppermute | solution.py:427
  15.1 1.2 %collective-permute-start.5 = (bf16[2,128,128]{2,1,0:T(8,128)(2,1)S(1)}, bf16[2,128,128]{2,1,0:T(8,128)(2,1)S(1)}, u32[]{:S(2)}, u32[]{:S(2)}) collective-permute-start(bf16[2,128,128]{2,1,0:T(8,128)(2,1)S(1)} %get-tuple-element.23), channel_id=1, source_target_pairs={{0,3},{1,0},{2,1},{3,2},{4,7},{5,4},{6,5},{7,6},{8,11},{9,8},{10,9... | collective-permute-start | bytes 196616 | tf_op jit(solution)/shard_map/ppermute | solution.py:427
  16.3 0.7 %concatenate.7.refs_0_ = f32[16,64]{1,0:T(8,128)S(1)} concatenate(f32[9,64]{1,0:T(8,128)S(1)} %pad_convert_fusion, f32[3,64]{1,0:T(4,128)} %param.24, f32[1,64]{1,0:T(1,128)S(1)} %pad.19, f32[1,64]{1,0:T(1,128)S(1)} %pad.20, f32[1,64]{1,0:T(1,128)S(1)} %pad.21, f32[1,64]{1,0:T(1,128)} %bitcast.16), dimensions={0} | concatenate | bytes 8192 | tf_op jit(solution)/shard_map/concatenate | solution.py:373
  17.0 0.0 copy-start
  17.0 0.9 %copy-done = bf16[64,32,3,3,3]{0,1,4,3,2:T(8,128)(2,1)S(1)} copy-done((bf16[64,32,3,3,3]{0,1,4,3,2:T(8,128)(2,1)S(1)}, bf16[64,32,3,3,3]{0,1,4,3,2:T(8,128)(2,1)}, u32[]{:S(2)}) %copy-start) | copy-done | bytes 110616
  17.9 0.0 copy-start.1
  17.9 0.9 %copy-done.1 = bf16[32,32,3,3]{1,0,3,2:T(8,128)(2,1)S(1)} copy-done((bf16[32,32,3,3]{1,0,3,2:T(8,128)(2,1)S(1)}, bf16[32,32,3,3]{1,0,3,2:T(8,128)(2,1)}, u32[]{:S(2)}) %copy-start.1) | copy-done | bytes 18456
  18.8 0.8 %prepare.1 = (bf16[128,2688]{1,0:T(8,128)(2,1)S(1)}, f32[32,384]{1,0:T(8,128)S(1)}, bf16[768,256]{1,0:T(8,128)(2,1)S(1)}, f32[1,256]{1,0:T(1,128)S(1)}, bf16[256...) custom-call(f32[16,64]{1,0:T(8,128)S(1)} %concatenate.7.refs_0_, ...), custom_call_target="tpu_custom_call" | custom-call | flops 1000000 | bytes 4000000 | tf_op jit(solution)/shard_map/prepare/pallas_call | solution.py:380
  19.6 0.0 collective-permute-done.3.one
  19.6 0.0 collective-permute-done.4.two
  19.6 0.0 collective-permute-done.5.three
  19.6 0.7 %align.1 = (bf16[1,128,256]{2,1,0:T(8,128)(2,1)S(1)}, bf16[1,128,256]{2,1,0:T(8,128)(2,1)S(1)}) custom-call(s32[6]{0:T(128)S(1)} %pad_add_fusion.spot, bf16[2,128,128]{2,1,0:T(8,128)(2,1)S(1)} %get-tuple-element.20.keep, bf16[2,128,128]{2,1,0:T(8,128)(2,1)S(1)} %collective-permute-done.3.one, bf16[2,128,128]{2,1,0:T(8,128)(2,1)S(1)} %collective-permute-done.4.two, ...), custom_call_target="tpu_custom_call" | custom-call | bytes 4000000 | tf_op jit(solution)/shard_map/align/pallas_call | solution.py:86
  20.3 7.0 %collective-permute-start.6 = (bf16[1,128,256]{2,1,0:T(8,128)(2,1)S(1)}, bf16[1,128,256]{2,1,0:T(8,128)(2,1)S(1)}, u32[]{:S(2)}, u32[]{:S(2)}) collective-permute-start(bf16[1,128,256]{2,1,0:T(8,128)(2,1)S(1)} %get-tuple-element.24.high_section), channel_id=1, source_target_pairs={{0,16},{16,32},{32,48},{48,64},{64,80},{80,96},{96,112},{112,128},... | collective-permute-start | bytes 196616 | tf_op jit(solution)/shard_map/ppermute | solution.py:431
  27.3 1.9 %collective-permute-start.7 = (bf16[1,128,256]{2,1,0:T(8,128)(2,1)S(1)}, bf16[1,128,256]{2,1,0:T(8,128)(2,1)S(1)}, u32[]{:S(2)}, u32[]{:S(2)}) collective-permute-start(bf16[1,128,256]{2,1,0:T(8,128)(2,1)S(1)} %get-tuple-element.25.low_section), channel_id=1, source_target_pairs={{16,0},{32,16},{48,32},{64,48},{80,64},{96,80},{112,96},{128,112},... | collective-permute-start | bytes 196616 | tf_op jit(solution)/shard_map/ppermute | solution.py:432
  29.3 0.0 copy-start.3
  29.3 4.9 %own.1.middle = bf16[2,2,33,32,128]{4,3,2,1,0:T(8,128)(2,1)S(1)} custom-call(s32[6]{0:T(128)S(1)} %pad_add_fusion.spot, bf16[1,128,256]{2,1,0:T(8,128)(2,1)S(1)} %get-tuple-element.25.low_section, bf16[1,128,256]{2,1,0:T(8,128)(2,1)S(1)} %get-tuple-element.24.high_section, bf16[128,2688]{1,0:T(8,128)(2,1)S(1)} %get-tuple-element.26.w1, ...), custom_call_target="tpu_custom_call" | custom-call | flops 4000000000 | bytes 4000000 | tf_op jit(solution)/shard_map/own/pallas_call | solution.py:186
  34.2 0.0 collective-permute-done.6.before
  34.2 0.0 collective-permute-done.7.after
  34.2 0.0 copy-done.3
  34.2 8.6 %convs.1 = f32[3,2,64,64]{3,2,1,0:T(8,128)} custom-call(s32[6]{0:T(128)S(1)} %pad_add_fusion.spot, bf16[1,128,256]{2,1,0:T(8,128)(2,1)S(1)} %collective-permute-done.6.before, bf16[1,128,256]{2,1,0:T(8,128)(2,1)S(1)} %collective-permute-done.7.after, bf16[2,2,33,32,128]{4,3,2,1,0:T(8,128)(2,1)S(1)} %own.1.middle, ...), custom_call_target="tpu_custom_call" | custom-call | tf_op jit(solution)/shard_map/convs/pallas_call | solution.py:264
  (1 shorter events, 0.0 us)
Async XLA Ops:
  0.0 9.9 %collective-permute-start.1 = (bf16[2,128,128]{2,1,0:T(8,128)(2,1)}, bf16[2,128,128]{2,1,0:T(8,128)(2,1)S(1)}, u32[]{:S(2)}, u32[]{:S(2)}) collective-permute-start(bf16[2,128,128]{2,1,0:T(8,128)(2,1)} %mine.1), channel_id=1, source_target_pairs={{0,8},{1,9},{2,10},{3,11},{4,12},{5,13},{6,14},{7,15},{8,0},{9,1},... | collective-permute-start | bytes 196616 | tf_op jit(solution)/shard_map/ppermute | solution.py:422
  2.9 7.0 %collective-permute-start = (bf16[2,128,128]{2,1,0:T(8,128)(2,1)}, bf16[2,128,128]{2,1,0:T(8,128)(2,1)S(1)}, u32[]{:S(2)}, u32[]{:S(2)}) collective-permute-start(bf16[2,128,128]{2,1,0:T(8,128)(2,1)} %mine.1), channel_id=1, source_target_pairs={{0,4},{1,5},{2,6},{3,7},{4,8},{5,9},{6,10},{7,11},{8,12},{9,13},{1... | collective-permute-start | bytes 196616 | tf_op jit(solution)/shard_map/ppermute | solution.py:422
  3.3 6.6 %collective-permute-start.2 = (bf16[2,128,128]{2,1,0:T(8,128)(2,1)}, bf16[2,128,128]{2,1,0:T(8,128)(2,1)S(1)}, u32[]{:S(2)}, u32[]{:S(2)}) collective-permute-start(bf16[2,128,128]{2,1,0:T(8,128)(2,1)} %mine.1), channel_id=1, source_target_pairs={{0,12},{1,13},{2,14},{3,15},{4,0},{5,1},{6,2},{7,3},{8,4},{9,5},{1... | collective-permute-start | bytes 196616 | tf_op jit(solution)/shard_map/ppermute | solution.py:422
  9.9 0.8 %copy-start.2 = (bf16[2,128,128]{2,1,0:T(8,128)(2,1)S(1)}, bf16[2,128,128]{2,1,0:T(8,128)(2,1)}, u32[]{:S(2)}) copy-start(bf16[2,128,128]{2,1,0:T(8,128)(2,1)} %mine.1) | copy-start | bytes 196612
  11.4 8.2 %collective-permute-start.3 = (bf16[2,128,128]{2,1,0:T(8,128)(2,1)S(1)}, bf16[2,128,128]{2,1,0:T(8,128)(2,1)S(1)}, u32[]{:S(2)}, u32[]{:S(2)}) collective-permute-start(bf16[2,128,128]{2,1,0:T(8,128)(2,1)S(1)} %get-tuple-element.21), channel_id=1, source_target_pairs={{0,1},{1,2},{2,3},{3,0},{4,5},{5,6},{6,7},{7,4},{8,9},{9,10},{10,1... | collective-permute-start | bytes 196616 | tf_op jit(solution)/shard_map/ppermute | solution.py:427
  12.7 6.9 %collective-permute-start.4 = (bf16[2,128,128]{2,1,0:T(8,128)(2,1)S(1)}, bf16[2,128,128]{2,1,0:T(8,128)(2,1)S(1)}, u32[]{:S(2)}, u32[]{:S(2)}) collective-permute-start(bf16[2,128,128]{2,1,0:T(8,128)(2,1)S(1)} %get-tuple-element.22), channel_id=1, source_target_pairs={{0,2},{1,3},{2,0},{3,1},{4,6},{5,7},{6,4},{7,5},{8,10},{9,11},{10,... | collective-permute-start | bytes 196616 | tf_op jit(solution)/shard_map/ppermute | solution.py:427
  15.1 4.5 %collective-permute-start.5 = (bf16[2,128,128]{2,1,0:T(8,128)(2,1)S(1)}, bf16[2,128,128]{2,1,0:T(8,128)(2,1)S(1)}, u32[]{:S(2)}, u32[]{:S(2)}) collective-permute-start(bf16[2,128,128]{2,1,0:T(8,128)(2,1)S(1)} %get-tuple-element.23), channel_id=1, source_target_pairs={{0,3},{1,0},{2,1},{3,2},{4,7},{5,4},{6,5},{7,6},{8,11},{9,8},{10,9... | collective-permute-start | bytes 196616 | tf_op jit(solution)/shard_map/ppermute | solution.py:427
  17.0 0.9 %copy-start = (bf16[64,32,3,3,3]{0,1,4,3,2:T(8,128)(2,1)S(1)}, bf16[64,32,3,3,3]{0,1,4,3,2:T(8,128)(2,1)}, u32[]{:S(2)}) copy-start(bf16[64,32,3,3,3]{0,1,4,3,2:T(8,128)(2,1)} %param.22) | copy-start | bytes 331780
  17.9 0.9 %copy-start.1 = (bf16[32,32,3,3]{1,0,3,2:T(8,128)(2,1)S(1)}, bf16[32,32,3,3]{1,0,3,2:T(8,128)(2,1)}, u32[]{:S(2)}) copy-start(bf16[32,32,3,3]{1,0,3,2:T(8,128)(2,1)} %param.18) | copy-start | bytes 55300
  20.3 13.9 %collective-permute-start.6 = (bf16[1,128,256]{2,1,0:T(8,128)(2,1)S(1)}, bf16[1,128,256]{2,1,0:T(8,128)(2,1)S(1)}, u32[]{:S(2)}, u32[]{:S(2)}) collective-permute-start(bf16[1,128,256]{2,1,0:T(8,128)(2,1)S(1)} %get-tuple-element.24.high_section), channel_id=1, source_target_pairs={{0,16},{16,32},{32,48},{48,64},{64,80},{80,96},{96,112},{112,128},... | collective-permute-start | bytes 196616 | tf_op jit(solution)/shard_map/ppermute | solution.py:431
  27.3 6.9 %collective-permute-start.7 = (bf16[1,128,256]{2,1,0:T(8,128)(2,1)S(1)}, bf16[1,128,256]{2,1,0:T(8,128)(2,1)S(1)}, u32[]{:S(2)}, u32[]{:S(2)}) collective-permute-start(bf16[1,128,256]{2,1,0:T(8,128)(2,1)S(1)} %get-tuple-element.25.low_section), channel_id=1, source_target_pairs={{16,0},{32,16},{48,32},{64,48},{80,64},{96,80},{112,96},{128,112},... | collective-permute-start | bytes 196616 | tf_op jit(solution)/shard_map/ppermute | solution.py:432
  29.3 5.0 %copy-start.3 = (f32[3]{0:T(128)S(1)}, f32[3]{0:T(128)}, u32[]{:S(2)}) copy-start(f32[3]{0:T(128)} %bh.1) | copy-start | bytes 40

commit v3 on v2

v3 whole, which is shorter than its diff:
```python
import jax
import jax.numpy as jnp
from jax import lax
from jax.experimental import pallas as pl
from jax.experimental.pallas import tpu as pltpu
from jax.sharding import PartitionSpec as P

BLK = 16
TILES = 16
SECS = 16
HALO = 4
OFF = -1e30
BF = jnp.bfloat16
F32 = jnp.float32
SG = 11
VMEM = pltpu.VMEM
SMEM = pltpu.SMEM


COLS, ROWS, TILE, SEC = 0, 2, 4, 5


def floor_lane(shape, dim):
    return lax.broadcasted_iota(jnp.int32, shape, dim)


def first_tile_of(tile, shift):
    start = 128 * tile - BLK * shift - HALO
    first = lax.shift_right_arithmetic(start, 7)
    return first, start - first * 128


def chosen(sources, index, z):
    value = sources[0][z]
    for k in range(1, len(sources)):
        value = jnp.where(index == k, sources[k][z], value)
    return value


def stage_kernel(given, out):
    out[...] = given[...]


def stage(raw):
    return pl.pallas_call(
        stage_kernel,
        out_shape=jax.ShapeDtypeStruct(raw.shape, raw.dtype),
        in_specs=[pl.BlockSpec(memory_space=VMEM)],
        out_specs=pl.BlockSpec(memory_space=VMEM),
        compiler_params=pltpu.CompilerParams(vmem_limit_bytes=8 * 1024 * 1024),
        cost_estimate=pl.CostEstimate(flops=0, bytes_accessed=4000000, transcendentals=0),
        name="stage",
    )(raw)


def pick_kernel(spot, mine, one, two, three, keep, send_1, send_2, send_3):
    sources = (mine, one, two, three)
    tile = spot[TILE]
    place = tile & 3
    for z in range(2):
        for step, out in enumerate((keep, send_1, send_2, send_3)):
            goal = tile ^ step
            first, _ = first_tile_of(goal, spot[COLS + z])
            wanted = first + ((place - first) & 3)
            index = (lax.shift_right_arithmetic(tile, 2) ^ lax.shift_right_arithmetic(wanted, 2)) & 3
            out[z] = chosen(sources, index, z)


def pick(spot, *sources):
    return pl.pallas_call(
        pick_kernel,
        out_shape=[jax.ShapeDtypeStruct((2, 128, 128), BF)] * 4,
        in_specs=[pl.BlockSpec(memory_space=SMEM)] + [pl.BlockSpec(memory_space=VMEM)] * 4,
        out_specs=[pl.BlockSpec(memory_space=VMEM)] * 4,
        compiler_params=pltpu.CompilerParams(vmem_limit_bytes=8 * 1024 * 1024),
        cost_estimate=pl.CostEstimate(flops=0, bytes_accessed=16000000, transcendentals=0),
        name="pick",
    )(spot, *sources)


def align_kernel(spot, keep, one, two, three, both, to_chip, lifted):
    sources = (keep, one, two, three)
    tile = spot[TILE]
    lifted[0:32, :] = jnp.zeros((32, 256), F32)
    lifted[160:192, :] = jnp.zeros((32, 256), F32)
    lane = floor_lane((128, 128), 1)
    odd = spot[SEC] & 1
    for z in range(2):
        first, offset = first_tile_of(tile, spot[COLS + z])
        turned = []
        for k in range(3):
            inside = ((first + k >= 0) & (first + k < TILES)).astype(F32)
            value = chosen(sources, (tile ^ (first + k)) & 3, z).astype(F32) * inside
            turned.append(pltpu.roll(value, 128 - offset, 1))
        low = jnp.where(lane < 128 - offset, turned[0], turned[1])
        high = jnp.where(lane < 128 - offset, turned[1], turned[2])
        low = jnp.where((tile == 0) & (lane < HALO), 0.0, low)
        high = jnp.where((tile == TILES - 1) & (lane >= HALO), 0.0, high)
        lifted[32:160, 0:128] = low
        lifted[32:160, 128:256] = high
        base = pl.multiple_of(32 - BLK * spot[ROWS + z], BLK)
        window = lifted[pl.ds(base, 128), :].astype(BF)
        both[z] = window

        @pl.when(odd == z)
        def _():
            to_chip[0] = window


def align(spot, *sources):
    return pl.pallas_call(
        align_kernel,
        out_shape=[jax.ShapeDtypeStruct((n, 128, 256), BF) for n in (2, 1)],
        in_specs=[pl.BlockSpec(memory_space=SMEM)] + [pl.BlockSpec(memory_space=VMEM)] * 4,
        out_specs=[pl.BlockSpec(memory_space=VMEM)] * 2,
        scratch_shapes=[pltpu.VMEM((192, 256), F32)],
        compiler_params=pltpu.CompilerParams(vmem_limit_bytes=8 * 1024 * 1024),
        cost_estimate=pl.CostEstimate(flops=0, bytes_accessed=4000000, transcendentals=0),
        name="align",
    )(spot, *sources)


def front(tile, windows, w1, bias1, w2, bias2, ws, biass, left, right, feats, second, strided):
    count = len(windows)
    for side in (left, right):
        side[:, 0:2, :] = jnp.zeros((count, 2, 128), F32)
        side[:, 130:136, :] = jnp.zeros((count, 6, 128), F32)
    lane = floor_lane((32, 128), 1)
    patches = []
    for z in range(count):
        value = windows[z].astype(F32)
        left[z, 2:130, :] = value[:, 0:128]
        right[z, 2:130, :] = value[:, 128:256]
        made = [None] * SG
        for j in range(8):
            low = left[z, pl.ds(j, 32, stride=4), :]
            high = right[z, pl.ds(j, 32, stride=4), :]
            ring = jnp.where(lane < 8, high, low)
            mine = lane // 16 == j
            for g in range(SG):
                source = low if g < SG - 1 else ring
                shift = (16 * j - 12 * g) % 128
                turned = pltpu.roll(source, shift, 1) if shift else source
                made[g] = turned if j == 0 else jnp.where(mine, turned, made[g])
        patches += made
    patch = jnp.concatenate(patches, axis=0).astype(BF)
    groups = count * SG
    low_edge = tile == 0
    high_edge = tile == TILES - 1
    lane = floor_lane((32, 384), 1)
    for q in range(7):
        made = jnp.dot(patch, w1[:, 384 * q : 384 * (q + 1)], preferred_element_type=F32)
        made = jnp.maximum(made.reshape(groups, 32, 384) + bias1[...][None], 0.0)
        feats[:, 384 * q : 384 * (q + 1)] = made.reshape(groups * 32, 384).astype(BF)
        outside = {0: low_edge & (lane < 384), 1: low_edge & (lane < 192)}
        outside.update({5: high_edge & (lane >= 192), 6: high_edge & (lane >= 0)})
        if q in outside:
            for z in range(count):
                g = SG * z + (0 if q < 2 else SG - 1)
                kept = jnp.where(outside[q], 0.0, made[g])
                feats[32 * g : 32 * g + 32, 384 * q : 384 * (q + 1)] = kept.astype(BF)

    for p in range(6):
        made = jnp.dot(
            feats[:, 384 * p : 384 * p + 768], w2[...], preferred_element_type=F32
        )
        second[p] = jnp.maximum(made + bias2[...], 0.0).astype(BF)
    lane = floor_lane((1, 32, 128), 2)
    row = floor_lane((1, 32, 128), 1)
    from_above = (lane < 32) & (row > 0)
    from_below = (lane >= 96) & (row < 31)
    kept = (lane >= 32) & (lane < 96)
    for p in range(6):
        made = jnp.dot(second[p], ws[...], preferred_element_type=F32)
        made = jnp.maximum(made + biass[...], 0.0)
        down = pltpu.roll(made, 1, 0).reshape(groups, 32, 128)
        up = pltpu.roll(made, groups * 32 - 1, 0).reshape(groups, 32, 128)
        made = made.reshape(groups, 32, 128)
        made = jnp.where(kept, made, jnp.where(from_above, down, jnp.where(from_below, up, 0.0)))
        for g in range(groups):
            value = made[g]
            if p == 0 and g % SG == 0:
                value = jnp.where(low_edge, 0.0, value)
            if p == 5 and g % SG == SG - 1:
                value = jnp.where(high_edge, 0.0, value)
            strided[g // SG, p % 2, 3 * (g % SG) + p // 2] = value.astype(BF)


def own_kernel(
    spot, both, w1, bias1, w2, bias2, ws, biass, out, to_core, left, right, feats, second
):
    windows = (both[0], both[1])
    front(
        spot[TILE], windows, w1, bias1, w2, bias2, ws, biass, left, right, feats, second, out
    )
    odd = spot[SEC] & 1

    @pl.when(odd == 0)
    def _():
        to_core[0] = out[1]

    @pl.when(odd == 1)
    def _():
        to_core[0] = out[0]


def scratch(count):
    return [
        pltpu.VMEM((count, 136, 128), F32),
        pltpu.VMEM((count, 136, 128), F32),
        pltpu.VMEM((count * SG * 32, 2688), BF),
        pltpu.VMEM((6, count * SG * 32, 256), BF),
    ]


def features(count):
    return jax.ShapeDtypeStruct((count, 2, 33, 32, 128), BF)


def own(spot, both, *weights):
    return pl.pallas_call(
        own_kernel,
        out_shape=[features(2), features(1)],
        in_specs=[pl.BlockSpec(memory_space=SMEM)] + [pl.BlockSpec(memory_space=VMEM)] * 7,
        out_specs=[pl.BlockSpec(memory_space=VMEM)] * 2,
        scratch_shapes=scratch(2),
        compiler_params=pltpu.CompilerParams(vmem_limit_bytes=24 * 1024 * 1024),
        cost_estimate=pl.CostEstimate(flops=40000000000, bytes_accessed=4000000, transcendentals=0),
        name="own",
    )(spot, both, *weights)


def beyond_kernel(
    spot, window, w1, bias1, w2, bias2, ws, biass, out, left, right, feats, second
):
    sec = spot[SEC]
    front(
        spot[TILE], (window[0],), w1, bias1, w2, bias2, ws, biass, left, right, feats, second, out
    )

    @pl.when((sec == 0) | (sec == SECS - 1))
    def _():
        out[0] = jnp.zeros((2, 33, 32, 128), BF)


def beyond(spot, window, *weights):
    return pl.pallas_call(
        beyond_kernel,
        out_shape=features(1),
        in_specs=[pl.BlockSpec(memory_space=SMEM)] + [pl.BlockSpec(memory_space=VMEM)] * 7,
        out_specs=pl.BlockSpec(memory_space=VMEM),
        scratch_shapes=scratch(1),
        compiler_params=pltpu.CompilerParams(vmem_limit_bytes=24 * 1024 * 1024),
        cost_estimate=pl.CostEstimate(flops=20000000000, bytes_accessed=4000000, transcendentals=0),
        name="beyond",
    )(spot, window, *weights)


def main_kernel(spot, chip_side, core_side, middle, wd, biasd, wh, bh, out, outer, deeps):
    odd = spot[SEC] & 1
    outer[odd] = chip_side[0]
    outer[1 - odd] = core_side[0]
    for z in range(2):
        for part in range(4):
            blocks = []
            for dz in range(3):
                source = (outer.at[0], middle.at[0], middle.at[1], outer.at[1])[z + dz]
                for kx in range(4):
                    first = kx // 2 + 8 * part
                    blocks.append(source[kx % 2, first : first + 8].reshape(256, 128))
            patch = jnp.concatenate(blocks, axis=1)
            deep = jnp.dot(patch, wd[...], preferred_element_type=F32)
            deep = jnp.maximum(deep + biasd[...], 0.0)
            high = deep.astype(BF)
            deeps[z, part, :, 0:256] = high
            deeps[z, part, :, 256:512] = (deep - high.astype(F32)).astype(BF)
            deeps[z, part, :, 512:768] = high
    pair = lax.shift_right_logical(floor_lane((1, 8, 128), 2) & 63, 1)
    for z in range(2):
        spots = [jnp.zeros((4, 8, 128), F32)] * 3
        for part in range(4):
            logits = jnp.dot(deeps[z, part], wh[...], preferred_element_type=F32)
            for step in range(8):
                m = 8 * part + step
                slab = logits[32 * step : 32 * step + 32]
                for i in range(3):
                    shift = (2 * m - 2 * i) % 128
                    turned = pltpu.roll(slab, shift, 1) if shift else slab
                    spots[i] = jnp.where(pair == m, turned.reshape(4, 8, 128), spots[i])
        for i in range(3):
            value = spots[i].reshape(32, 128)
            for half in range(2):
                yp, k = divmod(2 * i + half, 3)
                if half == 1:
                    value = pltpu.roll(value, 64, 1)
                out[k, z, pl.ds(yp, 32, stride=2), :] = jax.nn.sigmoid(value[:, 0:64] + bh[k])


def main(spot, chip_side, core_side, middle, *weights):
    return pl.pallas_call(
        main_kernel,
        out_shape=jax.ShapeDtypeStruct((3, 2, 64, 64), F32),
        in_specs=[pl.BlockSpec(memory_space=SMEM)]
        + [pl.BlockSpec(memory_space=VMEM)] * 6
        + [pl.BlockSpec(memory_space=SMEM)],
        out_specs=pl.BlockSpec(memory_space=VMEM),
        scratch_shapes=[pltpu.VMEM((2, 2, 33, 32, 128), BF), pltpu.VMEM((2, 4, 256, 768), BF)],
        compiler_params=pltpu.CompilerParams(vmem_limit_bytes=24 * 1024 * 1024),
        name="convs",
    )(spot, chip_side, core_side, middle, *weights)


def prepare_kernel(*refs):
    small, t1, t2, ts = refs[:4]
    w1, bias1, w2, bias2, ws, biass = refs[4:]
    b1, b2, bs = (small[:, 32 * i : 32 * i + 32] for i in range(3))
    row = floor_lane((128, 384), 0)
    group = floor_lane((128, 384), 1) // 32
    dy = row // 16 - group % 6
    dx = row % 16 - group // 6
    base = jnp.zeros((128, 384), F32)
    for a in range(3):
        for b in range(3):
            spread = jnp.concatenate([t1[a, b : b + 1, :].astype(F32)] * 12, axis=1)
            base = jnp.where((dy == a) & (dx == b), spread, base)
    for q in range(7):
        turned = pltpu.roll(base, 2 * q, 0) if q else base
        w1[:, 384 * q : 384 * (q + 1)] = turned.astype(BF)
    lone = jnp.concatenate([b1] * 12, axis=1)
    row = floor_lane((32, 384), 0)
    group = floor_lane((32, 384), 1) // 32 % 6
    outside = ((row == 0) & (group == 0)) | ((row == 31) & (group == 5))
    bias1[...] = jnp.where(outside, OFF, lone)
    bias2[...] = jnp.concatenate([b2] * 8, axis=1)
    biass[...] = jnp.concatenate([bs] * 4, axis=1)

    lane = floor_lane((32, 128), 1)
    none = jnp.zeros((32, 128), F32)
    tiled = [
        [jnp.concatenate([t2[a, b].astype(F32).T] * 4, axis=1) for b in range(3)] for a in range(3)
    ]
    for kx in range(4):
        for xp in range(2):
            b = kx - xp
            for j in range(6):
                made = none
                if 0 <= b < 3:
                    for a in range(3):
                        if 0 <= j - a < 4:
                            made = jnp.where(lane // 32 == j - a, tiled[a][b], made)
                start = 32 * (6 * kx + j)
                w2[start : start + 32, 128 * xp : 128 * xp + 128] = made.astype(BF)

    tiled = [
        [jnp.concatenate([ts[a, b].astype(F32)] * 4, axis=1) for b in range(2)] for a in range(2)
    ]
    for xp in range(2):
        for yp in range(4):
            mine = (lane // 32) % 2 == (1 if yp < 2 else 0)
            start = 32 * (4 * xp + yp)
            ws[start : start + 32, :] = jnp.where(mine, tiled[yp % 2][xp], 0.0).astype(BF)


def prepare_deep_kernel(small, td, wd, biasd, wh):
    lane = floor_lane((32, 128), 1)
    none = jnp.zeros((32, 128), F32)
    biasd[...] = jnp.concatenate([small[3:4, :]] * 4, axis=1)
    for dz in range(3):
        tiled = [
            [jnp.concatenate([td[dz, a, b].astype(F32)] * 2, axis=1) for b in range(3)]
            for a in range(3)
        ]
        for kx in range(4):
            for xp in range(2):
                b = kx - xp
                for slot in range(4):
                    made = none
                    if 0 <= b < 3:
                        low = tiled[slot][b] if slot < 3 else none
                        high = tiled[slot - 1][b] if slot > 0 else none
                        made = jnp.where(lane < 64, low, high)
                    start = 128 * (4 * dz + kx) + 32 * slot
                    wd[start : start + 32, 128 * xp : 128 * xp + 128] = made.astype(BF)

    lane = floor_lane((64, 128), 1)
    heads = jnp.concatenate([small[0:3, :], jnp.zeros((5, 64), F32)], axis=0).T
    for xp in range(2):
        for yp in range(2):
            made = jnp.zeros((64, 128), F32)
            for k in range(3):
                c = 3 * yp + k
                made = jnp.where(lane == 64 * (c % 2) + 2 * (c // 2) + xp, heads[:, k : k + 1], made)
            high = made.astype(BF)
            low = (made - high.astype(F32)).astype(BF)
            start = 64 * (2 * xp + yp)
            wh[start : start + 64, :] = high
            wh[256 + start : 256 + start + 64, :] = high
            wh[512 + start : 512 + start + 64, :] = low


def prepare_deep(small, td):
    shape = jax.ShapeDtypeStruct
    return pl.pallas_call(
        prepare_deep_kernel,
        out_shape=(shape((1536, 256), BF), shape((1, 256), F32), shape((768, 128), BF)),
        in_specs=[pl.BlockSpec(memory_space=VMEM)] * 2,
        out_specs=[pl.BlockSpec(memory_space=VMEM)] * 3,
        compiler_params=pltpu.CompilerParams(vmem_limit_bytes=8 * 1024 * 1024),
        cost_estimate=pl.CostEstimate(flops=1000000, bytes_accessed=4000000, transcendentals=0),
        name="prepare_deep",
    )(small, td)


def prepare(small, w_first, w_second, ts):
    shape = jax.ShapeDtypeStruct
    return pl.pallas_call(
        prepare_kernel,
        out_shape=(
            shape((128, 2688), BF),
            shape((32, 384), F32),
            shape((768, 256), BF),
            shape((1, 256), F32),
            shape((256, 128), BF),
            shape((1, 128), F32),
        ),
        in_specs=[pl.BlockSpec(memory_space=VMEM)] * 4,
        out_specs=[pl.BlockSpec(memory_space=VMEM)] * 6,
        compiler_params=pltpu.CompilerParams(vmem_limit_bytes=16 * 1024 * 1024),
        cost_estimate=pl.CostEstimate(flops=1000000, bytes_accessed=4000000, transcendentals=0),
        name="prepare",
    )(
        small,
        jnp.transpose(w_first[:, 0], (1, 2, 0)),
        jnp.transpose(w_second, (2, 3, 0, 1)),
        ts,
    )


def local(
    raw_sections,
    shift_cols,
    shift_rows,
    w_first,
    b_first,
    w_second,
    b_second,
    w_stride,
    b_stride,
    w_depth,
    b_depth,
    w_head,
    b_head,
):
    place = jnp.stack([lax.axis_index("tile"), lax.axis_index("sec")])
    spot = jnp.concatenate([shift_cols, shift_rows, place.astype(jnp.int32)])
    small = jnp.concatenate([w_head, b_depth[None]], axis=0)
    deep = prepare_deep(small, jnp.transpose(w_depth, (2, 3, 4, 1, 0)))
    mine, ts, deep = lax.optimization_barrier(
        (stage(raw_sections), jnp.transpose(w_stride, (2, 3, 1, 0)), deep)
    )
    columns = [
        lax.ppermute(raw_sections, "tile", [(i, i ^ (4 * k)) for i in range(TILES)])
        for k in (1, 2, 3)
    ]
    keep, *sends = pick(spot, mine, *columns)
    sends, firsts, seconds = lax.optimization_barrier((sends, w_first, w_second))
    biases = jnp.concatenate([b_first, b_second, b_stride])[None]
    weights = prepare(biases, firsts, seconds, ts)
    pieces = [
        lax.ppermute(send, "tile", [(i, i ^ k) for i in range(TILES)])
        for k, send in zip((1, 2, 3), sends)
    ]
    both, to_chip = align(spot, keep, *pieces)
    window = lax.ppermute(
        to_chip, "sec", [(i, ((i + 1) ^ 1) - 1) for i in range(1, SECS - 1)]
    )
    middle, to_core = own(spot, both, *weights)
    core_side = lax.ppermute(to_core, "sec", [(i, i ^ 1) for i in range(SECS)])
    chip_side = beyond(spot, window, *weights)
    return main(spot, chip_side, core_side, middle, *deep, b_head)


def solution(mesh):
    in_specs = (P("sec", None, "tile"), P("sec"), P("sec")) + (P(),) * 10
    out_specs = P(None, "sec", None, "tile")
    return jax.shard_map(local, mesh=mesh, in_specs=in_specs, out_specs=out_specs, check_vma=False)
```

time: 43.2 us -> 38.6 us (0.89)
  starting transfers between devices: 19.4 us -> 16.6 us
  local copies, waits for them, and re-layouts: 6.89 us -> 4.26 us
  Pallas kernels: 15.6 us -> 13.6 us
  waiting for transfers between devices: 0.02 us -> 1.49 us
  other arithmetic: 0.76 us -> 2.22 us
    pallas_call x1, Pallas kernels: 8.58 us -> 4.23 us  [main(): pl.pallas_call(main_kernel, out_shape=jax.ShapeDtypeStruct((3, 2, 64, 64)...]
    ppermute x8, starting transfers between devices: 19.4 us -> 16.6 us  [the longest x1 8.61 us: local(): lax.ppermute(to_chip, 'sec', [(i, (i + 1 ^ 1) - 1) for i in range(1, SECS...]
    pallas_call x2 -> x5, Pallas kernels: 5.66 us -> 8.18 us  [the longest x1 4.42 us: own(): pl.pallas_call(own_kernel, out_shape=[features(2), features(1)], in_specs...]
    pad x3 -> x0, local copies, waits for them, and re-layouts: 1.98 us -> none  [prepare(): jnp.pad(v, ((0, 0), (0, 64 - v.shape[1])))]
    ppermute x8, waiting for transfers between devices: 0.02 us -> 1.49 us  [the longest x3 1.2 us: local(): lax.ppermute(send, 'tile', [(i, i ^ k) for i in range(TILES)])]
    broadcast_in_dim x0 -> x1, other arithmetic: none -> 0.76 us  [local(): biases = jnp.concatenate([b_first, b_second, b_stride])[None]]
    unnamed x9 -> x11, local copies, waits for them, and re-layouts: 3.51 us -> 4.26 us
    concatenate x1 -> x0, local copies, waits for them, and re-layouts: 0.71 us -> none  [prepare(): jnp.concatenate([jnp.pad(v, ((0, 0), (0, 64 - v.shape[1]))) for v in line...]
  transfers between devices with their start and end apart: 8 -> 8, of which waited for: 0 -> 2; matrix products, arithmetic and copies ran while one was open for 12% -> 8% of each run, Pallas kernels for 13% -> 21%
where the time goes in v3:
time: 38.6 us; the launch traced here: 38.3 us
  starting transfers between devices  16.6 us (43%)
  Pallas kernels  13.6 us (35%)
  local copies, waits for them, and re-layouts  4.26 us (11%)
  other arithmetic  2.22 us (6%)
  waiting for transfers between devices  1.49 us (4%)
    ppermute x1, starting transfers between devices, local(): lax.ppermute(to_chip, 'sec', [(i, (i + 1 ^ 1) - 1) for i in range(1, SECS...  8.61 us
    pallas_call x1, Pallas kernels, own(): pl.pallas_call(own_kernel, out_shape=[features(2), features(1)], in_specs...  4.42 us
    unnamed x11, local copies, waits for them, and re-layouts  4.26 us
    pallas_call x1, Pallas kernels, main(): pl.pallas_call(main_kernel, out_shape=jax.ShapeDtypeStruct((3, 2, 64, 64)...  4.23 us
    ppermute x3, starting transfers between devices, local(): lax.ppermute(send, 'tile', [(i, i ^ k) for i in range(TILES)])  3.94 us
    ppermute x3, starting transfers between devices, local(): lax.ppermute(raw_sections, 'tile', [(i, i ^ 4 * k) for i in range(TILES)])  3.92 us
    pallas_call x1, Pallas kernels, beyond(): pl.pallas_call(beyond_kernel, out_shape=features(1), in_specs=[pl.BlockSp...  2.74 us
    ppermute x3, waiting for transfers between devices, local(): lax.ppermute(send, 'tile', [(i, i ^ k) for i in range(TILES)])  1.2 us
  transfers between devices with their start and end apart: 8, of which 2 were waited for; matrix products, arithmetic and copies ran while one was open for 8% of the time, Pallas kernels for 21%

profile of v3, /device:TPU:97, one launch (start us, length us, event | category | flops | bytes accessed | tf_op | source)
XLA Modules:
  0.0 38.3 jit_solution(13894126815622920741)
XLA Ops:
  0.0 1.3 %collective-permute-start = (bf16[2,128,128]{2,1,0:T(8,128)(2,1)}, bf16[2,128,128]{2,1,0:T(8,128)(2,1)S(1)}, u32[]{:S(2)}, u32[]{:S(2)}) collective-permute-start(bf16[2,128,128]{2,1,0:T(8,128)(2,1)} %given.1), channel_id=1, source_target_pairs={{0,4},{1,5},{2,6},{3,7},{4,0},{5,1},{6,2},{7,3},{8,12},{9,13},{10,... | collective-permute-start | bytes 196616 | tf_op jit(solution)/shard_map/ppermute | solution.py:462
  1.3 2.6 %collective-permute-start.1 = (bf16[2,128,128]{2,1,0:T(8,128)(2,1)}, bf16[2,128,128]{2,1,0:T(8,128)(2,1)S(1)}, u32[]{:S(2)}, u32[]{:S(2)}) collective-permute-start(bf16[2,128,128]{2,1,0:T(8,128)(2,1)} %given.1), channel_id=1, source_target_pairs={{0,8},{1,9},{2,10},{3,11},{4,12},{5,13},{6,14},{7,15},{8,0},{9,1},... | collective-permute-start | bytes 196616 | tf_op jit(solution)/shard_map/ppermute | solution.py:462
  3.9 0.0 collective-permute-start.2
  3.9 0.0 copy-start.2
  3.9 0.9 %copy-done.2 = bf16[2,128,128]{2,1,0:T(8,128)(2,1)S(1)} copy-done((bf16[2,128,128]{2,1,0:T(8,128)(2,1)S(1)}, bf16[2,128,128]{2,1,0:T(8,128)(2,1)}, u32[]{:S(2)}) %copy-start.2) | copy-done | bytes 65560
  4.8 0.8 %copy.14 = bf16[32,32,2,2]{0,1,3,2:T(8,128)(2,1)S(1)} copy(bf16[32,32,2,2]{1,3,2,0:T(2,128)(2,1)} %param.20) | data formatting | bytes 16384 | tf_op args[7]
  5.7 0.7 %pad_maximum_fusion.small = f32[4,64]{1,0:T(4,128)S(1)} fusion(f32[1,64]{1,0:T(1,128)} %bitcast.15, f32[3,64]{1,0:T(4,128)} %param.24), kind=kLoop, calls=%fused_computation | loop fusion | flops 256 | bytes 2048 | tf_op jit(solution)/shard_map/concatenate | solution.py:456
  6.4 0.0 copy-start
  6.4 0.9 %copy-done = bf16[64,32,3,3,3]{0,1,4,3,2:T(8,128)(2,1)S(1)} copy-done((bf16[64,32,3,3,3]{0,1,4,3,2:T(8,128)(2,1)S(1)}, bf16[64,32,3,3,3]{0,1,4,3,2:T(8,128)(2,1)}, u32[]{:S(2)}) %copy-start) | copy-done | bytes 110616
  7.3 0.2 prepare_deep.1
  7.5 0.8 %pad_add_fusion.spot = s32[6]{0:T(128)S(1)} fusion(s32[1]{0:T(128)} %bitcast.1, s32[1]{0:T(128)} %bitcast, s32[2]{0:T(128)} %param.15, s32[2]{0:T(128)} %param.14), kind=kLoop, calls=%fused_computation.1 | loop fusion | flops 18 | bytes 48 | tf_op jit(solution)/shard_map/concatenate | solution.py:455
  8.3 0.0 collective-permute-done.one
  8.3 0.0 collective-permute-done.1.two
  8.3 0.3 collective-permute-done.2.three
  8.6 0.6 %pick.1 = (bf16[2,128,128]{2,1,0:T(8,128)(2,1)S(1)}, bf16[2,128,128]{2,1,0:T(8,128)(2,1)S(1)}, bf16[2,128,128]{2,1,0:T(8,128)(2,1)S(1)}, bf16[2,128,128]{2,1,0:T(8,128)(2,1)S(1)}) custom-call(s32[6]{0:T(128)S(1)} %pad_add_fusion.spot, bf16[2,128,128]{2,1,0:T(8,128)(2,1)S(1)} %stage.1.mine, bf16[2,128,128]{2,1,0:T(8,128)(2,1)S(1)} %collective-permute-done.one, ...), custom_call_target="tpu_custom_call" | custom-call | bytes 16000000 | tf_op jit(solution)/shard_map/pick/pallas_call | solution.py:70
  9.2 1.3 %collective-permute-start.3 = (bf16[2,128,128]{2,1,0:T(8,128)(2,1)S(1)}, bf16[2,128,128]{2,1,0:T(8,128)(2,1)S(1)}, u32[]{:S(2)}, u32[]{:S(2)}) collective-permute-start(bf16[2,128,128]{2,1,0:T(8,128)(2,1)S(1)} %get-tuple-element.40), channel_id=1, source_target_pairs={{0,1},{1,0},{2,3},{3,2},{4,5},{5,4},{6,7},{7,6},{8,9},{9,8},{10,11... | collective-permute-start | bytes 196616 | tf_op jit(solution)/shard_map/ppermute | solution.py:470
  10.5 2.5 %collective-permute-start.4 = (bf16[2,128,128]{2,1,0:T(8,128)(2,1)S(1)}, bf16[2,128,128]{2,1,0:T(8,128)(2,1)S(1)}, u32[]{:S(2)}, u32[]{:S(2)}) collective-permute-start(bf16[2,128,128]{2,1,0:T(8,128)(2,1)S(1)} %get-tuple-element.41), channel_id=1, source_target_pairs={{0,2},{1,3},{2,0},{3,1},{4,6},{5,7},{6,4},{7,5},{8,10},{9,11},{10,... | collective-permute-start | bytes 196616 | tf_op jit(solution)/shard_map/ppermute | solution.py:470
  13.0 0.2 collective-permute-start.5
  13.2 0.8 %maximum_bitcast_fusion.refs_0_ = f32[1,96]{1,0:T(1,128)S(1)} fusion(f32[32]{0:T(128)} %param.21, f32[32]{0:T(128)} %param.19, f32[32]{0:T(128)} %param.17), kind=kLoop, calls=%fused_computation.2 | loop fusion | flops 192 | bytes 768 | tf_op jit(solution)/shard_map/broadcast_in_dim | solution.py:467
  13.9 0.0 copy-start.1
  13.9 0.9 %copy-done.1 = bf16[32,32,3,3]{1,0,3,2:T(8,128)(2,1)S(1)} copy-done((bf16[32,32,3,3]{1,0,3,2:T(8,128)(2,1)S(1)}, bf16[32,32,3,3]{1,0,3,2:T(8,128)(2,1)}, u32[]{:S(2)}) %copy-start.1) | copy-done | bytes 18456
  14.8 0.0 copy-start.3
  14.8 0.7 %copy-done.3 = bf16[32,1,3,3]{0,3,2,1:T(4,128)(2,1)S(1)} copy-done((bf16[32,1,3,3]{0,3,2,1:T(4,128)(2,1)S(1)}, bf16[32,1,3,3]{0,3,2,1:T(4,128)(2,1)}, u32[]{:S(2)}) %copy-start.3) | copy-done | bytes 600
  15.5 0.6 %prepare.1 = (bf16[128,2688]{1,0:T(8,128)(2,1)S(1)}, f32[32,384]{1,0:T(8,128)S(1)}, bf16[768,256]{1,0:T(8,128)(2,1)S(1)}, f32[1,256]{1,0:T(1,128)S(1)}, bf16[256...) custom-call(f32[1,96]{1,0:T(1,128)S(1)} %maximum_bitcast_fusion.refs_0_, bf16[3,3,32]{2,1,0:T(4,128)(2,1)S(1)} %bitcast.14, ...), custom_call_target="tpu_custom_call" | custom-call | flops 1000000 | bytes 4000000 | tf_op jit(solution)/shard_map/prepare/pallas_call | solution.py:416
  16.1 0.0 collective-permute-done.3.one
  16.1 0.0 collective-permute-done.4.two
  16.1 1.2 %collective-permute-done.5.three = bf16[2,128,128]{2,1,0:T(8,128)(2,1)S(1)} collective-permute-done((bf16[2,128,128]{2,1,0:T(8,128)(2,1)S(1)}, bf16[2,128,128]{2,1,0:T(8,128)(2,1)S(1)}, u32[]{:S(2)}, u32[]{:S(2)}) %collective-permute-start.5) | collective-permute-done | bytes 65568 | tf_op jit(solution)/shard_map/ppermute | solution.py:470
  17.3 0.8 %align.1 = (bf16[2,128,256]{2,1,0:T(8,128)(2,1)S(1)}, bf16[1,128,256]{2,1,0:T(8,128)(2,1)S(1)}) custom-call(s32[6]{0:T(128)S(1)} %pad_add_fusion.spot, bf16[2,128,128]{2,1,0:T(8,128)(2,1)S(1)} %get-tuple-element.36.keep, bf16[2,128,128]{2,1,0:T(8,128)(2,1)S(1)} %collective-permute-done.3.one, bf16[2,128,128]{2,1,0:T(8,128)(2,1)S(1)} %collective-permute-done.4.two, ...), custom_call_target="tpu_custom_call" | custom-call | bytes 4000000 | tf_op jit(solution)/shard_map/align/pallas_call | solution.py:111
  18.1 8.6 %collective-permute-start.6 = (bf16[1,128,256]{2,1,0:T(8,128)(2,1)S(1)}, bf16[1,128,256]{2,1,0:T(8,128)(2,1)S(1)}, u32[]{:S(2)}, u32[]{:S(2)}) collective-permute-start(bf16[1,128,256]{2,1,0:T(8,128)(2,1)S(1)} %get-tuple-element.43), channel_id=1, source_target_pairs={{16,32},{32,16},{48,64},{64,48},{80,96},{96,80},{112,128},{128,112... | collective-permute-start | bytes 196616 | tf_op jit(solution)/shard_map/ppermute | solution.py:474
  26.7 4.4 %own.1 = (bf16[2,2,33,32,128]{4,3,2,1,0:T(8,128)(2,1)S(1)}, bf16[1,2,33,32,128]{4,3,2,1,0:T(8,128)(2,1)S(1)}) custom-call(s32[6]{0:T(128)S(1)} %pad_add_fusion.spot, bf16[2,128,256]{2,1,0:T(8,128)(2,1)S(1)} %get-tuple-element.53.both, bf16[128,2688]{1,0:T(8,128)(2,1)S(1)} %get-tuple-element.47.w1, f32[32,384]{1,0:T(8,128)S(1)} %get-tuple-element.48.bias1, ...), custom_call_target="tpu_custom_call" | custom-call | flops 40000000000 | bytes 4000000 | tf_op jit(solution)/shard_map/own/pallas_call | solution.py:221
  31.2 0.0 copy-start.4
  31.2 0.1 collective-permute-start.7
  31.3 0.0 collective-permute-done.6.window
  31.3 2.7 %beyond.1.chip_side = bf16[1,2,33,32,128]{4,3,2,1,0:T(8,128)(2,1)S(1)} custom-call(s32[6]{0:T(128)S(1)} %pad_add_fusion.spot, bf16[1,128,256]{2,1,0:T(8,128)(2,1)S(1)} %collective-permute-done.6.window, bf16[128,2688]{1,0:T(8,128)(2,1)S(1)} %get-tuple-element.47.w1, f32[32,384]{1,0:T(8,128)S(1)} %get-tuple-element.48.bias1, ...), custom_call_target="tpu_custom_call" | custom-call | flops 20000000000 | bytes 4000000 | tf_op jit(solution)/shard_map/beyond/pallas_call | solution.py:247
  34.0 0.0 collective-permute-done.7.core_side
  34.0 0.0 copy-done.4
  34.0 4.2 %convs.1 = f32[3,2,64,64]{3,2,1,0:T(8,128)} custom-call(s32[6]{0:T(128)S(1)} %pad_add_fusion.spot, bf16[1,2,33,32,128]{4,3,2,1,0:T(8,128)(2,1)S(1)} %beyond.1.chip_side, bf16[1,2,33,32,128]{4,3,2,1,0:T(8,128)(2,1)S(1)} %collective-permute-done.7.core_side, bf16[2,2,33,32,128]{4,3,2,1,0:T(8,128)(2,1)S(1)} %get-tuple-element.55.middle, ...), custom_call_target="tpu_custom_call" | custom-call | tf_op jit(solution)/shard_map/convs/pallas_call | solution.py:300
  (1 shorter events, 0.0 us)
Async XLA Ops:
  0.0 8.3 %collective-permute-start = (bf16[2,128,128]{2,1,0:T(8,128)(2,1)}, bf16[2,128,128]{2,1,0:T(8,128)(2,1)S(1)}, u32[]{:S(2)}, u32[]{:S(2)}) collective-permute-start(bf16[2,128,128]{2,1,0:T(8,128)(2,1)} %given.1), channel_id=1, source_target_pairs={{0,4},{1,5},{2,6},{3,7},{4,0},{5,1},{6,2},{7,3},{8,12},{9,13},{10,... | collective-permute-start | bytes 196616 | tf_op jit(solution)/shard_map/ppermute | solution.py:462
  1.3 7.0 %collective-permute-start.1 = (bf16[2,128,128]{2,1,0:T(8,128)(2,1)}, bf16[2,128,128]{2,1,0:T(8,128)(2,1)S(1)}, u32[]{:S(2)}, u32[]{:S(2)}) collective-permute-start(bf16[2,128,128]{2,1,0:T(8,128)(2,1)} %given.1), channel_id=1, source_target_pairs={{0,8},{1,9},{2,10},{3,11},{4,12},{5,13},{6,14},{7,15},{8,0},{9,1},... | collective-permute-start | bytes 196616 | tf_op jit(solution)/shard_map/ppermute | solution.py:462
  3.9 4.7 %collective-permute-start.2 = (bf16[2,128,128]{2,1,0:T(8,128)(2,1)}, bf16[2,128,128]{2,1,0:T(8,128)(2,1)S(1)}, u32[]{:S(2)}, u32[]{:S(2)}) collective-permute-start(bf16[2,128,128]{2,1,0:T(8,128)(2,1)} %given.1), channel_id=1, source_target_pairs={{0,12},{1,13},{2,14},{3,15},{4,8},{5,9},{6,10},{7,11},{8,4},{9,5},... | collective-permute-start | bytes 196616 | tf_op jit(solution)/shard_map/ppermute | solution.py:462
  3.9 0.9 %copy-start.2 = (bf16[2,128,128]{2,1,0:T(8,128)(2,1)S(1)}, bf16[2,128,128]{2,1,0:T(8,128)(2,1)}, u32[]{:S(2)}) copy-start(bf16[2,128,128]{2,1,0:T(8,128)(2,1)} %given.1) | copy-start | bytes 196612
  6.4 0.9 %copy-start = (bf16[64,32,3,3,3]{0,1,4,3,2:T(8,128)(2,1)S(1)}, bf16[64,32,3,3,3]{0,1,4,3,2:T(8,128)(2,1)}, u32[]{:S(2)}) copy-start(bf16[64,32,3,3,3]{0,1,4,3,2:T(8,128)(2,1)} %param.22) | copy-start | bytes 331780
  9.2 6.9 %collective-permute-start.3 = (bf16[2,128,128]{2,1,0:T(8,128)(2,1)S(1)}, bf16[2,128,128]{2,1,0:T(8,128)(2,1)S(1)}, u32[]{:S(2)}, u32[]{:S(2)}) collective-permute-start(bf16[2,128,128]{2,1,0:T(8,128)(2,1)S(1)} %get-tuple-element.40), channel_id=1, source_target_pairs={{0,1},{1,0},{2,3},{3,2},{4,5},{5,4},{6,7},{7,6},{8,9},{9,8},{10,11... | collective-permute-start | bytes 196616 | tf_op jit(solution)/shard_map/ppermute | solution.py:470
  10.5 5.6 %collective-permute-start.4 = (bf16[2,128,128]{2,1,0:T(8,128)(2,1)S(1)}, bf16[2,128,128]{2,1,0:T(8,128)(2,1)S(1)}, u32[]{:S(2)}, u32[]{:S(2)}) collective-permute-start(bf16[2,128,128]{2,1,0:T(8,128)(2,1)S(1)} %get-tuple-element.41), channel_id=1, source_target_pairs={{0,2},{1,3},{2,0},{3,1},{4,6},{5,7},{6,4},{7,5},{8,10},{9,11},{10,... | collective-permute-start | bytes 196616 | tf_op jit(solution)/shard_map/ppermute | solution.py:470
  13.0 4.3 %collective-permute-start.5 = (bf16[2,128,128]{2,1,0:T(8,128)(2,1)S(1)}, bf16[2,128,128]{2,1,0:T(8,128)(2,1)S(1)}, u32[]{:S(2)}, u32[]{:S(2)}) collective-permute-start(bf16[2,128,128]{2,1,0:T(8,128)(2,1)S(1)} %get-tuple-element.42), channel_id=1, source_target_pairs={{0,3},{1,2},{2,1},{3,0},{4,7},{5,6},{6,5},{7,4},{8,11},{9,10},{10,... | collective-permute-start | bytes 196616 | tf_op jit(solution)/shard_map/ppermute | solution.py:470
  13.9 0.9 %copy-start.1 = (bf16[32,32,3,3]{1,0,3,2:T(8,128)(2,1)S(1)}, bf16[32,32,3,3]{1,0,3,2:T(8,128)(2,1)}, u32[]{:S(2)}) copy-start(bf16[32,32,3,3]{1,0,3,2:T(8,128)(2,1)} %param.18) | copy-start | bytes 55300
  14.8 0.7 %copy-start.3 = (bf16[32,1,3,3]{0,3,2,1:T(4,128)(2,1)S(1)}, bf16[32,1,3,3]{0,3,2,1:T(4,128)(2,1)}, u32[]{:S(2)}) copy-start(bf16[32,1,3,3]{0,3,2,1:T(4,128)(2,1)} %param.16) | copy-start | bytes 1732
  18.1 13.2 %collective-permute-start.6 = (bf16[1,128,256]{2,1,0:T(8,128)(2,1)S(1)}, bf16[1,128,256]{2,1,0:T(8,128)(2,1)S(1)}, u32[]{:S(2)}, u32[]{:S(2)}) collective-permute-start(bf16[1,128,256]{2,1,0:T(8,128)(2,1)S(1)} %get-tuple-element.43), channel_id=1, source_target_pairs={{16,32},{32,16},{48,64},{64,48},{80,96},{96,80},{112,128},{128,112... | collective-permute-start | bytes 196616 | tf_op jit(solution)/shard_map/ppermute | solution.py:474
  31.2 2.9 %copy-start.4 = (f32[3]{0:T(128)S(1)}, f32[3]{0:T(128)}, u32[]{:S(2)}) copy-start(f32[3]{0:T(128)} %bh.1) | copy-start | bytes 40
  31.2 2.9 %collective-permute-start.7 = (bf16[1,2,33,32,128]{4,3,2,1,0:T(8,128)(2,1)S(1)}, bf16[1,2,33,32,128]{4,3,2,1,0:T(8,128)(2,1)S(1)}, u32[]{:S(2)}, u32[]{:S(2)}) collective-permute-start(bf16[1,2,33,32,128]{4,3,2,1,0:T(8,128)(2,1)S(1)} %get-tuple-element.54), channel_id=1, source_target_pairs={{0,16},{16,0},{32,48},{48,32},{64,80},{80,64},{96,112},{112,96},{1... | collective-permute-start | bytes 1622024 | tf_op jit(solution)/shard_map/ppermute | solution.py:478

commit v4 on v3

--- a/solution.py
+++ b/solution.py
@@ -78,7 +78,10 @@
     )(spot, *sources)
 
 
-def align_kernel(spot, keep, one, two, three, both, to_chip, lifted):
+def align_kernel(
+    spot, keep, one, two, three, w1, bias1, w2, bias2, ws, biass, both, to_chip, ahead,
+    lifted, left, right, feats, second,
+):
     sources = (keep, one, two, three)
     tile = spot[TILE]
     lifted[0:32, :] = jnp.zeros((32, 256), F32)
@@ -106,15 +109,21 @@
         def _():
             to_chip[0] = window
 
+    @pl.when(odd == 1)
+    def _():
+        front(
+            tile, (both[0],), w1, bias1, w2, bias2, ws, biass, left, right, feats, second, ahead
+        )
+
 
 def align(spot, *sources):
     return pl.pallas_call(
         align_kernel,
-        out_shape=[jax.ShapeDtypeStruct((n, 128, 256), BF) for n in (2, 1)],
-        in_specs=[pl.BlockSpec(memory_space=SMEM)] + [pl.BlockSpec(memory_space=VMEM)] * 4,
-        out_specs=[pl.BlockSpec(memory_space=VMEM)] * 2,
-        scratch_shapes=[pltpu.VMEM((192, 256), F32)],
-        compiler_params=pltpu.CompilerParams(vmem_limit_bytes=8 * 1024 * 1024),
+        out_shape=[jax.ShapeDtypeStruct((n, 128, 256), BF) for n in (2, 1)] + [features(1)],
+        in_specs=[pl.BlockSpec(memory_space=SMEM)] + [pl.BlockSpec(memory_space=VMEM)] * 10,
+        out_specs=[pl.BlockSpec(memory_space=VMEM)] * 3,
+        scratch_shapes=[pltpu.VMEM((192, 256), F32)] + scratch(1),
+        compiler_params=pltpu.CompilerParams(vmem_limit_bytes=24 * 1024 * 1024),
         cost_estimate=pl.CostEstimate(flops=0, bytes_accessed=4000000, transcendentals=0),
         name="align",
     )(spot, *sources)
@@ -187,21 +196,25 @@
 
 
 def own_kernel(
-    spot, both, w1, bias1, w2, bias2, ws, biass, out, to_core, left, right, feats, second
+    spot, both, ahead, w1, bias1, w2, bias2, ws, biass, out, to_core, left, right, feats, second
 ):
-    windows = (both[0], both[1])
-    front(
-        spot[TILE], windows, w1, bias1, w2, bias2, ws, biass, left, right, feats, second, out
-    )
+    tile = spot[TILE]
     odd = spot[SEC] & 1
 
     @pl.when(odd == 0)
     def _():
+        windows = (both[0], both[1])
+        front(tile, windows, w1, bias1, w2, bias2, ws, biass, left, right, feats, second, out)
         to_core[0] = out[1]
 
     @pl.when(odd == 1)
     def _():
-        to_core[0] = out[0]
+        front(
+            tile, (both[1],), w1, bias1, w2, bias2, ws, biass,
+            left.at[0:1], right.at[0:1], feats.at[0 : SG * 32], second.at[:, 0 : SG * 32], out.at[1:2],
+        )
+        out[0] = ahead[0]
+        to_core[0] = ahead[0]
 
 
 def scratch(count):
@@ -217,17 +230,17 @@
     return jax.ShapeDtypeStruct((count, 2, 33, 32, 128), BF)
 
 
-def own(spot, both, *weights):
+def own(spot, both, ahead, *weights):
     return pl.pallas_call(
         own_kernel,
         out_shape=[features(2), features(1)],
-        in_specs=[pl.BlockSpec(memory_space=SMEM)] + [pl.BlockSpec(memory_space=VMEM)] * 7,
+        in_specs=[pl.BlockSpec(memory_space=SMEM)] + [pl.BlockSpec(memory_space=VMEM)] * 8,
         out_specs=[pl.BlockSpec(memory_space=VMEM)] * 2,
         scratch_shapes=scratch(2),
         compiler_params=pltpu.CompilerParams(vmem_limit_bytes=24 * 1024 * 1024),
         cost_estimate=pl.CostEstimate(flops=40000000000, bytes_accessed=4000000, transcendentals=0),
         name="own",
-    )(spot, both, *weights)
+    )(spot, both, ahead, *weights)
 
 
 def beyond_kernel(
@@ -470,11 +483,11 @@
         lax.ppermute(send, "tile", [(i, i ^ k) for i in range(TILES)])
         for k, send in zip((1, 2, 3), sends)
     ]
-    both, to_chip = align(spot, keep, *pieces)
+    both, to_chip, ahead = align(spot, keep, *pieces, *weights)
     window = lax.ppermute(
         to_chip, "sec", [(i, ((i + 1) ^ 1) - 1) for i in range(1, SECS - 1)]
     )
-    middle, to_core = own(spot, both, *weights)
+    middle, to_core = own(spot, both, ahead, *weights)
     core_side = lax.ppermute(to_core, "sec", [(i, i ^ 1) for i in range(SECS)])
     chip_side = beyond(spot, window, *weights)
     return main(spot, chip_side, core_side, middle, *deep, b_head)

time: 38.6 us -> 36.8 us (0.953)
  starting transfers between devices: 16.6 us -> 14.7 us
    pallas_call x1, Pallas kernels: 0.82 us -> 2.84 us  [align(): pl.pallas_call(align_kernel, out_shape=[jax.ShapeDtypeStruct((n, 128, 256...]
    ppermute x1, starting transfers between devices: 8.61 us -> 6.59 us  [local(): lax.ppermute(to_chip, 'sec', [(i, (i + 1 ^ 1) - 1) for i in range(1, SECS...]
    pallas_call x1, Pallas kernels: 4.42 us -> 2.6 us  [own(): pl.pallas_call(own_kernel, out_shape=[features(2), features(1)], in_specs...]
  transfers between devices with their start and end apart: 8 -> 8, of which waited for: 2 -> 2; matrix products, arithmetic and copies ran while one was open for 8% -> 8% of each run, Pallas kernels for 21% -> 16%
where the time goes in v4:
time: 36.8 us; the launch traced here: 36.5 us
  starting transfers between devices  14.7 us (40%)
  Pallas kernels  13.7 us (37%)
  local copies, waits for them, and re-layouts  4.26 us (12%)
  other arithmetic  2.22 us (6%)
  waiting for transfers between devices  1.49 us (4%)
    ppermute x1, starting transfers between devices, local(): lax.ppermute(to_chip, 'sec', [(i, (i + 1 ^ 1) - 1) for i in range(1, SECS...  6.59 us
    unnamed x11, local copies, waits for them, and re-layouts  4.26 us
    pallas_call x1, Pallas kernels, main(): pl.pallas_call(main_kernel, out_shape=jax.ShapeDtypeStruct((3, 2, 64, 64)...  4.25 us
    ppermute x3, starting transfers between devices, local(): lax.ppermute(send, 'tile', [(i, i ^ k) for i in range(TILES)])  3.94 us
    ppermute x3, starting transfers between devices, local(): lax.ppermute(raw_sections, 'tile', [(i, i ^ 4 * k) for i in range(TILES)])  3.92 us
    pallas_call x1, Pallas kernels, align(): pl.pallas_call(align_kernel, out_shape=[jax.ShapeDtypeStruct((n, 128, 256...  2.84 us
    pallas_call x1, Pallas kernels, own(): pl.pallas_call(own_kernel, out_shape=[features(2), features(1)], in_specs...  2.6 us
    pallas_call x1, Pallas kernels, beyond(): pl.pallas_call(beyond_kernel, out_shape=features(1), in_specs=[pl.BlockSp...  2.56 us
  transfers between devices with their start and end apart: 8, of which 2 were waited for; matrix products, arithmetic and copies ran while one was open for 8% of the time, Pallas kernels for 16%

profile of v4, /device:TPU:97, one launch (start us, length us, event | category | flops | bytes accessed | tf_op | source)
XLA Modules:
  0.0 36.5 jit_solution(10765728418879234147)
XLA Ops:
  0.0 1.3 %collective-permute-start = (bf16[2,128,128]{2,1,0:T(8,128)(2,1)}, bf16[2,128,128]{2,1,0:T(8,128)(2,1)S(1)}, u32[]{:S(2)}, u32[]{:S(2)}) collective-permute-start(bf16[2,128,128]{2,1,0:T(8,128)(2,1)} %given.1), channel_id=1, source_target_pairs={{0,4},{1,5},{2,6},{3,7},{4,0},{5,1},{6,2},{7,3},{8,12},{9,13},{10,... | collective-permute-start | bytes 196616 | tf_op jit(solution)/shard_map/ppermute | solution.py:475
  1.3 2.6 %collective-permute-start.1 = (bf16[2,128,128]{2,1,0:T(8,128)(2,1)}, bf16[2,128,128]{2,1,0:T(8,128)(2,1)S(1)}, u32[]{:S(2)}, u32[]{:S(2)}) collective-permute-start(bf16[2,128,128]{2,1,0:T(8,128)(2,1)} %given.1), channel_id=1, source_target_pairs={{0,8},{1,9},{2,10},{3,11},{4,12},{5,13},{6,14},{7,15},{8,0},{9,1},... | collective-permute-start | bytes 196616 | tf_op jit(solution)/shard_map/ppermute | solution.py:475
  3.9 0.0 collective-permute-start.2
  3.9 0.0 copy-start.2
  3.9 0.9 %copy-done.2 = bf16[2,128,128]{2,1,0:T(8,128)(2,1)S(1)} copy-done((bf16[2,128,128]{2,1,0:T(8,128)(2,1)S(1)}, bf16[2,128,128]{2,1,0:T(8,128)(2,1)}, u32[]{:S(2)}) %copy-start.2) | copy-done | bytes 65560
  4.8 0.8 %copy.14 = bf16[32,32,2,2]{0,1,3,2:T(8,128)(2,1)S(1)} copy(bf16[32,32,2,2]{1,3,2,0:T(2,128)(2,1)} %param.20) | data formatting | bytes 16384 | tf_op args[7]
  5.7 0.7 %pad_maximum_fusion.small = f32[4,64]{1,0:T(4,128)S(1)} fusion(f32[1,64]{1,0:T(1,128)} %bitcast.15, f32[3,64]{1,0:T(4,128)} %param.24), kind=kLoop, calls=%fused_computation | loop fusion | flops 256 | bytes 2048 | tf_op jit(solution)/shard_map/concatenate | solution.py:469
  6.4 0.0 copy-start
  6.4 0.9 %copy-done = bf16[64,32,3,3,3]{0,1,4,3,2:T(8,128)(2,1)S(1)} copy-done((bf16[64,32,3,3,3]{0,1,4,3,2:T(8,128)(2,1)S(1)}, bf16[64,32,3,3,3]{0,1,4,3,2:T(8,128)(2,1)}, u32[]{:S(2)}) %copy-start) | copy-done | bytes 110616
  7.3 0.2 prepare_deep.1
  7.5 0.8 %pad_add_fusion.spot = s32[6]{0:T(128)S(1)} fusion(s32[1]{0:T(128)} %bitcast.1, s32[1]{0:T(128)} %bitcast, s32[2]{0:T(128)} %param.15, s32[2]{0:T(128)} %param.14), kind=kLoop, calls=%fused_computation.1 | loop fusion | flops 18 | bytes 48 | tf_op jit(solution)/shard_map/concatenate | solution.py:468
  8.3 0.0 collective-permute-done.one
  8.3 0.0 collective-permute-done.1.two
  8.3 0.3 collective-permute-done.2.three
  8.6 0.6 %pick.1 = (bf16[2,128,128]{2,1,0:T(8,128)(2,1)S(1)}, bf16[2,128,128]{2,1,0:T(8,128)(2,1)S(1)}, bf16[2,128,128]{2,1,0:T(8,128)(2,1)S(1)}, bf16[2,128,128]{2,1,0:T(8,128)(2,1)S(1)}) custom-call(s32[6]{0:T(128)S(1)} %pad_add_fusion.spot, bf16[2,128,128]{2,1,0:T(8,128)(2,1)S(1)} %stage.1.mine, bf16[2,128,128]{2,1,0:T(8,128)(2,1)S(1)} %collective-permute-done.one, ...), custom_call_target="tpu_custom_call" | custom-call | bytes 16000000 | tf_op jit(solution)/shard_map/pick/pallas_call | solution.py:70
  9.2 1.3 %collective-permute-start.3 = (bf16[2,128,128]{2,1,0:T(8,128)(2,1)S(1)}, bf16[2,128,128]{2,1,0:T(8,128)(2,1)S(1)}, u32[]{:S(2)}, u32[]{:S(2)}) collective-permute-start(bf16[2,128,128]{2,1,0:T(8,128)(2,1)S(1)} %get-tuple-element.41), channel_id=1, source_target_pairs={{0,1},{1,0},{2,3},{3,2},{4,5},{5,4},{6,7},{7,6},{8,9},{9,8},{10,11... | collective-permute-start | bytes 196616 | tf_op jit(solution)/shard_map/ppermute | solution.py:483
  10.5 2.5 %collective-permute-start.4 = (bf16[2,128,128]{2,1,0:T(8,128)(2,1)S(1)}, bf16[2,128,128]{2,1,0:T(8,128)(2,1)S(1)}, u32[]{:S(2)}, u32[]{:S(2)}) collective-permute-start(bf16[2,128,128]{2,1,0:T(8,128)(2,1)S(1)} %get-tuple-element.42), channel_id=1, source_target_pairs={{0,2},{1,3},{2,0},{3,1},{4,6},{5,7},{6,4},{7,5},{8,10},{9,11},{10,... | collective-permute-start | bytes 196616 | tf_op jit(solution)/shard_map/ppermute | solution.py:483
  13.0 0.2 collective-permute-start.5
  13.2 0.8 %maximum_bitcast_fusion.refs_0_ = f32[1,96]{1,0:T(1,128)S(1)} fusion(f32[32]{0:T(128)} %param.21, f32[32]{0:T(128)} %param.19, f32[32]{0:T(128)} %param.17), kind=kLoop, calls=%fused_computation.2 | loop fusion | flops 192 | bytes 768 | tf_op jit(solution)/shard_map/broadcast_in_dim | solution.py:480
  13.9 0.0 copy-start.1
  13.9 0.9 %copy-done.1 = bf16[32,32,3,3]{1,0,3,2:T(8,128)(2,1)S(1)} copy-done((bf16[32,32,3,3]{1,0,3,2:T(8,128)(2,1)S(1)}, bf16[32,32,3,3]{1,0,3,2:T(8,128)(2,1)}, u32[]{:S(2)}) %copy-start.1) | copy-done | bytes 18456
  14.8 0.0 copy-start.3
  14.8 0.7 %copy-done.3 = bf16[32,1,3,3]{0,3,2,1:T(4,128)(2,1)S(1)} copy-done((bf16[32,1,3,3]{0,3,2,1:T(4,128)(2,1)S(1)}, bf16[32,1,3,3]{0,3,2,1:T(4,128)(2,1)}, u32[]{:S(2)}) %copy-start.3) | copy-done | bytes 600
  15.5 0.6 %prepare.1 = (bf16[128,2688]{1,0:T(8,128)(2,1)S(1)}, f32[32,384]{1,0:T(8,128)S(1)}, bf16[768,256]{1,0:T(8,128)(2,1)S(1)}, f32[1,256]{1,0:T(1,128)S(1)}, bf16[256...) custom-call(f32[1,96]{1,0:T(1,128)S(1)} %maximum_bitcast_fusion.refs_0_, bf16[3,3,32]{2,1,0:T(4,128)(2,1)S(1)} %bitcast.14, ...), custom_call_target="tpu_custom_call" | custom-call | flops 1000000 | bytes 4000000 | tf_op jit(solution)/shard_map/prepare/pallas_call | solution.py:429
  16.1 0.0 collective-permute-done.3.one
  16.1 0.0 collective-permute-done.4.two
  16.1 1.2 %collective-permute-done.5.three = bf16[2,128,128]{2,1,0:T(8,128)(2,1)S(1)} collective-permute-done((bf16[2,128,128]{2,1,0:T(8,128)(2,1)S(1)}, bf16[2,128,128]{2,1,0:T(8,128)(2,1)S(1)}, u32[]{:S(2)}, u32[]{:S(2)}) %collective-permute-start.5) | collective-permute-done | bytes 65568 | tf_op jit(solution)/shard_map/ppermute | solution.py:483
  17.3 2.8 %align.1 = (bf16[2,128,256]{2,1,0:T(8,128)(2,1)S(1)}, bf16[1,128,256]{2,1,0:T(8,128)(2,1)S(1)}, bf16[1,2,33,32,128]{4,3,2,1,0:T(8,128)(2,1)S(1)}) custom-call(s32[6]{0:T(128)S(1)} %pad_add_fusion.spot, bf16[2,128,128]{2,1,0:T(8,128)(2,1)S(1)} %get-tuple-element.37.keep, bf16[2,128,128]{2,1,0:T(8,128)(2,1)S(1)} %collective-permute-done.3.one, ...), custom_call_target="tpu_custom_call" | custom-call | bytes 4000000 | tf_op jit(solution)/shard_map/align/pallas_call | solution.py:120
  20.1 6.6 %collective-permute-start.6 = (bf16[1,128,256]{2,1,0:T(8,128)(2,1)S(1)}, bf16[1,128,256]{2,1,0:T(8,128)(2,1)S(1)}, u32[]{:S(2)}, u32[]{:S(2)}) collective-permute-start(bf16[1,128,256]{2,1,0:T(8,128)(2,1)S(1)} %get-tuple-element.53), channel_id=1, source_target_pairs={{16,32},{32,16},{48,64},{64,48},{80,96},{96,80},{112,128},{128,112... | collective-permute-start | bytes 196616 | tf_op jit(solution)/shard_map/ppermute | solution.py:487
  26.7 2.6 %own.1 = (bf16[2,2,33,32,128]{4,3,2,1,0:T(8,128)(2,1)S(1)}, bf16[1,2,33,32,128]{4,3,2,1,0:T(8,128)(2,1)S(1)}) custom-call(s32[6]{0:T(128)S(1)} %pad_add_fusion.spot, bf16[2,128,256]{2,1,0:T(8,128)(2,1)S(1)} %get-tuple-element.54.both, bf16[1,2,33,32,128]{4,3,2,1,0:T(8,128)(2,1)S(1)} %get-tuple-element.55.ahead, bf16[128,2688]{1,0:T(8,128)(2,1)S(1)} %get-tuple-element.47.w1, ...), custom_call_target="tpu_custom_call" | custom-call | flops 40000000000 | bytes 4000000 | tf_op jit(solution)/shard_map/own/pallas_call | solution.py:234
  29.3 0.0 copy-start.4
  29.4 0.3 collective-permute-start.7
  29.6 0.0 collective-permute-done.6.window
  29.6 2.6 %beyond.1.chip_side = bf16[1,2,33,32,128]{4,3,2,1,0:T(8,128)(2,1)S(1)} custom-call(s32[6]{0:T(128)S(1)} %pad_add_fusion.spot, bf16[1,128,256]{2,1,0:T(8,128)(2,1)S(1)} %collective-permute-done.6.window, bf16[128,2688]{1,0:T(8,128)(2,1)S(1)} %get-tuple-element.47.w1, f32[32,384]{1,0:T(8,128)S(1)} %get-tuple-element.48.bias1, ...), custom_call_target="tpu_custom_call" | custom-call | flops 20000000000 | bytes 4000000 | tf_op jit(solution)/shard_map/beyond/pallas_call | solution.py:260
  32.2 0.0 collective-permute-done.7.core_side
  32.2 0.0 copy-done.4
  32.2 4.2 %convs.1 = f32[3,2,64,64]{3,2,1,0:T(8,128)} custom-call(s32[6]{0:T(128)S(1)} %pad_add_fusion.spot, bf16[1,2,33,32,128]{4,3,2,1,0:T(8,128)(2,1)S(1)} %beyond.1.chip_side, bf16[1,2,33,32,128]{4,3,2,1,0:T(8,128)(2,1)S(1)} %collective-permute-done.7.core_side, bf16[2,2,33,32,128]{4,3,2,1,0:T(8,128)(2,1)S(1)} %get-tuple-element.57.middle, ...), custom_call_target="tpu_custom_call" | custom-call | tf_op jit(solution)/shard_map/convs/pallas_call | solution.py:313
  (1 shorter events, 0.0 us)
Async XLA Ops:
  0.0 8.3 %collective-permute-start = (bf16[2,128,128]{2,1,0:T(8,128)(2,1)}, bf16[2,128,128]{2,1,0:T(8,128)(2,1)S(1)}, u32[]{:S(2)}, u32[]{:S(2)}) collective-permute-start(bf16[2,128,128]{2,1,0:T(8,128)(2,1)} %given.1), channel_id=1, source_target_pairs={{0,4},{1,5},{2,6},{3,7},{4,0},{5,1},{6,2},{7,3},{8,12},{9,13},{10,... | collective-permute-start | bytes 196616 | tf_op jit(solution)/shard_map/ppermute | solution.py:475
  1.3 7.0 %collective-permute-start.1 = (bf16[2,128,128]{2,1,0:T(8,128)(2,1)}, bf16[2,128,128]{2,1,0:T(8,128)(2,1)S(1)}, u32[]{:S(2)}, u32[]{:S(2)}) collective-permute-start(bf16[2,128,128]{2,1,0:T(8,128)(2,1)} %given.1), channel_id=1, source_target_pairs={{0,8},{1,9},{2,10},{3,11},{4,12},{5,13},{6,14},{7,15},{8,0},{9,1},... | collective-permute-start | bytes 196616 | tf_op jit(solution)/shard_map/ppermute | solution.py:475
  3.9 4.7 %collective-permute-start.2 = (bf16[2,128,128]{2,1,0:T(8,128)(2,1)}, bf16[2,128,128]{2,1,0:T(8,128)(2,1)S(1)}, u32[]{:S(2)}, u32[]{:S(2)}) collective-permute-start(bf16[2,128,128]{2,1,0:T(8,128)(2,1)} %given.1), channel_id=1, source_target_pairs={{0,12},{1,13},{2,14},{3,15},{4,8},{5,9},{6,10},{7,11},{8,4},{9,5},... | collective-permute-start | bytes 196616 | tf_op jit(solution)/shard_map/ppermute | solution.py:475
  3.9 0.9 %copy-start.2 = (bf16[2,128,128]{2,1,0:T(8,128)(2,1)S(1)}, bf16[2,128,128]{2,1,0:T(8,128)(2,1)}, u32[]{:S(2)}) copy-start(bf16[2,128,128]{2,1,0:T(8,128)(2,1)} %given.1) | copy-start | bytes 196612
  6.4 0.9 %copy-start = (bf16[64,32,3,3,3]{0,1,4,3,2:T(8,128)(2,1)S(1)}, bf16[64,32,3,3,3]{0,1,4,3,2:T(8,128)(2,1)}, u32[]{:S(2)}) copy-start(bf16[64,32,3,3,3]{0,1,4,3,2:T(8,128)(2,1)} %param.22) | copy-start | bytes 331780
  9.2 6.9 %collective-permute-start.3 = (bf16[2,128,128]{2,1,0:T(8,128)(2,1)S(1)}, bf16[2,128,128]{2,1,0:T(8,128)(2,1)S(1)}, u32[]{:S(2)}, u32[]{:S(2)}) collective-permute-start(bf16[2,128,128]{2,1,0:T(8,128)(2,1)S(1)} %get-tuple-element.41), channel_id=1, source_target_pairs={{0,1},{1,0},{2,3},{3,2},{4,5},{5,4},{6,7},{7,6},{8,9},{9,8},{10,11... | collective-permute-start | bytes 196616 | tf_op jit(solution)/shard_map/ppermute | solution.py:483
  10.5 5.6 %collective-permute-start.4 = (bf16[2,128,128]{2,1,0:T(8,128)(2,1)S(1)}, bf16[2,128,128]{2,1,0:T(8,128)(2,1)S(1)}, u32[]{:S(2)}, u32[]{:S(2)}) collective-permute-start(bf16[2,128,128]{2,1,0:T(8,128)(2,1)S(1)} %get-tuple-element.42), channel_id=1, source_target_pairs={{0,2},{1,3},{2,0},{3,1},{4,6},{5,7},{6,4},{7,5},{8,10},{9,11},{10,... | collective-permute-start | bytes 196616 | tf_op jit(solution)/shard_map/ppermute | solution.py:483
  13.0 4.3 %collective-permute-start.5 = (bf16[2,128,128]{2,1,0:T(8,128)(2,1)S(1)}, bf16[2,128,128]{2,1,0:T(8,128)(2,1)S(1)}, u32[]{:S(2)}, u32[]{:S(2)}) collective-permute-start(bf16[2,128,128]{2,1,0:T(8,128)(2,1)S(1)} %get-tuple-element.43), channel_id=1, source_target_pairs={{0,3},{1,2},{2,1},{3,0},{4,7},{5,6},{6,5},{7,4},{8,11},{9,10},{10,... | collective-permute-start | bytes 196616 | tf_op jit(solution)/shard_map/ppermute | solution.py:483
  13.9 0.9 %copy-start.1 = (bf16[32,32,3,3]{1,0,3,2:T(8,128)(2,1)S(1)}, bf16[32,32,3,3]{1,0,3,2:T(8,128)(2,1)}, u32[]{:S(2)}) copy-start(bf16[32,32,3,3]{1,0,3,2:T(8,128)(2,1)} %param.18) | copy-start | bytes 55300
  14.8 0.7 %copy-start.3 = (bf16[32,1,3,3]{0,3,2,1:T(4,128)(2,1)S(1)}, bf16[32,1,3,3]{0,3,2,1:T(4,128)(2,1)}, u32[]{:S(2)}) copy-start(bf16[32,1,3,3]{0,3,2,1:T(4,128)(2,1)} %param.16) | copy-start | bytes 1732
  20.1 9.5 %collective-permute-start.6 = (bf16[1,128,256]{2,1,0:T(8,128)(2,1)S(1)}, bf16[1,128,256]{2,1,0:T(8,128)(2,1)S(1)}, u32[]{:S(2)}, u32[]{:S(2)}) collective-permute-start(bf16[1,128,256]{2,1,0:T(8,128)(2,1)S(1)} %get-tuple-element.53), channel_id=1, source_target_pairs={{16,32},{32,16},{48,64},{64,48},{80,96},{96,80},{112,128},{128,112... | collective-permute-start | bytes 196616 | tf_op jit(solution)/shard_map/ppermute | solution.py:487
  29.3 2.9 %copy-start.4 = (f32[3]{0:T(128)S(1)}, f32[3]{0:T(128)}, u32[]{:S(2)}) copy-start(f32[3]{0:T(128)} %bh.1) | copy-start | bytes 40
  29.4 2.9 %collective-permute-start.7 = (bf16[1,2,33,32,128]{4,3,2,1,0:T(8,128)(2,1)S(1)}, bf16[1,2,33,32,128]{4,3,2,1,0:T(8,128)(2,1)S(1)}, u32[]{:S(2)}, u32[]{:S(2)}) collective-permute-start(bf16[1,2,33,32,128]{4,3,2,1,0:T(8,128)(2,1)S(1)} %get-tuple-element.56), channel_id=1, source_target_pairs={{0,16},{16,0},{32,48},{48,32},{64,80},{80,64},{96,112},{112,96},{1... | collective-permute-start | bytes 1622024 | tf_op jit(solution)/shard_map/ppermute | solution.py:491

commit v5 on v4

--- a/solution.py
+++ b/solution.py
@@ -285,21 +285,24 @@
             deep = jnp.dot(patch, wd[...], preferred_element_type=F32)
             deep = jnp.maximum(deep + biasd[...], 0.0)
             high = deep.astype(BF)
-            deeps[z, part, :, 0:256] = high
-            deeps[z, part, :, 256:512] = (deep - high.astype(F32)).astype(BF)
-            deeps[z, part, :, 512:768] = high
-    pair = lax.shift_right_logical(floor_lane((1, 8, 128), 2) & 63, 1)
+            low = (deep - high.astype(F32)).astype(BF)
+            for m in range(8):
+                here = slice(32 * m, 32 * m + 32)
+                rows = pl.ds(32 * (8 * z + 2 * part + m // 4), 32)
+                at = 512 * (m % 4)
+                deeps[rows, at : at + 256] = high[here]
+                deeps[rows, at + 256 : at + 512] = low[here]
+    block = lax.shift_right_logical(floor_lane((1, 8, 128), 2) & 63, 3)
     for z in range(2):
+        logits = jnp.dot(deeps[256 * z : 256 * z + 256], wh[...], preferred_element_type=F32)
+        logits = logits + pltpu.roll(logits, 96, 1)
         spots = [jnp.zeros((4, 8, 128), F32)] * 3
-        for part in range(4):
-            logits = jnp.dot(deeps[z, part], wh[...], preferred_element_type=F32)
-            for step in range(8):
-                m = 8 * part + step
-                slab = logits[32 * step : 32 * step + 32]
-                for i in range(3):
-                    shift = (2 * m - 2 * i) % 128
-                    turned = pltpu.roll(slab, shift, 1) if shift else slab
-                    spots[i] = jnp.where(pair == m, turned.reshape(4, 8, 128), spots[i])
+        for part in range(8):
+            slab = logits[32 * part : 32 * part + 32]
+            for i in range(3):
+                shift = 8 * (part - i) % 128
+                turned = pltpu.roll(slab, shift, 1) if shift else slab
+                spots[i] = jnp.where(block == part, turned.reshape(4, 8, 128), spots[i])
         for i in range(3):
             value = spots[i].reshape(32, 128)
             for half in range(2):
@@ -317,7 +320,7 @@
         + [pl.BlockSpec(memory_space=VMEM)] * 6
         + [pl.BlockSpec(memory_space=SMEM)],
         out_specs=pl.BlockSpec(memory_space=VMEM),
-        scratch_shapes=[pltpu.VMEM((2, 2, 33, 32, 128), BF), pltpu.VMEM((2, 4, 256, 768), BF)],
+        scratch_shapes=[pltpu.VMEM((2, 2, 33, 32, 128), BF), pltpu.VMEM((512, 2048), BF)],
         compiler_params=pltpu.CompilerParams(vmem_limit_bytes=24 * 1024 * 1024),
         name="convs",
     )(spot, chip_side, core_side, middle, *weights)
@@ -399,23 +402,29 @@
     heads = jnp.concatenate([small[0:3, :], jnp.zeros((5, 64), F32)], axis=0).T
     for xp in range(2):
         for yp in range(2):
-            made = jnp.zeros((64, 128), F32)
+            highs = jnp.zeros((64, 128), F32)
+            lows = jnp.zeros((64, 128), F32)
             for k in range(3):
                 c = 3 * yp + k
-                made = jnp.where(lane == 64 * (c % 2) + 2 * (c // 2) + xp, heads[:, k : k + 1], made)
-            high = made.astype(BF)
-            low = (made - high.astype(F32)).astype(BF)
-            start = 64 * (2 * xp + yp)
-            wh[start : start + 64, :] = high
-            wh[256 + start : 256 + start + 64, :] = high
-            wh[512 + start : 512 + start + 64, :] = low
+                at = 64 * (c % 2) + 8 * (c // 2) + xp
+                column = heads[:, k : k + 1]
+                high = column.astype(BF).astype(F32)
+                highs = jnp.where(lane == at, high, highs)
+                lows = jnp.where(lane == at + 32, column - high, lows)
+            for m in range(4):
+                start = 512 * m + 64 * (2 * xp + yp)
+                both = highs + lows
+                wh[start : start + 64, :] = (pltpu.roll(both, 2 * m, 1) if m else both).astype(BF)
+                wh[start + 256 : start + 320, :] = (
+                    pltpu.roll(highs, 2 * m, 1) if m else highs
+                ).astype(BF)
 
 
 def prepare_deep(small, td):
     shape = jax.ShapeDtypeStruct
     return pl.pallas_call(
         prepare_deep_kernel,
-        out_shape=(shape((1536, 256), BF), shape((1, 256), F32), shape((768, 128), BF)),
+        out_shape=(shape((1536, 256), BF), shape((1, 256), F32), shape((2048, 128), BF)),
         in_specs=[pl.BlockSpec(memory_space=VMEM)] * 2,
         out_specs=[pl.BlockSpec(memory_space=VMEM)] * 3,
         compiler_params=pltpu.CompilerParams(vmem_limit_bytes=8 * 1024 * 1024),

time: 36.8 us -> 36.5 us (level)
  transfers between devices with their start and end apart: 8 -> 8, of which waited for: 2 -> 2; matrix products, arithmetic and copies ran while one was open for 8% -> 9% of each run, Pallas kernels for 16% -> 17%
where the time goes in v5:
time: 36.5 us; the launch traced here: 36.1 us
  starting transfers between devices  14.7 us (40%)
  Pallas kernels  13.5 us (37%)
  local copies, waits for them, and re-layouts  4.26 us (12%)
  other arithmetic  2.22 us (6%)
  waiting for transfers between devices  1.3 us (4%)
    ppermute x1, starting transfers between devices, local(): lax.ppermute(to_chip, 'sec', [(i, (i + 1 ^ 1) - 1) for i in range(1, SECS...  6.59 us
    unnamed x11, local copies, waits for them, and re-layouts  4.26 us
    ppermute x3, starting transfers between devices, local(): lax.ppermute(send, 'tile', [(i, i ^ k) for i in range(TILES)])  3.94 us
    ppermute x3, starting transfers between devices, local(): lax.ppermute(raw_sections, 'tile', [(i, i ^ 4 * k) for i in range(TILES)])  3.92 us
    pallas_call x1, Pallas kernels, main(): pl.pallas_call(main_kernel, out_shape=jax.ShapeDtypeStruct((3, 2, 64, 64)...  3.88 us
    pallas_call x1, Pallas kernels, align(): pl.pallas_call(align_kernel, out_shape=[jax.ShapeDtypeStruct((n, 128, 256...  2.84 us
    pallas_call x1, Pallas kernels, own(): pl.pallas_call(own_kernel, out_shape=[features(2), features(1)], in_specs...  2.6 us
    pallas_call x1, Pallas kernels, beyond(): pl.pallas_call(beyond_kernel, out_shape=features(1), in_specs=[pl.BlockSp...  2.56 us
  transfers between devices with their start and end apart: 8, of which 2 were waited for; matrix products, arithmetic and copies ran while one was open for 9% of the time, Pallas kernels for 17%

profile of v5, /device:TPU:97, one launch (start us, length us, event | category | flops | bytes accessed | tf_op | source)
XLA Modules:
  0.0 36.1 jit_solution(18029665177270723796)
XLA Ops:
  0.0 1.3 %collective-permute-start = (bf16[2,128,128]{2,1,0:T(8,128)(2,1)}, bf16[2,128,128]{2,1,0:T(8,128)(2,1)S(1)}, u32[]{:S(2)}, u32[]{:S(2)}) collective-permute-start(bf16[2,128,128]{2,1,0:T(8,128)(2,1)} %given.1), channel_id=1, source_target_pairs={{0,4},{1,5},{2,6},{3,7},{4,0},{5,1},{6,2},{7,3},{8,12},{9,13},{10,... | collective-permute-start | bytes 196616 | tf_op jit(solution)/shard_map/ppermute | solution.py:484
  1.3 2.6 %collective-permute-start.1 = (bf16[2,128,128]{2,1,0:T(8,128)(2,1)}, bf16[2,128,128]{2,1,0:T(8,128)(2,1)S(1)}, u32[]{:S(2)}, u32[]{:S(2)}) collective-permute-start(bf16[2,128,128]{2,1,0:T(8,128)(2,1)} %given.1), channel_id=1, source_target_pairs={{0,8},{1,9},{2,10},{3,11},{4,12},{5,13},{6,14},{7,15},{8,0},{9,1},... | collective-permute-start | bytes 196616 | tf_op jit(solution)/shard_map/ppermute | solution.py:484
  3.9 0.0 collective-permute-start.2
  3.9 0.0 copy-start.2
  3.9 0.9 %copy-done.2 = bf16[2,128,128]{2,1,0:T(8,128)(2,1)S(1)} copy-done((bf16[2,128,128]{2,1,0:T(8,128)(2,1)S(1)}, bf16[2,128,128]{2,1,0:T(8,128)(2,1)}, u32[]{:S(2)}) %copy-start.2) | copy-done | bytes 65560
  4.8 0.8 %copy.14 = bf16[32,32,2,2]{0,1,3,2:T(8,128)(2,1)S(1)} copy(bf16[32,32,2,2]{1,3,2,0:T(2,128)(2,1)} %param.20) | data formatting | bytes 16384 | tf_op args[7]
  5.7 0.7 %pad_maximum_fusion.small = f32[4,64]{1,0:T(4,128)S(1)} fusion(f32[1,64]{1,0:T(1,128)} %bitcast.15, f32[3,64]{1,0:T(4,128)} %param.24), kind=kLoop, calls=%fused_computation | loop fusion | flops 256 | bytes 2048 | tf_op jit(solution)/shard_map/concatenate | solution.py:478
  6.4 0.0 copy-start
  6.4 0.9 %copy-done = bf16[64,32,3,3,3]{0,1,4,3,2:T(8,128)(2,1)S(1)} copy-done((bf16[64,32,3,3,3]{0,1,4,3,2:T(8,128)(2,1)S(1)}, bf16[64,32,3,3,3]{0,1,4,3,2:T(8,128)(2,1)}, u32[]{:S(2)}) %copy-start) | copy-done | bytes 110616
  7.3 0.4 %prepare_deep.1 = (bf16[1536,256]{1,0:T(8,128)(2,1)S(1)}, f32[1,256]{1,0:T(1,128)S(1)}, bf16[2048,128]{1,0:T(8,128)(2,1)S(1)}) custom-call(f32[4,64]{1,0:T(4,128)S(1)} %pad_maximum_fusion.small, bf16[3,3,3,32,64]{4,3,2,1,0:T(8,128)(2,1)S(1)} %bitcast.11), custom_call_target="tpu_custom_call" | custom-call | flops 1000000 | bytes 4000000 | tf_op jit(solution)/shard_map/prepare_deep/pallas_call | solution.py:425
  7.7 0.8 %pad_add_fusion.spot = s32[6]{0:T(128)S(1)} fusion(s32[1]{0:T(128)} %bitcast.1, s32[1]{0:T(128)} %bitcast, s32[2]{0:T(128)} %param.15, s32[2]{0:T(128)} %param.14), kind=kLoop, calls=%fused_computation.1 | loop fusion | flops 18 | bytes 48 | tf_op jit(solution)/shard_map/concatenate | solution.py:477
  8.5 0.0 collective-permute-done.one
  8.5 0.0 collective-permute-done.1.two
  8.5 0.1 collective-permute-done.2.three
  8.6 0.6 %pick.1 = (bf16[2,128,128]{2,1,0:T(8,128)(2,1)S(1)}, bf16[2,128,128]{2,1,0:T(8,128)(2,1)S(1)}, bf16[2,128,128]{2,1,0:T(8,128)(2,1)S(1)}, bf16[2,128,128]{2,1,0:T(8,128)(2,1)S(1)}) custom-call(s32[6]{0:T(128)S(1)} %pad_add_fusion.spot, bf16[2,128,128]{2,1,0:T(8,128)(2,1)S(1)} %stage.1.mine, bf16[2,128,128]{2,1,0:T(8,128)(2,1)S(1)} %collective-permute-done.one, ...), custom_call_target="tpu_custom_call" | custom-call | bytes 16000000 | tf_op jit(solution)/shard_map/pick/pallas_call | solution.py:70
  9.2 1.3 %collective-permute-start.3 = (bf16[2,128,128]{2,1,0:T(8,128)(2,1)S(1)}, bf16[2,128,128]{2,1,0:T(8,128)(2,1)S(1)}, u32[]{:S(2)}, u32[]{:S(2)}) collective-permute-start(bf16[2,128,128]{2,1,0:T(8,128)(2,1)S(1)} %get-tuple-element.41), channel_id=1, source_target_pairs={{0,1},{1,0},{2,3},{3,2},{4,5},{5,4},{6,7},{7,6},{8,9},{9,8},{10,11... | collective-permute-start | bytes 196616 | tf_op jit(solution)/shard_map/ppermute | solution.py:492
  10.5 2.5 %collective-permute-start.4 = (bf16[2,128,128]{2,1,0:T(8,128)(2,1)S(1)}, bf16[2,128,128]{2,1,0:T(8,128)(2,1)S(1)}, u32[]{:S(2)}, u32[]{:S(2)}) collective-permute-start(bf16[2,128,128]{2,1,0:T(8,128)(2,1)S(1)} %get-tuple-element.42), channel_id=1, source_target_pairs={{0,2},{1,3},{2,0},{3,1},{4,6},{5,7},{6,4},{7,5},{8,10},{9,11},{10,... | collective-permute-start | bytes 196616 | tf_op jit(solution)/shard_map/ppermute | solution.py:492
  13.0 0.2 collective-permute-start.5
  13.2 0.8 %maximum_bitcast_fusion.refs_0_ = f32[1,96]{1,0:T(1,128)S(1)} fusion(f32[32]{0:T(128)} %param.21, f32[32]{0:T(128)} %param.19, f32[32]{0:T(128)} %param.17), kind=kLoop, calls=%fused_computation.2 | loop fusion | flops 192 | bytes 768 | tf_op jit(solution)/shard_map/broadcast_in_dim | solution.py:489
  13.9 0.0 copy-start.1
  13.9 0.9 %copy-done.1 = bf16[32,32,3,3]{1,0,3,2:T(8,128)(2,1)S(1)} copy-done((bf16[32,32,3,3]{1,0,3,2:T(8,128)(2,1)S(1)}, bf16[32,32,3,3]{1,0,3,2:T(8,128)(2,1)}, u32[]{:S(2)}) %copy-start.1) | copy-done | bytes 18456
  14.8 0.0 copy-start.3
  14.8 0.7 %copy-done.3 = bf16[32,1,3,3]{0,3,2,1:T(4,128)(2,1)S(1)} copy-done((bf16[32,1,3,3]{0,3,2,1:T(4,128)(2,1)S(1)}, bf16[32,1,3,3]{0,3,2,1:T(4,128)(2,1)}, u32[]{:S(2)}) %copy-start.3) | copy-done | bytes 600
  15.5 0.6 %prepare.1 = (bf16[128,2688]{1,0:T(8,128)(2,1)S(1)}, f32[32,384]{1,0:T(8,128)S(1)}, bf16[768,256]{1,0:T(8,128)(2,1)S(1)}, f32[1,256]{1,0:T(1,128)S(1)}, bf16[256...) custom-call(f32[1,96]{1,0:T(1,128)S(1)} %maximum_bitcast_fusion.refs_0_, bf16[3,3,32]{2,1,0:T(4,128)(2,1)S(1)} %bitcast.14, ...), custom_call_target="tpu_custom_call" | custom-call | flops 1000000 | bytes 4000000 | tf_op jit(solution)/shard_map/prepare/pallas_call | solution.py:438
  16.1 0.0 collective-permute-done.3.one
  16.1 0.0 collective-permute-done.4.two
  16.1 1.2 %collective-permute-done.5.three = bf16[2,128,128]{2,1,0:T(8,128)(2,1)S(1)} collective-permute-done((bf16[2,128,128]{2,1,0:T(8,128)(2,1)S(1)}, bf16[2,128,128]{2,1,0:T(8,128)(2,1)S(1)}, u32[]{:S(2)}, u32[]{:S(2)}) %collective-permute-start.5) | collective-permute-done | bytes 65568 | tf_op jit(solution)/shard_map/ppermute | solution.py:492
  17.3 2.8 %align.1 = (bf16[2,128,256]{2,1,0:T(8,128)(2,1)S(1)}, bf16[1,128,256]{2,1,0:T(8,128)(2,1)S(1)}, bf16[1,2,33,32,128]{4,3,2,1,0:T(8,128)(2,1)S(1)}) custom-call(s32[6]{0:T(128)S(1)} %pad_add_fusion.spot, bf16[2,128,128]{2,1,0:T(8,128)(2,1)S(1)} %get-tuple-element.37.keep, bf16[2,128,128]{2,1,0:T(8,128)(2,1)S(1)} %collective-permute-done.3.one, ...), custom_call_target="tpu_custom_call" | custom-call | bytes 4000000 | tf_op jit(solution)/shard_map/align/pallas_call | solution.py:120
  20.1 6.6 %collective-permute-start.6 = (bf16[1,128,256]{2,1,0:T(8,128)(2,1)S(1)}, bf16[1,128,256]{2,1,0:T(8,128)(2,1)S(1)}, u32[]{:S(2)}, u32[]{:S(2)}) collective-permute-start(bf16[1,128,256]{2,1,0:T(8,128)(2,1)S(1)} %get-tuple-element.53), channel_id=1, source_target_pairs={{16,32},{32,16},{48,64},{64,48},{80,96},{96,80},{112,128},{128,112... | collective-permute-start | bytes 196616 | tf_op jit(solution)/shard_map/ppermute | solution.py:496
  26.7 2.6 %own.1 = (bf16[2,2,33,32,128]{4,3,2,1,0:T(8,128)(2,1)S(1)}, bf16[1,2,33,32,128]{4,3,2,1,0:T(8,128)(2,1)S(1)}) custom-call(s32[6]{0:T(128)S(1)} %pad_add_fusion.spot, bf16[2,128,256]{2,1,0:T(8,128)(2,1)S(1)} %get-tuple-element.54.both, bf16[1,2,33,32,128]{4,3,2,1,0:T(8,128)(2,1)S(1)} %get-tuple-element.55.ahead, bf16[128,2688]{1,0:T(8,128)(2,1)S(1)} %get-tuple-element.47.w1, ...), custom_call_target="tpu_custom_call" | custom-call | flops 40000000000 | bytes 4000000 | tf_op jit(solution)/shard_map/own/pallas_call | solution.py:234
  29.3 0.0 copy-start.4
  29.4 0.3 collective-permute-start.7
  29.6 0.0 collective-permute-done.6.window
  29.6 2.6 %beyond.1.chip_side = bf16[1,2,33,32,128]{4,3,2,1,0:T(8,128)(2,1)S(1)} custom-call(s32[6]{0:T(128)S(1)} %pad_add_fusion.spot, bf16[1,128,256]{2,1,0:T(8,128)(2,1)S(1)} %collective-permute-done.6.window, bf16[128,2688]{1,0:T(8,128)(2,1)S(1)} %get-tuple-element.47.w1, f32[32,384]{1,0:T(8,128)S(1)} %get-tuple-element.48.bias1, ...), custom_call_target="tpu_custom_call" | custom-call | flops 20000000000 | bytes 4000000 | tf_op jit(solution)/shard_map/beyond/pallas_call | solution.py:260
  32.2 0.0 collective-permute-done.7.core_side
  32.2 0.0 copy-done.4
  32.2 3.9 %convs.1 = f32[3,2,64,64]{3,2,1,0:T(8,128)} custom-call(s32[6]{0:T(128)S(1)} %pad_add_fusion.spot, bf16[1,2,33,32,128]{4,3,2,1,0:T(8,128)(2,1)S(1)} %beyond.1.chip_side, bf16[1,2,33,32,128]{4,3,2,1,0:T(8,128)(2,1)S(1)} %collective-permute-done.7.core_side, bf16[2,2,33,32,128]{4,3,2,1,0:T(8,128)(2,1)S(1)} %get-tuple-element.57.middle, ...), custom_call_target="tpu_custom_call" | custom-call | tf_op jit(solution)/shard_map/convs/pallas_call | solution.py:316
  (1 shorter events, 0.0 us)
Async XLA Ops:
  0.0 8.5 %collective-permute-start = (bf16[2,128,128]{2,1,0:T(8,128)(2,1)}, bf16[2,128,128]{2,1,0:T(8,128)(2,1)S(1)}, u32[]{:S(2)}, u32[]{:S(2)}) collective-permute-start(bf16[2,128,128]{2,1,0:T(8,128)(2,1)} %given.1), channel_id=1, source_target_pairs={{0,4},{1,5},{2,6},{3,7},{4,0},{5,1},{6,2},{7,3},{8,12},{9,13},{10,... | collective-permute-start | bytes 196616 | tf_op jit(solution)/shard_map/ppermute | solution.py:484
  1.3 7.2 %collective-permute-start.1 = (bf16[2,128,128]{2,1,0:T(8,128)(2,1)}, bf16[2,128,128]{2,1,0:T(8,128)(2,1)S(1)}, u32[]{:S(2)}, u32[]{:S(2)}) collective-permute-start(bf16[2,128,128]{2,1,0:T(8,128)(2,1)} %given.1), channel_id=1, source_target_pairs={{0,8},{1,9},{2,10},{3,11},{4,12},{5,13},{6,14},{7,15},{8,0},{9,1},... | collective-permute-start | bytes 196616 | tf_op jit(solution)/shard_map/ppermute | solution.py:484
  3.9 4.7 %collective-permute-start.2 = (bf16[2,128,128]{2,1,0:T(8,128)(2,1)}, bf16[2,128,128]{2,1,0:T(8,128)(2,1)S(1)}, u32[]{:S(2)}, u32[]{:S(2)}) collective-permute-start(bf16[2,128,128]{2,1,0:T(8,128)(2,1)} %given.1), channel_id=1, source_target_pairs={{0,12},{1,13},{2,14},{3,15},{4,8},{5,9},{6,10},{7,11},{8,4},{9,5},... | collective-permute-start | bytes 196616 | tf_op jit(solution)/shard_map/ppermute | solution.py:484
  3.9 0.9 %copy-start.2 = (bf16[2,128,128]{2,1,0:T(8,128)(2,1)S(1)}, bf16[2,128,128]{2,1,0:T(8,128)(2,1)}, u32[]{:S(2)}) copy-start(bf16[2,128,128]{2,1,0:T(8,128)(2,1)} %given.1) | copy-start | bytes 196612
  6.4 0.9 %copy-start = (bf16[64,32,3,3,3]{0,1,4,3,2:T(8,128)(2,1)S(1)}, bf16[64,32,3,3,3]{0,1,4,3,2:T(8,128)(2,1)}, u32[]{:S(2)}) copy-start(bf16[64,32,3,3,3]{0,1,4,3,2:T(8,128)(2,1)} %param.22) | copy-start | bytes 331780
  9.2 6.9 %collective-permute-start.3 = (bf16[2,128,128]{2,1,0:T(8,128)(2,1)S(1)}, bf16[2,128,128]{2,1,0:T(8,128)(2,1)S(1)}, u32[]{:S(2)}, u32[]{:S(2)}) collective-permute-start(bf16[2,128,128]{2,1,0:T(8,128)(2,1)S(1)} %get-tuple-element.41), channel_id=1, source_target_pairs={{0,1},{1,0},{2,3},{3,2},{4,5},{5,4},{6,7},{7,6},{8,9},{9,8},{10,11... | collective-permute-start | bytes 196616 | tf_op jit(solution)/shard_map/ppermute | solution.py:492
  10.5 5.6 %collective-permute-start.4 = (bf16[2,128,128]{2,1,0:T(8,128)(2,1)S(1)}, bf16[2,128,128]{2,1,0:T(8,128)(2,1)S(1)}, u32[]{:S(2)}, u32[]{:S(2)}) collective-permute-start(bf16[2,128,128]{2,1,0:T(8,128)(2,1)S(1)} %get-tuple-element.42), channel_id=1, source_target_pairs={{0,2},{1,3},{2,0},{3,1},{4,6},{5,7},{6,4},{7,5},{8,10},{9,11},{10,... | collective-permute-start | bytes 196616 | tf_op jit(solution)/shard_map/ppermute | solution.py:492
  13.0 4.3 %collective-permute-start.5 = (bf16[2,128,128]{2,1,0:T(8,128)(2,1)S(1)}, bf16[2,128,128]{2,1,0:T(8,128)(2,1)S(1)}, u32[]{:S(2)}, u32[]{:S(2)}) collective-permute-start(bf16[2,128,128]{2,1,0:T(8,128)(2,1)S(1)} %get-tuple-element.43), channel_id=1, source_target_pairs={{0,3},{1,2},{2,1},{3,0},{4,7},{5,6},{6,5},{7,4},{8,11},{9,10},{10,... | collective-permute-start | bytes 196616 | tf_op jit(solution)/shard_map/ppermute | solution.py:492
  13.9 0.9 %copy-start.1 = (bf16[32,32,3,3]{1,0,3,2:T(8,128)(2,1)S(1)}, bf16[32,32,3,3]{1,0,3,2:T(8,128)(2,1)}, u32[]{:S(2)}) copy-start(bf16[32,32,3,3]{1,0,3,2:T(8,128)(2,1)} %param.18) | copy-start | bytes 55300
  14.8 0.7 %copy-start.3 = (bf16[32,1,3,3]{0,3,2,1:T(4,128)(2,1)S(1)}, bf16[32,1,3,3]{0,3,2,1:T(4,128)(2,1)}, u32[]{:S(2)}) copy-start(bf16[32,1,3,3]{0,3,2,1:T(4,128)(2,1)} %param.16) | copy-start | bytes 1732
  20.1 9.5 %collective-permute-start.6 = (bf16[1,128,256]{2,1,0:T(8,128)(2,1)S(1)}, bf16[1,128,256]{2,1,0:T(8,128)(2,1)S(1)}, u32[]{:S(2)}, u32[]{:S(2)}) collective-permute-start(bf16[1,128,256]{2,1,0:T(8,128)(2,1)S(1)} %get-tuple-element.53), channel_id=1, source_target_pairs={{16,32},{32,16},{48,64},{64,48},{80,96},{96,80},{112,128},{128,112... | collective-permute-start | bytes 196616 | tf_op jit(solution)/shard_map/ppermute | solution.py:496
  29.3 2.9 %copy-start.4 = (f32[3]{0:T(128)S(1)}, f32[3]{0:T(128)}, u32[]{:S(2)}) copy-start(f32[3]{0:T(128)} %bh.1) | copy-start | bytes 40
  29.4 2.9 %collective-permute-start.7 = (bf16[1,2,33,32,128]{4,3,2,1,0:T(8,128)(2,1)S(1)}, bf16[1,2,33,32,128]{4,3,2,1,0:T(8,128)(2,1)S(1)}, u32[]{:S(2)}, u32[]{:S(2)}) collective-permute-start(bf16[1,2,33,32,128]{4,3,2,1,0:T(8,128)(2,1)S(1)} %get-tuple-element.56), channel_id=1, source_target_pairs={{0,16},{16,0},{32,48},{48,32},{64,80},{80,64},{96,112},{112,96},{1... | collective-permute-start | bytes 1622024 | tf_op jit(solution)/shard_map/ppermute | solution.py:500

commit v6 on v5

--- a/solution.py
+++ b/solution.py
@@ -53,7 +53,7 @@
     )(raw)
 
 
-def pick_kernel(spot, mine, one, two, three, keep, send_1, send_2, send_3):
+def pick_kernel(spot, mine, two, one, three, keep, send_2, send_1, send_3):
     sources = (mine, one, two, three)
     tile = spot[TILE]
     place = tile & 3
@@ -79,7 +79,7 @@
 
 
 def align_kernel(
-    spot, keep, one, two, three, w1, bias1, w2, bias2, ws, biass, both, to_chip, ahead,
+    spot, keep, two, one, three, w1, bias1, w2, bias2, ws, biass, both, to_chip, ahead,
     lifted, left, right, feats, second,
 ):
     sources = (keep, one, two, three)
@@ -244,8 +244,10 @@
 
 
 def beyond_kernel(
-    spot, window, w1, bias1, w2, bias2, ws, biass, out, left, right, feats, second
+    spot, th, bd, td, window, w1, bias1, w2, bias2, ws, biass, out, wd, biasd, wh,
+    left, right, feats, second,
 ):
+    prepare_deep(th, bd, td, wd, biasd, wh)
     sec = spot[SEC]
     front(
         spot[TILE], (window[0],), w1, bias1, w2, bias2, ws, biass, left, right, feats, second, out
@@ -256,17 +258,18 @@
         out[0] = jnp.zeros((2, 33, 32, 128), BF)
 
 
-def beyond(spot, window, *weights):
+def beyond(spot, th, bd, td, window, *weights):
+    shape = jax.ShapeDtypeStruct
     return pl.pallas_call(
         beyond_kernel,
-        out_shape=features(1),
-        in_specs=[pl.BlockSpec(memory_space=SMEM)] + [pl.BlockSpec(memory_space=VMEM)] * 7,
-        out_specs=pl.BlockSpec(memory_space=VMEM),
+        out_shape=[features(1), shape((1536, 256), BF), shape((1, 256), F32), shape((2048, 128), BF)],
+        in_specs=[pl.BlockSpec(memory_space=SMEM)] + [pl.BlockSpec(memory_space=VMEM)] * 10,
+        out_specs=[pl.BlockSpec(memory_space=VMEM)] * 4,
         scratch_shapes=scratch(1),
         compiler_params=pltpu.CompilerParams(vmem_limit_bytes=24 * 1024 * 1024),
         cost_estimate=pl.CostEstimate(flops=20000000000, bytes_accessed=4000000, transcendentals=0),
         name="beyond",
-    )(spot, window, *weights)
+    )(spot, th, bd, td, window, *weights)
 
 
 def main_kernel(spot, chip_side, core_side, middle, wd, biasd, wh, bh, out, outer, deeps):
@@ -377,10 +380,10 @@
             ws[start : start + 32, :] = jnp.where(mine, tiled[yp % 2][xp], 0.0).astype(BF)
 
 
-def prepare_deep_kernel(small, td, wd, biasd, wh):
+def prepare_deep(th, bd, td, wd, biasd, wh):
     lane = floor_lane((32, 128), 1)
     none = jnp.zeros((32, 128), F32)
-    biasd[...] = jnp.concatenate([small[3:4, :]] * 4, axis=1)
+    biasd[...] = jnp.concatenate([bd[...]] * 4, axis=1)
     for dz in range(3):
         tiled = [
             [jnp.concatenate([td[dz, a, b].astype(F32)] * 2, axis=1) for b in range(3)]
@@ -399,7 +402,7 @@
                     wd[start : start + 32, 128 * xp : 128 * xp + 128] = made.astype(BF)
 
     lane = floor_lane((64, 128), 1)
-    heads = jnp.concatenate([small[0:3, :], jnp.zeros((5, 64), F32)], axis=0).T
+    heads = jnp.concatenate([th[...], jnp.zeros((5, 64), F32)], axis=0).T
     for xp in range(2):
         for yp in range(2):
             highs = jnp.zeros((64, 128), F32)
@@ -418,19 +421,6 @@
                 wh[start + 256 : start + 320, :] = (
                     pltpu.roll(highs, 2 * m, 1) if m else highs
                 ).astype(BF)
-
-
-def prepare_deep(small, td):
-    shape = jax.ShapeDtypeStruct
-    return pl.pallas_call(
-        prepare_deep_kernel,
-        out_shape=(shape((1536, 256), BF), shape((1, 256), F32), shape((2048, 128), BF)),
-        in_specs=[pl.BlockSpec(memory_space=VMEM)] * 2,
-        out_specs=[pl.BlockSpec(memory_space=VMEM)] * 3,
-        compiler_params=pltpu.CompilerParams(vmem_limit_bytes=8 * 1024 * 1024),
-        cost_estimate=pl.CostEstimate(flops=1000000, bytes_accessed=4000000, transcendentals=0),
-        name="prepare_deep",
-    )(small, td)
 
 
 def prepare(small, w_first, w_second, ts):
@@ -475,22 +465,19 @@
 ):
     place = jnp.stack([lax.axis_index("tile"), lax.axis_index("sec")])
     spot = jnp.concatenate([shift_cols, shift_rows, place.astype(jnp.int32)])
-    small = jnp.concatenate([w_head, b_depth[None]], axis=0)
-    deep = prepare_deep(small, jnp.transpose(w_depth, (2, 3, 4, 1, 0)))
-    mine, ts, deep = lax.optimization_barrier(
-        (stage(raw_sections), jnp.transpose(w_stride, (2, 3, 1, 0)), deep)
+    mine, ts = lax.optimization_barrier((stage(raw_sections), jnp.transpose(w_stride, (2, 3, 1, 0))))
+    far, near, around = (
+        lax.ppermute(raw_sections, "tile", [(i, i ^ (4 * k)) for i in range(TILES)])
+        for k in (2, 1, 3)
     )
-    columns = [
-        lax.ppermute(raw_sections, "tile", [(i, i ^ (4 * k)) for i in range(TILES)])
-        for k in (1, 2, 3)
-    ]
+    columns = (far, near, around)
     keep, *sends = pick(spot, mine, *columns)
     sends, firsts, seconds = lax.optimization_barrier((sends, w_first, w_second))
     biases = jnp.concatenate([b_first, b_second, b_stride])[None]
     weights = prepare(biases, firsts, seconds, ts)
     pieces = [
         lax.ppermute(send, "tile", [(i, i ^ k) for i in range(TILES)])
-        for k, send in zip((1, 2, 3), sends)
+        for k, send in zip((2, 1, 3), sends)
     ]
     both, to_chip, ahead = align(spot, keep, *pieces, *weights)
     window = lax.ppermute(
@@ -498,7 +485,8 @@
     )
     middle, to_core = own(spot, both, ahead, *weights)
     core_side = lax.ppermute(to_core, "sec", [(i, i ^ 1) for i in range(SECS)])
-    chip_side = beyond(spot, window, *weights)
+    td = jnp.transpose(w_depth, (2, 3, 4, 1, 0))
+    chip_side, *deep = beyond(spot, w_head, b_depth[None], td, window, *weights)
     return main(spot, chip_side, core_side, middle, *deep, b_head)
 
 

time: 36.5 us -> 34.7 us (0.951)
  waiting for transfers between devices: 1.3 us -> 2.6 us
  starting transfers between devices: 14.7 us -> 13.6 us
  local copies, waits for them, and re-layouts: 4.26 us -> 3.35 us
  other arithmetic: 2.22 us -> 1.52 us
    ppermute x3, waiting for transfers between devices: 0.1 us -> 1.25 us  [local(): lax.ppermute(raw_sections, 'tile', [(i, i ^ 4 * k) for i in range(TILES)])]
    unnamed x11 -> x15, local copies, waits for them, and re-layouts: 4.26 us -> 3.35 us
    concatenate x1 -> x0, other arithmetic: 0.71 us -> none  [local(): small = jnp.concatenate([w_head, b_depth[None]], axis=0)]
    ppermute x1, starting transfers between devices: 6.59 us -> 5.93 us  [local(): lax.ppermute(to_chip, 'sec', [(i, (i + 1 ^ 1) - 1) for i in range(1, SECS...]
    pallas_call x2 -> x1, Pallas kernels: 2.95 us -> 2.67 us  [beyond(): pl.pallas_call(beyond_kernel, out_shape=[features(1), shape((1536, 256),...]
  transfers between devices with their start and end apart: 8 -> 8, of which waited for: 2 -> 2; matrix products, arithmetic and copies ran while one was open for 9% -> 7% of each run, Pallas kernels for 17% -> 17%
where the time goes in v6:
time: 34.7 us; the launch traced here: 34.4 us
  starting transfers between devices  13.6 us (39%)
  Pallas kernels  13.2 us (38%)
  local copies, waits for them, and re-layouts  3.35 us (10%)
  waiting for transfers between devices  2.6 us (7%)
  other arithmetic  1.52 us (4%)
    ppermute x1, starting transfers between devices, local(): lax.ppermute(to_chip, 'sec', [(i, (i + 1 ^ 1) - 1) for i in range(1, SECS...  5.93 us
    pallas_call x1, Pallas kernels, main(): pl.pallas_call(main_kernel, out_shape=jax.ShapeDtypeStruct((3, 2, 64, 64)...  3.9 us
    ppermute x3, starting transfers between devices, local(): lax.ppermute(send, 'tile', [(i, i ^ k) for i in range(TILES)])  3.69 us
    ppermute x3, starting transfers between devices, local(): lax.ppermute(raw_sections, 'tile', [(i, i ^ 4 * k) for i in range(TILES)])  3.69 us
    unnamed x15, local copies, waits for them, and re-layouts  3.35 us
    pallas_call x1, Pallas kernels, align(): pl.pallas_call(align_kernel, out_shape=[jax.ShapeDtypeStruct((n, 128, 256...  2.84 us
    pallas_call x1, Pallas kernels, beyond(): pl.pallas_call(beyond_kernel, out_shape=[features(1), shape((1536, 256),...  2.67 us
    pallas_call x1, Pallas kernels, own(): pl.pallas_call(own_kernel, out_shape=[features(2), features(1)], in_specs...  2.6 us
  transfers between devices with their start and end apart: 8, of which 2 were waited for; matrix products, arithmetic and copies ran while one was open for 7% of the time, Pallas kernels for 17%

profile of v6, /device:TPU:97, one launch (start us, length us, event | category | flops | bytes accessed | tf_op | source)
XLA Modules:
  0.0 34.4 jit_solution(5564908702106307979)
XLA Ops:
  0.0 2.9 %collective-permute-start = (bf16[2,128,128]{2,1,0:T(8,128)(2,1)}, bf16[2,128,128]{2,1,0:T(8,128)(2,1)S(1)}, u32[]{:S(2)}, u32[]{:S(2)}) collective-permute-start(bf16[2,128,128]{2,1,0:T(8,128)(2,1)} %given.1), channel_id=1, source_target_pairs={{0,8},{1,9},{2,10},{3,11},{4,12},{5,13},{6,14},{7,15},{8,0},{9,1},... | collective-permute-start | bytes 196616 | tf_op jit(solution)/shard_map/ppermute | solution.py:470
  2.9 0.8 %collective-permute-start.2 = (bf16[2,128,128]{2,1,0:T(8,128)(2,1)}, bf16[2,128,128]{2,1,0:T(8,128)(2,1)S(1)}, u32[]{:S(2)}, u32[]{:S(2)}) collective-permute-start(bf16[2,128,128]{2,1,0:T(8,128)(2,1)} %given.1), channel_id=1, source_target_pairs={{0,12},{1,13},{2,14},{3,15},{4,8},{5,9},{6,10},{7,11},{8,4},{9,5},... | collective-permute-start | bytes 196616 | tf_op jit(solution)/shard_map/ppermute | solution.py:470
  3.7 0.0 collective-permute-start.1
  3.7 0.0 copy-start.1
  3.7 0.9 %copy-done.1 = bf16[2,128,128]{2,1,0:T(8,128)(2,1)S(1)} copy-done((bf16[2,128,128]{2,1,0:T(8,128)(2,1)S(1)}, bf16[2,128,128]{2,1,0:T(8,128)(2,1)}, u32[]{:S(2)}) %copy-start.1) | copy-done | bytes 65560
  4.6 0.8 %copy.14 = bf16[32,32,2,2]{0,1,3,2:T(8,128)(2,1)S(1)} copy(bf16[32,32,2,2]{1,3,2,0:T(2,128)(2,1)} %param.20) | data formatting | bytes 16384 | tf_op args[7]
  5.5 0.8 %pad_add_fusion.spot = s32[6]{0:T(128)S(1)} fusion(s32[1]{0:T(128)} %bitcast.1, s32[1]{0:T(128)} %bitcast, s32[2]{0:T(128)} %param.15, s32[2]{0:T(128)} %param.14), kind=kLoop, calls=%fused_computation | loop fusion | flops 18 | bytes 48 | tf_op jit(solution)/shard_map/concatenate | solution.py:467
  6.2 0.0 collective-permute-done.two
  6.2 1.2 %collective-permute-done.2.three = bf16[2,128,128]{2,1,0:T(8,128)(2,1)S(1)} collective-permute-done((bf16[2,128,128]{2,1,0:T(8,128)(2,1)}, bf16[2,128,128]{2,1,0:T(8,128)(2,1)S(1)}, u32[]{:S(2)}, u32[]{:S(2)}) %collective-permute-start.2) | collective-permute-done | bytes 65568 | tf_op jit(solution)/shard_map/ppermute | solution.py:470
  7.5 0.0 collective-permute-done.1.one
  7.5 0.6 %pick.1 = (bf16[2,128,128]{2,1,0:T(8,128)(2,1)S(1)}, bf16[2,128,128]{2,1,0:T(8,128)(2,1)S(1)}, bf16[2,128,128]{2,1,0:T(8,128)(2,1)S(1)}, bf16[2,128,128]{2,1,0:T(8,128)(2,1)S(1)}) custom-call(s32[6]{0:T(128)S(1)} %pad_add_fusion.spot, bf16[2,128,128]{2,1,0:T(8,128)(2,1)S(1)} %stage.1.mine, bf16[2,128,128]{2,1,0:T(8,128)(2,1)S(1)} %collective-permute-done.two, ...), custom_call_target="tpu_custom_call" | custom-call | bytes 16000000 | tf_op jit(solution)/shard_map/pick/pallas_call | solution.py:70
  8.1 2.8 %collective-permute-start.3 = (bf16[2,128,128]{2,1,0:T(8,128)(2,1)S(1)}, bf16[2,128,128]{2,1,0:T(8,128)(2,1)S(1)}, u32[]{:S(2)}, u32[]{:S(2)}) collective-permute-start(bf16[2,128,128]{2,1,0:T(8,128)(2,1)S(1)} %get-tuple-element.36), channel_id=1, source_target_pairs={{0,2},{1,3},{2,0},{3,1},{4,6},{5,7},{6,4},{7,5},{8,10},{9,11},{10,... | collective-permute-start | bytes 196616 | tf_op jit(solution)/shard_map/ppermute | solution.py:479
  10.9 0.3 collective-permute-start.4
  11.2 0.6 %collective-permute-start.5 = (bf16[2,128,128]{2,1,0:T(8,128)(2,1)S(1)}, bf16[2,128,128]{2,1,0:T(8,128)(2,1)S(1)}, u32[]{:S(2)}, u32[]{:S(2)}) collective-permute-start(bf16[2,128,128]{2,1,0:T(8,128)(2,1)S(1)} %get-tuple-element.38), channel_id=1, source_target_pairs={{0,3},{1,2},{2,1},{3,0},{4,7},{5,6},{6,5},{7,4},{8,11},{9,10},{10,... | collective-permute-start | bytes 196616 | tf_op jit(solution)/shard_map/ppermute | solution.py:479
  11.8 0.8 %maximum_bitcast_fusion.refs_0_ = f32[1,96]{1,0:T(1,128)S(1)} fusion(f32[32]{0:T(128)} %param.21, f32[32]{0:T(128)} %param.19, f32[32]{0:T(128)} %param.17), kind=kLoop, calls=%fused_computation.1 | loop fusion | flops 192 | bytes 768 | tf_op jit(solution)/shard_map/broadcast_in_dim | solution.py:476
  12.5 0.0 copy-start
  12.5 0.9 %copy-done = bf16[32,32,3,3]{1,0,3,2:T(8,128)(2,1)S(1)} copy-done((bf16[32,32,3,3]{1,0,3,2:T(8,128)(2,1)S(1)}, bf16[32,32,3,3]{1,0,3,2:T(8,128)(2,1)}, u32[]{:S(2)}) %copy-start) | copy-done | bytes 18456
  13.4 0.0 copy-start.2
  13.4 0.7 %copy-done.2 = bf16[32,1,3,3]{0,3,2,1:T(4,128)(2,1)S(1)} copy-done((bf16[32,1,3,3]{0,3,2,1:T(4,128)(2,1)S(1)}, bf16[32,1,3,3]{0,3,2,1:T(4,128)(2,1)}, u32[]{:S(2)}) %copy-start.2) | copy-done | bytes 600
  14.1 0.6 %prepare.1 = (bf16[128,2688]{1,0:T(8,128)(2,1)S(1)}, f32[32,384]{1,0:T(8,128)S(1)}, bf16[768,256]{1,0:T(8,128)(2,1)S(1)}, f32[1,256]{1,0:T(1,128)S(1)}, bf16[256...) custom-call(f32[1,96]{1,0:T(1,128)S(1)} %maximum_bitcast_fusion.refs_0_, bf16[3,3,32]{2,1,0:T(4,128)(2,1)S(1)} %bitcast.13, ...), custom_call_target="tpu_custom_call" | custom-call | flops 1000000 | bytes 4000000 | tf_op jit(solution)/shard_map/prepare/pallas_call | solution.py:428
  14.7 0.0 collective-permute-done.3.two
  14.7 0.0 collective-permute-done.4.one
  14.7 1.3 %collective-permute-done.5.three = bf16[2,128,128]{2,1,0:T(8,128)(2,1)S(1)} collective-permute-done((bf16[2,128,128]{2,1,0:T(8,128)(2,1)S(1)}, bf16[2,128,128]{2,1,0:T(8,128)(2,1)S(1)}, u32[]{:S(2)}, u32[]{:S(2)}) %collective-permute-start.5) | collective-permute-done | bytes 65568 | tf_op jit(solution)/shard_map/ppermute | solution.py:479
  16.1 2.8 %align.1 = (bf16[2,128,256]{2,1,0:T(8,128)(2,1)S(1)}, bf16[1,128,256]{2,1,0:T(8,128)(2,1)S(1)}, bf16[1,2,33,32,128]{4,3,2,1,0:T(8,128)(2,1)S(1)}) custom-call(s32[6]{0:T(128)S(1)} %pad_add_fusion.spot, bf16[2,128,128]{2,1,0:T(8,128)(2,1)S(1)} %get-tuple-element.32.keep, bf16[2,128,128]{2,1,0:T(8,128)(2,1)S(1)} %collective-permute-done.3.two, ...), custom_call_target="tpu_custom_call" | custom-call | bytes 4000000 | tf_op jit(solution)/shard_map/align/pallas_call | solution.py:120
  18.9 5.9 %collective-permute-start.6 = (bf16[1,128,256]{2,1,0:T(8,128)(2,1)S(1)}, bf16[1,128,256]{2,1,0:T(8,128)(2,1)S(1)}, u32[]{:S(2)}, u32[]{:S(2)}) collective-permute-start(bf16[1,128,256]{2,1,0:T(8,128)(2,1)S(1)} %get-tuple-element.48), channel_id=1, source_target_pairs={{16,32},{32,16},{48,64},{64,48},{80,96},{96,80},{112,128},{128,112... | collective-permute-start | bytes 196616 | tf_op jit(solution)/shard_map/ppermute | solution.py:483
  24.9 0.0 copy-start.4
  24.9 0.0 copy-start.5
  24.9 0.0 copy-start.6
  24.9 2.6 %own.1 = (bf16[2,2,33,32,128]{4,3,2,1,0:T(8,128)(2,1)S(1)}, bf16[1,2,33,32,128]{4,3,2,1,0:T(8,128)(2,1)S(1)}) custom-call(s32[6]{0:T(128)S(1)} %pad_add_fusion.spot, bf16[2,128,256]{2,1,0:T(8,128)(2,1)S(1)} %get-tuple-element.50.both, bf16[1,2,33,32,128]{4,3,2,1,0:T(8,128)(2,1)S(1)} %get-tuple-element.51.ahead, bf16[128,2688]{1,0:T(8,128)(2,1)S(1)} %get-tuple-element.42.w1, ...), custom_call_target="tpu_custom_call" | custom-call | flops 40000000000 | bytes 4000000 | tf_op jit(solution)/shard_map/own/pallas_call | solution.py:234
  27.5 0.3 collective-permute-start.7
  27.8 0.0 collective-permute-done.6.window
  27.8 0.0 copy-done.4
  27.8 0.0 copy-done.5
  27.8 0.0 copy-done.6
  27.8 0.0 copy-start.3
  27.8 2.7 %beyond.1 = (bf16[1,2,33,32,128]{4,3,2,1,0:T(8,128)(2,1)S(1)}, bf16[1536,256]{1,0:T(8,128)(2,1)S(1)}, f32[1,256]{1,0:T(1,128)S(1)}, bf16[2048,128]{1,0:T(8,128)(2,1)S(1)}) custom-call(s32[6]{0:T(128)S(1)} %pad_add_fusion.spot, f32[3,64]{1,0:T(4,128)S(1)} %copy-done.5, f32[1,64]{1,0:T(1,128)S(1)} %bitcast.15, bf16[3,3,3,32,64]{4,3,2,1,0:T(8,128)(2,1)S(1)} %bitcast.14, ...), custom_call_target="tpu_custom_call" | custom-call | flops 20000000000 | bytes 4000000 | tf_op jit(solution)/shard_map/beyond/pallas_call | solution.py:263
  30.5 0.0 collective-permute-done.7.core_side
  30.5 0.0 copy-done.3
  30.5 3.9 %convs.1 = f32[3,2,64,64]{3,2,1,0:T(8,128)} custom-call(s32[6]{0:T(128)S(1)} %pad_add_fusion.spot, bf16[1,2,33,32,128]{4,3,2,1,0:T(8,128)(2,1)S(1)} %get-tuple-element.49.chip_side, bf16[1,2,33,32,128]{4,3,2,1,0:T(8,128)(2,1)S(1)} %collective-permute-done.7.core_side, bf16[2,2,33,32,128]{4,3,2,1,0:T(8,128)(2,1)S(1)} %get-tuple-element.53.middle, ...), custom_call_target="tpu_custom_call" | custom-call | tf_op jit(solution)/shard_map/convs/pallas_call | solution.py:319
  (1 shorter events, 0.0 us)
Async XLA Ops:
  0.0 6.2 %collective-permute-start = (bf16[2,128,128]{2,1,0:T(8,128)(2,1)}, bf16[2,128,128]{2,1,0:T(8,128)(2,1)S(1)}, u32[]{:S(2)}, u32[]{:S(2)}) collective-permute-start(bf16[2,128,128]{2,1,0:T(8,128)(2,1)} %given.1), channel_id=1, source_target_pairs={{0,8},{1,9},{2,10},{3,11},{4,12},{5,13},{6,14},{7,15},{8,0},{9,1},... | collective-permute-start | bytes 196616 | tf_op jit(solution)/shard_map/ppermute | solution.py:470
  2.9 4.5 %collective-permute-start.2 = (bf16[2,128,128]{2,1,0:T(8,128)(2,1)}, bf16[2,128,128]{2,1,0:T(8,128)(2,1)S(1)}, u32[]{:S(2)}, u32[]{:S(2)}) collective-permute-start(bf16[2,128,128]{2,1,0:T(8,128)(2,1)} %given.1), channel_id=1, source_target_pairs={{0,12},{1,13},{2,14},{3,15},{4,8},{5,9},{6,10},{7,11},{8,4},{9,5},... | collective-permute-start | bytes 196616 | tf_op jit(solution)/shard_map/ppermute | solution.py:470
  3.7 3.8 %collective-permute-start.1 = (bf16[2,128,128]{2,1,0:T(8,128)(2,1)}, bf16[2,128,128]{2,1,0:T(8,128)(2,1)S(1)}, u32[]{:S(2)}, u32[]{:S(2)}) collective-permute-start(bf16[2,128,128]{2,1,0:T(8,128)(2,1)} %given.1), channel_id=1, source_target_pairs={{0,4},{1,5},{2,6},{3,7},{4,0},{5,1},{6,2},{7,3},{8,12},{9,13},{10,... | collective-permute-start | bytes 196616 | tf_op jit(solution)/shard_map/ppermute | solution.py:470
  3.7 0.9 %copy-start.1 = (bf16[2,128,128]{2,1,0:T(8,128)(2,1)S(1)}, bf16[2,128,128]{2,1,0:T(8,128)(2,1)}, u32[]{:S(2)}) copy-start(bf16[2,128,128]{2,1,0:T(8,128)(2,1)} %given.1) | copy-start | bytes 196612
  8.1 6.6 %collective-permute-start.3 = (bf16[2,128,128]{2,1,0:T(8,128)(2,1)S(1)}, bf16[2,128,128]{2,1,0:T(8,128)(2,1)S(1)}, u32[]{:S(2)}, u32[]{:S(2)}) collective-permute-start(bf16[2,128,128]{2,1,0:T(8,128)(2,1)S(1)} %get-tuple-element.36), channel_id=1, source_target_pairs={{0,2},{1,3},{2,0},{3,1},{4,6},{5,7},{6,4},{7,5},{8,10},{9,11},{10,... | collective-permute-start | bytes 196616 | tf_op jit(solution)/shard_map/ppermute | solution.py:479
  10.9 3.8 %collective-permute-start.4 = (bf16[2,128,128]{2,1,0:T(8,128)(2,1)S(1)}, bf16[2,128,128]{2,1,0:T(8,128)(2,1)S(1)}, u32[]{:S(2)}, u32[]{:S(2)}) collective-permute-start(bf16[2,128,128]{2,1,0:T(8,128)(2,1)S(1)} %get-tuple-element.37), channel_id=1, source_target_pairs={{0,1},{1,0},{2,3},{3,2},{4,5},{5,4},{6,7},{7,6},{8,9},{9,8},{10,11... | collective-permute-start | bytes 196616 | tf_op jit(solution)/shard_map/ppermute | solution.py:479
  11.2 4.8 %collective-permute-start.5 = (bf16[2,128,128]{2,1,0:T(8,128)(2,1)S(1)}, bf16[2,128,128]{2,1,0:T(8,128)(2,1)S(1)}, u32[]{:S(2)}, u32[]{:S(2)}) collective-permute-start(bf16[2,128,128]{2,1,0:T(8,128)(2,1)S(1)} %get-tuple-element.38), channel_id=1, source_target_pairs={{0,3},{1,2},{2,1},{3,0},{4,7},{5,6},{6,5},{7,4},{8,11},{9,10},{10,... | collective-permute-start | bytes 196616 | tf_op jit(solution)/shard_map/ppermute | solution.py:479
  12.5 0.9 %copy-start = (bf16[32,32,3,3]{1,0,3,2:T(8,128)(2,1)S(1)}, bf16[32,32,3,3]{1,0,3,2:T(8,128)(2,1)}, u32[]{:S(2)}) copy-start(bf16[32,32,3,3]{1,0,3,2:T(8,128)(2,1)} %param.18) | copy-start | bytes 55300
  13.4 0.7 %copy-start.2 = (bf16[32,1,3,3]{0,3,2,1:T(4,128)(2,1)S(1)}, bf16[32,1,3,3]{0,3,2,1:T(4,128)(2,1)}, u32[]{:S(2)}) copy-start(bf16[32,1,3,3]{0,3,2,1:T(4,128)(2,1)} %param.16) | copy-start | bytes 1732
  18.9 8.9 %collective-permute-start.6 = (bf16[1,128,256]{2,1,0:T(8,128)(2,1)S(1)}, bf16[1,128,256]{2,1,0:T(8,128)(2,1)S(1)}, u32[]{:S(2)}, u32[]{:S(2)}) collective-permute-start(bf16[1,128,256]{2,1,0:T(8,128)(2,1)S(1)} %get-tuple-element.48), channel_id=1, source_target_pairs={{16,32},{32,16},{48,64},{64,48},{80,96},{96,80},{112,128},{128,112... | collective-permute-start | bytes 196616 | tf_op jit(solution)/shard_map/ppermute | solution.py:483
  24.9 2.9 %copy-start.4 = (bf16[64,32,3,3,3]{0,1,4,3,2:T(8,128)(2,1)S(1)}, bf16[64,32,3,3,3]{0,1,4,3,2:T(8,128)(2,1)}, u32[]{:S(2)}) copy-start(bf16[64,32,3,3,3]{0,1,4,3,2:T(8,128)(2,1)} %param.22) | copy-start | bytes 331780
  24.9 2.9 %copy-start.5 = (f32[3,64]{1,0:T(4,128)S(1)}, f32[3,64]{1,0:T(4,128)}, u32[]{:S(2)}) copy-start(f32[3,64]{1,0:T(4,128)} %th.1) | copy-start | bytes 2308
  24.9 2.9 %copy-start.6 = (f32[64]{0:T(128)S(1)}, f32[64]{0:T(128)}, u32[]{:S(2)}) copy-start(f32[64]{0:T(128)} %param.23) | copy-start | bytes 772
  27.5 3.0 %collective-permute-start.7 = (bf16[1,2,33,32,128]{4,3,2,1,0:T(8,128)(2,1)S(1)}, bf16[1,2,33,32,128]{4,3,2,1,0:T(8,128)(2,1)S(1)}, u32[]{:S(2)}, u32[]{:S(2)}) collective-permute-start(bf16[1,2,33,32,128]{4,3,2,1,0:T(8,128)(2,1)S(1)} %get-tuple-element.52), channel_id=1, source_target_pairs={{0,16},{16,0},{32,48},{48,32},{64,80},{80,64},{96,112},{112,96},{1... | collective-permute-start | bytes 1622024 | tf_op jit(solution)/shard_map/ppermute | solution.py:487
  27.8 2.7 %copy-start.3 = (f32[3]{0:T(128)S(1)}, f32[3]{0:T(128)}, u32[]{:S(2)}) copy-start(f32[3]{0:T(128)} %bh.1) | copy-start | bytes 40

commit v7 on v6

--- a/solution.py
+++ b/solution.py
@@ -112,7 +112,7 @@
     @pl.when(odd == 1)
     def _():
         front(
-            tile, (both[0],), w1, bias1, w2, bias2, ws, biass, left, right, feats, second, ahead
+            tile, (both[0],), w1, bias1, w2, bias2, ws, biass, left, right, feats, second, (ahead,)
         )
 
 
@@ -192,11 +192,11 @@
                 value = jnp.where(low_edge, 0.0, value)
             if p == 5 and g % SG == SG - 1:
                 value = jnp.where(high_edge, 0.0, value)
-            strided[g // SG, p % 2, 3 * (g % SG) + p // 2] = value.astype(BF)
+            strided[g // SG][0, p % 2, 3 * (g % SG) + p // 2] = value.astype(BF)
 
 
 def own_kernel(
-    spot, both, ahead, w1, bias1, w2, bias2, ws, biass, out, to_core, left, right, feats, second
+    spot, both, ahead, w1, bias1, w2, bias2, ws, biass, near, inner, left, right, feats, second
 ):
     tile = spot[TILE]
     odd = spot[SEC] & 1
@@ -204,17 +204,17 @@
     @pl.when(odd == 0)
     def _():
         windows = (both[0], both[1])
-        front(tile, windows, w1, bias1, w2, bias2, ws, biass, left, right, feats, second, out)
-        to_core[0] = out[1]
+        front(
+            tile, windows, w1, bias1, w2, bias2, ws, biass, left, right, feats, second, (near, inner)
+        )
 
     @pl.when(odd == 1)
     def _():
         front(
             tile, (both[1],), w1, bias1, w2, bias2, ws, biass,
-            left.at[0:1], right.at[0:1], feats.at[0 : SG * 32], second.at[:, 0 : SG * 32], out.at[1:2],
+            left.at[0:1], right.at[0:1], feats.at[0 : SG * 32], second.at[:, 0 : SG * 32], (near,),
         )
-        out[0] = ahead[0]
-        to_core[0] = ahead[0]
+        inner[0] = ahead[0]
 
 
 def scratch(count):
@@ -233,7 +233,7 @@
 def own(spot, both, ahead, *weights):
     return pl.pallas_call(
         own_kernel,
-        out_shape=[features(2), features(1)],
+        out_shape=[features(1), features(1)],
         in_specs=[pl.BlockSpec(memory_space=SMEM)] + [pl.BlockSpec(memory_space=VMEM)] * 8,
         out_specs=[pl.BlockSpec(memory_space=VMEM)] * 2,
         scratch_shapes=scratch(2),
@@ -244,13 +244,11 @@
 
 
 def beyond_kernel(
-    spot, th, bd, td, window, w1, bias1, w2, bias2, ws, biass, out, wd, biasd, wh,
-    left, right, feats, second,
+    spot, window, w1, bias1, w2, bias2, ws, biass, out, left, right, feats, second
 ):
-    prepare_deep(th, bd, td, wd, biasd, wh)
     sec = spot[SEC]
     front(
-        spot[TILE], (window[0],), w1, bias1, w2, bias2, ws, biass, left, right, feats, second, out
+        spot[TILE], (window[0],), w1, bias1, w2, bias2, ws, biass, left, right, feats, second, (out,)
     )
 
     @pl.when((sec == 0) | (sec == SECS - 1))
@@ -258,35 +256,35 @@
         out[0] = jnp.zeros((2, 33, 32, 128), BF)
 
 
-def beyond(spot, th, bd, td, window, *weights):
-    shape = jax.ShapeDtypeStruct
+def beyond(spot, window, *weights):
     return pl.pallas_call(
         beyond_kernel,
-        out_shape=[features(1), shape((1536, 256), BF), shape((1, 256), F32), shape((2048, 128), BF)],
-        in_specs=[pl.BlockSpec(memory_space=SMEM)] + [pl.BlockSpec(memory_space=VMEM)] * 10,
-        out_specs=[pl.BlockSpec(memory_space=VMEM)] * 4,
+        out_shape=features(1),
+        in_specs=[pl.BlockSpec(memory_space=SMEM)] + [pl.BlockSpec(memory_space=VMEM)] * 7,
+        out_specs=pl.BlockSpec(memory_space=VMEM),
         scratch_shapes=scratch(1),
         compiler_params=pltpu.CompilerParams(vmem_limit_bytes=24 * 1024 * 1024),
         cost_estimate=pl.CostEstimate(flops=20000000000, bytes_accessed=4000000, transcendentals=0),
         name="beyond",
-    )(spot, th, bd, td, window, *weights)
-
-
-def main_kernel(spot, chip_side, core_side, middle, wd, biasd, wh, bh, out, outer, deeps):
+    )(spot, window, *weights)
+
+
+def main_kernel(spot, beyond, near, inner, mate, wd, biasd, wh, bh, out, deeps):
     odd = spot[SEC] & 1
-    outer[odd] = chip_side[0]
-    outer[1 - odd] = core_side[0]
+    order = (beyond, near, inner, mate)
     for z in range(2):
         for part in range(4):
-            blocks = []
+            deep = biasd[...]
             for dz in range(3):
-                source = (outer.at[0], middle.at[0], middle.at[1], outer.at[1])[z + dz]
+                source = order[z + dz].at[0]
+                blocks = []
                 for kx in range(4):
                     first = kx // 2 + 8 * part
                     blocks.append(source[kx % 2, first : first + 8].reshape(256, 128))
-            patch = jnp.concatenate(blocks, axis=1)
-            deep = jnp.dot(patch, wd[...], preferred_element_type=F32)
-            deep = jnp.maximum(deep + biasd[...], 0.0)
+                patch = jnp.concatenate(blocks, axis=1)
+                layer = pl.multiple_of(512 * jnp.where(odd == 1, 2 - dz, dz), 512)
+                deep += jnp.dot(patch, wd[pl.ds(layer, 512), :], preferred_element_type=F32)
+            deep = jnp.maximum(deep, 0.0)
             high = deep.astype(BF)
             low = (deep - high.astype(F32)).astype(BF)
             for m in range(8):
@@ -306,32 +304,34 @@
                 shift = 8 * (part - i) % 128
                 turned = pltpu.roll(slab, shift, 1) if shift else slab
                 spots[i] = jnp.where(block == part, turned.reshape(4, 8, 128), spots[i])
+        goal = jnp.where(odd == 1, 1 - z, z)
         for i in range(3):
             value = spots[i].reshape(32, 128)
             for half in range(2):
                 yp, k = divmod(2 * i + half, 3)
                 if half == 1:
                     value = pltpu.roll(value, 64, 1)
-                out[k, z, pl.ds(yp, 32, stride=2), :] = jax.nn.sigmoid(value[:, 0:64] + bh[k])
-
-
-def main(spot, chip_side, core_side, middle, *weights):
+                out[k, goal, pl.ds(yp, 32, stride=2), :] = jax.nn.sigmoid(value[:, 0:64] + bh[0:1, 64 + k : 65 + k])
+
+
+def main(spot, beyond, near, inner, mate, *weights):
     return pl.pallas_call(
         main_kernel,
         out_shape=jax.ShapeDtypeStruct((3, 2, 64, 64), F32),
         in_specs=[pl.BlockSpec(memory_space=SMEM)]
-        + [pl.BlockSpec(memory_space=VMEM)] * 6
-        + [pl.BlockSpec(memory_space=SMEM)],
+        + [pl.BlockSpec(memory_space=VMEM)] * 8,
         out_specs=pl.BlockSpec(memory_space=VMEM),
-        scratch_shapes=[pltpu.VMEM((2, 2, 33, 32, 128), BF), pltpu.VMEM((512, 2048), BF)],
+        scratch_shapes=[pltpu.VMEM((512, 2048), BF)],
         compiler_params=pltpu.CompilerParams(vmem_limit_bytes=24 * 1024 * 1024),
         name="convs",
-    )(spot, chip_side, core_side, middle, *weights)
+    )(spot, beyond, near, inner, mate, *weights)
 
 
 def prepare_kernel(*refs):
-    small, t1, t2, ts = refs[:4]
-    w1, bias1, w2, bias2, ws, biass = refs[4:]
+    small, t1, t2, ts, th, td = refs[:6]
+    w1, bias1, w2, bias2, ws, biass, tail, wd, biasd, wh = refs[6:]
+    tail[:, 0:67] = small[:, 96:163]
+    prepare_deep(th, tail, td, wd, biasd, wh)
     b1, b2, bs = (small[:, 32 * i : 32 * i + 32] for i in range(3))
     row = floor_lane((128, 384), 0)
     group = floor_lane((128, 384), 1) // 32
@@ -383,7 +383,7 @@
 def prepare_deep(th, bd, td, wd, biasd, wh):
     lane = floor_lane((32, 128), 1)
     none = jnp.zeros((32, 128), F32)
-    biasd[...] = jnp.concatenate([bd[...]] * 4, axis=1)
+    biasd[...] = jnp.concatenate([bd[:, 0:64]] * 4, axis=1)
     for dz in range(3):
         tiled = [
             [jnp.concatenate([td[dz, a, b].astype(F32)] * 2, axis=1) for b in range(3)]
@@ -423,7 +423,7 @@
                 ).astype(BF)
 
 
-def prepare(small, w_first, w_second, ts):
+def prepare(small, w_first, w_second, ts, w_head, w_depth):
     shape = jax.ShapeDtypeStruct
     return pl.pallas_call(
         prepare_kernel,
@@ -434,9 +434,13 @@
             shape((1, 256), F32),
             shape((256, 128), BF),
             shape((1, 128), F32),
+            shape((1, 128), F32),
+            shape((1536, 256), BF),
+            shape((1, 256), F32),
+            shape((2048, 128), BF),
         ),
-        in_specs=[pl.BlockSpec(memory_space=VMEM)] * 4,
-        out_specs=[pl.BlockSpec(memory_space=VMEM)] * 6,
+        in_specs=[pl.BlockSpec(memory_space=VMEM)] * 6,
+        out_specs=[pl.BlockSpec(memory_space=VMEM)] * 10,
         compiler_params=pltpu.CompilerParams(vmem_limit_bytes=16 * 1024 * 1024),
         cost_estimate=pl.CostEstimate(flops=1000000, bytes_accessed=4000000, transcendentals=0),
         name="prepare",
@@ -445,6 +449,8 @@
         jnp.transpose(w_first[:, 0], (1, 2, 0)),
         jnp.transpose(w_second, (2, 3, 0, 1)),
         ts,
+        w_head,
+        jnp.transpose(w_depth, (2, 3, 4, 1, 0)),
     )
 
 
@@ -472,9 +478,11 @@
     )
     columns = (far, near, around)
     keep, *sends = pick(spot, mine, *columns)
-    sends, firsts, seconds = lax.optimization_barrier((sends, w_first, w_second))
-    biases = jnp.concatenate([b_first, b_second, b_stride])[None]
-    weights = prepare(biases, firsts, seconds, ts)
+    sends, firsts, seconds, heads, depths = lax.optimization_barrier(
+        (sends, w_first, w_second, w_head, w_depth)
+    )
+    biases = jnp.concatenate([b_first, b_second, b_stride, b_depth, b_head])[None]
+    *weights, tail, wd, biasd, wh = prepare(biases, firsts, seconds, ts, heads, depths)
     pieces = [
         lax.ppermute(send, "tile", [(i, i ^ k) for i in range(TILES)])
         for k, send in zip((2, 1, 3), sends)
@@ -483,11 +491,10 @@
     window = lax.ppermute(
         to_chip, "sec", [(i, ((i + 1) ^ 1) - 1) for i in range(1, SECS - 1)]
     )
-    middle, to_core = own(spot, both, ahead, *weights)
-    core_side = lax.ppermute(to_core, "sec", [(i, i ^ 1) for i in range(SECS)])
-    td = jnp.transpose(w_depth, (2, 3, 4, 1, 0))
-    chip_side, *deep = beyond(spot, w_head, b_depth[None], td, window, *weights)
-    return main(spot, chip_side, core_side, middle, *deep, b_head)
+    near, inner = own(spot, both, ahead, *weights)
+    mate = lax.ppermute(inner, "sec", [(i, i ^ 1) for i in range(SECS)])
+    chip_side = beyond(spot, window, *weights)
+    return main(spot, chip_side, near, inner, mate, wd, biasd, wh, tail)
 
 
 def solution(mesh):

time: 34.7 us -> 35.1 us (1.012)
  waiting for transfers between devices: 2.6 us -> 4.41 us
  local copies, waits for them, and re-layouts: 3.35 us -> 2.56 us
  other arithmetic: 1.52 us -> 0.75 us
    ppermute x3, waiting for transfers between devices: 1.35 us -> 2.77 us  [local(): lax.ppermute(send, 'tile', [(i, i ^ k) for i in range(TILES)])]
    unnamed x15 -> x21, local copies, waits for them, and re-layouts: 3.35 us -> 2.48 us
    broadcast_in_dim x1 -> x0, other arithmetic: 0.76 us -> none  [local(): biases = jnp.concatenate([b_first, b_second, b_stride])[None]]
    ppermute x3, waiting for transfers between devices: 1.25 us -> 1.63 us  [local(): lax.ppermute(raw_sections, 'tile', [(i, i ^ 4 * k) for i in range(TILES)])]
  transfers between devices with their start and end apart: 8 -> 8, of which waited for: 2 -> 4; matrix products, arithmetic and copies ran while one was open for 7% -> 5% of each run, Pallas kernels for 17% -> 17%
where the time goes in v7:
time: 35.1 us; the launch traced here: 34.9 us
  starting transfers between devices  13.7 us (39%)
  Pallas kernels  13.4 us (38%)
  waiting for transfers between devices  4.41 us (13%)
  local copies, waits for them, and re-layouts  2.56 us (7%)
  other arithmetic  0.75 us (2%)
    ppermute x1, starting transfers between devices, local(): lax.ppermute(to_chip, 'sec', [(i, (i + 1 ^ 1) - 1) for i in range(1, SECS...  6.02 us
    pallas_call x1, Pallas kernels, main(): pl.pallas_call(main_kernel, out_shape=jax.ShapeDtypeStruct((3, 2, 64, 64)...  3.87 us
    ppermute x3, starting transfers between devices, local(): lax.ppermute(send, 'tile', [(i, i ^ k) for i in range(TILES)])  3.69 us
    ppermute x3, starting transfers between devices, local(): lax.ppermute(raw_sections, 'tile', [(i, i ^ 4 * k) for i in range(TILES)])  3.69 us
    pallas_call x1, Pallas kernels, align(): pl.pallas_call(align_kernel, out_shape=[jax.ShapeDtypeStruct((n, 128, 256...  2.84 us
    ppermute x3, waiting for transfers between devices, local(): lax.ppermute(send, 'tile', [(i, i ^ k) for i in range(TILES)])  2.77 us
    pallas_call x1, Pallas kernels, own(): pl.pallas_call(own_kernel, out_shape=[features(1), features(1)], in_specs...  2.59 us
    pallas_call x1, Pallas kernels, beyond(): pl.pallas_call(beyond_kernel, out_shape=features(1), in_specs=[pl.BlockSp...  2.56 us
  transfers between devices with their start and end apart: 8, of which 4 were waited for; matrix products, arithmetic and copies ran while one was open for 5% of the time, Pallas kernels for 17%

profile of v7, /device:TPU:97, one launch (start us, length us, event | category | flops | bytes accessed | tf_op | source)
XLA Modules:
  0.0 34.9 jit_solution(16343856376055361292)
XLA Ops:
  0.0 2.9 %collective-permute-start = (bf16[2,128,128]{2,1,0:T(8,128)(2,1)}, bf16[2,128,128]{2,1,0:T(8,128)(2,1)S(1)}, u32[]{:S(2)}, u32[]{:S(2)}) collective-permute-start(bf16[2,128,128]{2,1,0:T(8,128)(2,1)} %given.1), channel_id=1, source_target_pairs={{0,8},{1,9},{2,10},{3,11},{4,12},{5,13},{6,14},{7,15},{8,0},{9,1},... | collective-permute-start | bytes 196616 | tf_op jit(solution)/shard_map/ppermute | solution.py:476
  2.9 0.4 %collective-permute-start.1 = (bf16[2,128,128]{2,1,0:T(8,128)(2,1)}, bf16[2,128,128]{2,1,0:T(8,128)(2,1)S(1)}, u32[]{:S(2)}, u32[]{:S(2)}) collective-permute-start(bf16[2,128,128]{2,1,0:T(8,128)(2,1)} %given.1), channel_id=1, source_target_pairs={{0,4},{1,5},{2,6},{3,7},{4,0},{5,1},{6,2},{7,3},{8,12},{9,13},{10,... | collective-permute-start | bytes 196616 | tf_op jit(solution)/shard_map/ppermute | solution.py:476
  3.3 0.4 %collective-permute-start.2 = (bf16[2,128,128]{2,1,0:T(8,128)(2,1)}, bf16[2,128,128]{2,1,0:T(8,128)(2,1)S(1)}, u32[]{:S(2)}, u32[]{:S(2)}) collective-permute-start(bf16[2,128,128]{2,1,0:T(8,128)(2,1)} %given.1), channel_id=1, source_target_pairs={{0,12},{1,13},{2,14},{3,15},{4,8},{5,9},{6,10},{7,11},{8,4},{9,5},... | collective-permute-start | bytes 196616 | tf_op jit(solution)/shard_map/ppermute | solution.py:476
  3.7 0.0 copy-start.2
  3.7 0.9 %copy-done.2 = bf16[2,128,128]{2,1,0:T(8,128)(2,1)S(1)} copy-done((bf16[2,128,128]{2,1,0:T(8,128)(2,1)S(1)}, bf16[2,128,128]{2,1,0:T(8,128)(2,1)}, u32[]{:S(2)}) %copy-start.2) | copy-done | bytes 65560
  4.6 0.0 copy-start
  4.6 0.9 %copy.14 = bf16[32,32,2,2]{0,1,3,2:T(8,128)(2,1)S(1)} copy(bf16[32,32,2,2]{1,3,2,0:T(2,128)(2,1)} %param.20) | data formatting | bytes 16384 | tf_op args[7]
  5.5 0.8 %pad_add_fusion.spot = s32[6]{0:T(128)S(1)} fusion(s32[1]{0:T(128)} %bitcast.1, s32[1]{0:T(128)} %bitcast, s32[2]{0:T(128)} %param.15, s32[2]{0:T(128)} %param.14), kind=kLoop, calls=%fused_computation | loop fusion | flops 18 | bytes 48 | tf_op jit(solution)/shard_map/concatenate | solution.py:473
  6.2 0.0 copy-start.1
  6.2 0.0 collective-permute-done.two
  6.2 0.6 %collective-permute-done.1.one = bf16[2,128,128]{2,1,0:T(8,128)(2,1)S(1)} collective-permute-done((bf16[2,128,128]{2,1,0:T(8,128)(2,1)}, bf16[2,128,128]{2,1,0:T(8,128)(2,1)S(1)}, u32[]{:S(2)}, u32[]{:S(2)}) %collective-permute-start.1) | collective-permute-done | bytes 65568 | tf_op jit(solution)/shard_map/ppermute | solution.py:476
  6.9 1.0 %collective-permute-done.2.three = bf16[2,128,128]{2,1,0:T(8,128)(2,1)S(1)} collective-permute-done((bf16[2,128,128]{2,1,0:T(8,128)(2,1)}, bf16[2,128,128]{2,1,0:T(8,128)(2,1)S(1)}, u32[]{:S(2)}, u32[]{:S(2)}) %collective-permute-start.2) | collective-permute-done | bytes 65568 | tf_op jit(solution)/shard_map/ppermute | solution.py:476
  7.9 0.0 copy-start.8
  7.9 0.0 copy-start.9
  7.9 0.6 %pick.1 = (bf16[2,128,128]{2,1,0:T(8,128)(2,1)S(1)}, bf16[2,128,128]{2,1,0:T(8,128)(2,1)S(1)}, bf16[2,128,128]{2,1,0:T(8,128)(2,1)S(1)}, bf16[2,128,128]{2,1,0:T(8,128)(2,1)S(1)}) custom-call(s32[6]{0:T(128)S(1)} %pad_add_fusion.spot, bf16[2,128,128]{2,1,0:T(8,128)(2,1)S(1)} %stage.1.mine, bf16[2,128,128]{2,1,0:T(8,128)(2,1)S(1)} %collective-permute-done.two, ...), custom_call_target="tpu_custom_call" | custom-call | bytes 16000000 | tf_op jit(solution)/shard_map/pick/pallas_call | solution.py:70
  8.5 0.0 copy-start.5
  8.5 0.0 copy-start.6
  8.5 0.0 copy-start.7
  8.5 2.8 %collective-permute-start.3 = (bf16[2,128,128]{2,1,0:T(8,128)(2,1)S(1)}, bf16[2,128,128]{2,1,0:T(8,128)(2,1)S(1)}, u32[]{:S(2)}, u32[]{:S(2)}) collective-permute-start(bf16[2,128,128]{2,1,0:T(8,128)(2,1)S(1)} %get-tuple-element.38), channel_id=1, source_target_pairs={{0,2},{1,3},{2,0},{3,1},{4,6},{5,7},{6,4},{7,5},{8,10},{9,11},{10,... | collective-permute-start | bytes 196616 | tf_op jit(solution)/shard_map/ppermute | solution.py:487
  11.4 0.3 collective-permute-start.4
  11.7 0.6 %collective-permute-start.5 = (bf16[2,128,128]{2,1,0:T(8,128)(2,1)S(1)}, bf16[2,128,128]{2,1,0:T(8,128)(2,1)S(1)}, u32[]{:S(2)}, u32[]{:S(2)}) collective-permute-start(bf16[2,128,128]{2,1,0:T(8,128)(2,1)S(1)} %get-tuple-element.40), channel_id=1, source_target_pairs={{0,3},{1,2},{2,1},{3,0},{4,7},{5,6},{6,5},{7,4},{8,11},{9,10},{10,... | collective-permute-start | bytes 196616 | tf_op jit(solution)/shard_map/ppermute | solution.py:487
  12.2 0.0 copy-done.8
  12.2 0.0 copy-done.9
  12.2 0.0 copy-done.5
  12.2 0.0 copy-done.6
  12.2 0.0 copy-done.7
  12.2 0.1 concatenate.7
  12.3 0.0 copy-start.3
  12.3 0.0 copy-start.4
  12.3 0.0 copy-done
  12.3 0.0 copy-done.1
  12.3 0.7 %copy-done.3 = bf16[32,1,3,3]{0,3,2,1:T(4,128)(2,1)S(1)} copy-done((bf16[32,1,3,3]{0,3,2,1:T(4,128)(2,1)S(1)}, bf16[32,1,3,3]{0,3,2,1:T(4,128)(2,1)}, u32[]{:S(2)}) %copy-start.3) | copy-done | bytes 600
  13.0 0.0 copy-done.4
  13.0 0.9 %prepare.1 = (bf16[128,2688]{1,0:T(8,128)(2,1)S(1)}, f32[32,384]{1,0:T(8,128)S(1)}, bf16[768,256]{1,0:T(8,128)(2,1)S(1)}, f32[1,256]{1,0:T(1,128)S(1)}, bf16[256...) custom-call(f32[1,163]{1,0:T(1,128)S(1)} %bitcast.12, ...), custom_call_target="tpu_custom_call" | custom-call | flops 1000000 | bytes 4000000 | tf_op jit(solution)/shard_map/prepare/pallas_call | solution.py:428
  13.9 0.0 collective-permute-done.3.two
  13.9 0.5 %collective-permute-done.4.one = bf16[2,128,128]{2,1,0:T(8,128)(2,1)S(1)} collective-permute-done((bf16[2,128,128]{2,1,0:T(8,128)(2,1)S(1)}, bf16[2,128,128]{2,1,0:T(8,128)(2,1)S(1)}, u32[]{:S(2)}, u32[]{:S(2)}) %collective-permute-start.4) | collective-permute-done | bytes 65568 | tf_op jit(solution)/shard_map/ppermute | solution.py:487
  14.5 2.2 %collective-permute-done.5.three = bf16[2,128,128]{2,1,0:T(8,128)(2,1)S(1)} collective-permute-done((bf16[2,128,128]{2,1,0:T(8,128)(2,1)S(1)}, bf16[2,128,128]{2,1,0:T(8,128)(2,1)S(1)}, u32[]{:S(2)}, u32[]{:S(2)}) %collective-permute-start.5) | collective-permute-done | bytes 65568 | tf_op jit(solution)/shard_map/ppermute | solution.py:487
  16.7 2.8 %align.1 = (bf16[2,128,256]{2,1,0:T(8,128)(2,1)S(1)}, bf16[1,128,256]{2,1,0:T(8,128)(2,1)S(1)}, bf16[1,2,33,32,128]{4,3,2,1,0:T(8,128)(2,1)S(1)}) custom-call(s32[6]{0:T(128)S(1)} %pad_add_fusion.spot, bf16[2,128,128]{2,1,0:T(8,128)(2,1)S(1)} %get-tuple-element.34.keep, bf16[2,128,128]{2,1,0:T(8,128)(2,1)S(1)} %collective-permute-done.3.two, ...), custom_call_target="tpu_custom_call" | custom-call | bytes 4000000 | tf_op jit(solution)/shard_map/align/pallas_call | solution.py:120
  19.5 6.0 %collective-permute-start.6 = (bf16[1,128,256]{2,1,0:T(8,128)(2,1)S(1)}, bf16[1,128,256]{2,1,0:T(8,128)(2,1)S(1)}, u32[]{:S(2)}, u32[]{:S(2)}) collective-permute-start(bf16[1,128,256]{2,1,0:T(8,128)(2,1)S(1)} %get-tuple-element.52), channel_id=1, source_target_pairs={{16,32},{32,16},{48,64},{64,48},{80,96},{96,80},{112,128},{128,112... | collective-permute-start | bytes 196616 | tf_op jit(solution)/shard_map/ppermute | solution.py:491
  25.6 2.6 %own.1 = (bf16[1,2,33,32,128]{4,3,2,1,0:T(8,128)(2,1)S(1)}, bf16[1,2,33,32,128]{4,3,2,1,0:T(8,128)(2,1)S(1)}) custom-call(s32[6]{0:T(128)S(1)} %pad_add_fusion.spot, bf16[2,128,256]{2,1,0:T(8,128)(2,1)S(1)} %get-tuple-element.53.both, bf16[1,2,33,32,128]{4,3,2,1,0:T(8,128)(2,1)S(1)} %get-tuple-element.54.ahead, bf16[128,2688]{1,0:T(8,128)(2,1)S(1)} %get-tuple-element.46.w1, ...), custom_call_target="tpu_custom_call" | custom-call | flops 40000000000 | bytes 4000000 | tf_op jit(solution)/shard_map/own/pallas_call | solution.py:234
  28.2 0.3 collective-permute-start.7
  28.4 0.0 collective-permute-done.6.window
  28.5 2.6 %beyond.1 = bf16[1,2,33,32,128]{4,3,2,1,0:T(8,128)(2,1)S(1)} custom-call(s32[6]{0:T(128)S(1)} %pad_add_fusion.spot, bf16[1,128,256]{2,1,0:T(8,128)(2,1)S(1)} %collective-permute-done.6.window, bf16[128,2688]{1,0:T(8,128)(2,1)S(1)} %get-tuple-element.46.w1, f32[32,384]{1,0:T(8,128)S(1)} %get-tuple-element.47.bias1, ...), custom_call_target="tpu_custom_call" | custom-call | flops 20000000000 | bytes 4000000 | tf_op jit(solution)/shard_map/beyond/pallas_call | solution.py:260
  31.0 0.0 collective-permute-done.7.mate
  31.0 3.9 %convs.1 = f32[3,2,64,64]{3,2,1,0:T(8,128)} custom-call(s32[6]{0:T(128)S(1)} %pad_add_fusion.spot, bf16[1,2,33,32,128]{4,3,2,1,0:T(8,128)(2,1)S(1)} %beyond.1, bf16[1,2,33,32,128]{4,3,2,1,0:T(8,128)(2,1)S(1)} %get-tuple-element.55.near, bf16[1,2,33,32,128]{4,3,2,1,0:T(8,128)(2,1)S(1)} %get-tuple-element.56.inner, ...), custom_call_target="tpu_custom_call" | custom-call | tf_op jit(solution)/shard_map/convs/pallas_call | solution.py:318
  (1 shorter events, 0.0 us)
Async XLA Ops:
  0.0 6.2 %collective-permute-start = (bf16[2,128,128]{2,1,0:T(8,128)(2,1)}, bf16[2,128,128]{2,1,0:T(8,128)(2,1)S(1)}, u32[]{:S(2)}, u32[]{:S(2)}) collective-permute-start(bf16[2,128,128]{2,1,0:T(8,128)(2,1)} %given.1), channel_id=1, source_target_pairs={{0,8},{1,9},{2,10},{3,11},{4,12},{5,13},{6,14},{7,15},{8,0},{9,1},... | collective-permute-start | bytes 196616 | tf_op jit(solution)/shard_map/ppermute | solution.py:476
  2.9 4.0 %collective-permute-start.1 = (bf16[2,128,128]{2,1,0:T(8,128)(2,1)}, bf16[2,128,128]{2,1,0:T(8,128)(2,1)S(1)}, u32[]{:S(2)}, u32[]{:S(2)}) collective-permute-start(bf16[2,128,128]{2,1,0:T(8,128)(2,1)} %given.1), channel_id=1, source_target_pairs={{0,4},{1,5},{2,6},{3,7},{4,0},{5,1},{6,2},{7,3},{8,12},{9,13},{10,... | collective-permute-start | bytes 196616 | tf_op jit(solution)/shard_map/ppermute | solution.py:476
  3.3 4.5 %collective-permute-start.2 = (bf16[2,128,128]{2,1,0:T(8,128)(2,1)}, bf16[2,128,128]{2,1,0:T(8,128)(2,1)S(1)}, u32[]{:S(2)}, u32[]{:S(2)}) collective-permute-start(bf16[2,128,128]{2,1,0:T(8,128)(2,1)} %given.1), channel_id=1, source_target_pairs={{0,12},{1,13},{2,14},{3,15},{4,8},{5,9},{6,10},{7,11},{8,4},{9,5},... | collective-permute-start | bytes 196616 | tf_op jit(solution)/shard_map/ppermute | solution.py:476
  3.7 0.9 %copy-start.2 = (bf16[2,128,128]{2,1,0:T(8,128)(2,1)S(1)}, bf16[2,128,128]{2,1,0:T(8,128)(2,1)}, u32[]{:S(2)}) copy-start(bf16[2,128,128]{2,1,0:T(8,128)(2,1)} %given.1) | copy-start | bytes 196612
  4.6 7.8 %copy-start = (bf16[64,32,3,3,3]{0,1,4,3,2:T(8,128)(2,1)S(1)}, bf16[64,32,3,3,3]{0,1,4,3,2:T(8,128)(2,1)}, u32[]{:S(2)}) copy-start(bf16[64,32,3,3,3]{0,1,4,3,2:T(8,128)(2,1)} %param.22) | copy-start | bytes 331780
  6.2 6.1 %copy-start.1 = (bf16[32,32,3,3]{1,0,3,2:T(8,128)(2,1)S(1)}, bf16[32,32,3,3]{1,0,3,2:T(8,128)(2,1)}, u32[]{:S(2)}) copy-start(bf16[32,32,3,3]{1,0,3,2:T(8,128)(2,1)} %param.18) | copy-start | bytes 55300
  7.9 4.4 %copy-start.8 = (f32[64]{0:T(128)S(1)}, f32[64]{0:T(128)}, u32[]{:S(2)}) copy-start(f32[64]{0:T(128)} %param.23) | copy-start | bytes 772
  7.9 4.4 %copy-start.9 = (f32[3]{0:T(128)S(1)}, f32[3]{0:T(128)}, u32[]{:S(2)}) copy-start(f32[3]{0:T(128)} %param.25) | copy-start | bytes 40
  8.5 3.7 %copy-start.5 = (f32[32]{0:T(128)S(1)}, f32[32]{0:T(128)}, u32[]{:S(2)}) copy-start(f32[32]{0:T(128)} %param.17) | copy-start | bytes 388
  8.5 3.7 %copy-start.6 = (f32[32]{0:T(128)S(1)}, f32[32]{0:T(128)}, u32[]{:S(2)}) copy-start(f32[32]{0:T(128)} %param.19) | copy-start | bytes 388
  8.5 3.7 %copy-start.7 = (f32[32]{0:T(128)S(1)}, f32[32]{0:T(128)}, u32[]{:S(2)}) copy-start(f32[32]{0:T(128)} %param.21) | copy-start | bytes 388
  8.5 5.4 %collective-permute-start.3 = (bf16[2,128,128]{2,1,0:T(8,128)(2,1)S(1)}, bf16[2,128,128]{2,1,0:T(8,128)(2,1)S(1)}, u32[]{:S(2)}, u32[]{:S(2)}) collective-permute-start(bf16[2,128,128]{2,1,0:T(8,128)(2,1)S(1)} %get-tuple-element.38), channel_id=1, source_target_pairs={{0,2},{1,3},{2,0},{3,1},{4,6},{5,7},{6,4},{7,5},{8,10},{9,11},{10,... | collective-permute-start | bytes 196616 | tf_op jit(solution)/shard_map/ppermute | solution.py:487
  11.4 3.1 %collective-permute-start.4 = (bf16[2,128,128]{2,1,0:T(8,128)(2,1)S(1)}, bf16[2,128,128]{2,1,0:T(8,128)(2,1)S(1)}, u32[]{:S(2)}, u32[]{:S(2)}) collective-permute-start(bf16[2,128,128]{2,1,0:T(8,128)(2,1)S(1)} %get-tuple-element.39), channel_id=1, source_target_pairs={{0,1},{1,0},{2,3},{3,2},{4,5},{5,4},{6,7},{7,6},{8,9},{9,8},{10,11... | collective-permute-start | bytes 196616 | tf_op jit(solution)/shard_map/ppermute | solution.py:487
  11.7 5.0 %collective-permute-start.5 = (bf16[2,128,128]{2,1,0:T(8,128)(2,1)S(1)}, bf16[2,128,128]{2,1,0:T(8,128)(2,1)S(1)}, u32[]{:S(2)}, u32[]{:S(2)}) collective-permute-start(bf16[2,128,128]{2,1,0:T(8,128)(2,1)S(1)} %get-tuple-element.40), channel_id=1, source_target_pairs={{0,3},{1,2},{2,1},{3,0},{4,7},{5,6},{6,5},{7,4},{8,11},{9,10},{10,... | collective-permute-start | bytes 196616 | tf_op jit(solution)/shard_map/ppermute | solution.py:487
  12.3 0.7 %copy-start.3 = (bf16[32,1,3,3]{0,3,2,1:T(4,128)(2,1)S(1)}, bf16[32,1,3,3]{0,3,2,1:T(4,128)(2,1)}, u32[]{:S(2)}) copy-start(bf16[32,1,3,3]{0,3,2,1:T(4,128)(2,1)} %param.16) | copy-start | bytes 1732
  12.3 0.7 %copy-start.4 = (f32[3,64]{1,0:T(4,128)S(1)}, f32[3,64]{1,0:T(4,128)}, u32[]{:S(2)}) copy-start(f32[3,64]{1,0:T(4,128)} %refs_4_) | copy-start | bytes 2308
  19.5 8.9 %collective-permute-start.6 = (bf16[1,128,256]{2,1,0:T(8,128)(2,1)S(1)}, bf16[1,128,256]{2,1,0:T(8,128)(2,1)S(1)}, u32[]{:S(2)}, u32[]{:S(2)}) collective-permute-start(bf16[1,128,256]{2,1,0:T(8,128)(2,1)S(1)} %get-tuple-element.52), channel_id=1, source_target_pairs={{16,32},{32,16},{48,64},{64,48},{80,96},{96,80},{112,128},{128,112... | collective-permute-start | bytes 196616 | tf_op jit(solution)/shard_map/ppermute | solution.py:491
  28.2 2.9 %collective-permute-start.7 = (bf16[1,2,33,32,128]{4,3,2,1,0:T(8,128)(2,1)S(1)}, bf16[1,2,33,32,128]{4,3,2,1,0:T(8,128)(2,1)S(1)}, u32[]{:S(2)}, u32[]{:S(2)}) collective-permute-start(bf16[1,2,33,32,128]{4,3,2,1,0:T(8,128)(2,1)S(1)} %get-tuple-element.56.inner), channel_id=1, source_target_pairs={{0,16},{16,0},{32,48},{48,32},{64,80},{80,64},{96,112},{112,96},{1... | collective-permute-start | bytes 1622024 | tf_op jit(solution)/shard_map/ppermute | solution.py:495
